TPU v7x, 128 devices: a whole 4x4x4 slice. The times are simulated.
128 devices in a mesh: bx: 8 (over x_hi, y), by: 16 (over x_lo, z, core).
Axes of the slice: x: 4 (x_hi: 2, x_lo: 2; x = x_hi * 2 + x_lo), y: 4, z: 4, core: 2. Of those that a mesh axis runs over, the one named last changes fastest.
Arguments:
- right_sides: bfloat16 [8, 16, 16, 32, 256], P('bx', 'by'), may hold values from -6 to 6
- transform: bfloat16 [8, 16, 16, 256, 256], P('bx', 'by'), may hold values from -0.375 to 0.375
- inverse: bfloat16 [8, 16, 16, 128, 128], P('bx', 'by'), may hold values from -0.5 to 0.5
- fill_lower: bfloat16 [8, 16, 16, 16, 128, 128], P('bx', 'by'), may hold values from -0.25 to 0.25
- fill_upper: bfloat16 [8, 16, 16, 16, 128, 128], P('bx', 'by'), may hold values from -0.25 to 0.25
- parent_rows: bfloat16 [8, 16, 16, 1024, 128], P('bx', 'by'), may hold values from -0.1875 to 0.1875
- neighbours: int32 [8, 16, 16, 16], P('bx', 'by'), may hold values from 0 to 26, as said below
- counts: int32 [8, 16, 16], P('bx', 'by'), may hold values from 2 to 16, as said below
- child_slot: int32 [8, 16, 16], P('bx', 'by'), may hold values from 0 to 7, as said below
Outputs:
- solved: bfloat16 [8, 16, 16, 32, 256], P('bx', 'by')
Inputs may be any that keep to these rules, and one draw needn't show every extreme that they name: `neighbours`: codes name existing boxes adjacent to the box (never itself) within the first counts slots, all different; the remaining slots hold 13. `counts`: some box of every draw uses all 16 slots. `child_slot`: the eight children of each parent hold eight different slots.
All inputs are finite; a program needn't handle non-finite values.
Results may differ from a plain program's by a relative error of at most 0.012.
Values may be sent and summed in bfloat16 or wider, within the bound.
No kernel may reach another device: no remote copies, remote signals or barrier semaphores. Data moves between devices by JAX's collectives and lax.ppermute only.
A program may use at most 64 MiB of HBM per device.

v0:
```python
import jax
import jax.numpy as jnp
from jax import lax
from jax.sharding import PartitionSpec as P


def with_halo(value, sides, width):
    for axis, dim in sides:
        peers, length = (lax.axis_size(axis), value.shape[dim])
        up = [(i, (i + 1) % peers) for i in range(peers - 1)]
        down = [(j, i) for i, j in up]
        last = lax.slice_in_dim(value, length - width, length, axis=dim)
        initial = lax.slice_in_dim(value, 0, width, axis=dim)
        before = lax.ppermute(last, axis, up)
        after = lax.ppermute(initial, axis, down)
        value = jnp.concatenate([before, value, after], axis=dim)
    return value


def swapped(value, axis, distance):
    mask = 2**distance
    pairs = [(source, source ^ mask) for source in range(lax.axis_size(axis))]
    return lax.ppermute(value, axis, pairs)


def shortened(value):

    def short(part):
        return part.astype(jnp.bfloat16) if part.dtype == jnp.float32 else part

    return jax.tree.map(short, value)


def surround(field):
    height = field.shape[0]
    column_block = field[None, None]
    extended = with_halo(column_block, (("bx", 0), ("by", 1)), 1)
    extended = jnp.pad(extended, ((0, 0), (0, 0), (1, 1), (0, 0), (0, 0)))
    return extended.reshape(9 * (height + 2), field.shape[1] * field.shape[2])


def couple(field, fill_blocks, neighbours, counts):
    height, rhs_count, skel_width = (field.shape[0], field.shape[1], field.shape[2])
    slot_total = neighbours.shape[1]
    table = surround(field)
    cells = table.shape[0]
    positions = neighbours // 9 * (3 * (height + 2)) + neighbours // 3 % 3 * (height + 2)
    positions = positions + jnp.arange(height, dtype=jnp.int32)[:, None] + neighbours % 3
    active = jnp.arange(slot_total, dtype=jnp.int32)[None, :] < counts[:, None]
    cell_ids = jnp.arange(cells, dtype=jnp.int32)
    selector = ((positions[:, :, None] == cell_ids) & active[:, :, None]).astype(jnp.bfloat16)
    selector = selector.reshape(height * slot_total, cells)
    gathered = jnp.dot(selector, table, preferred_element_type=jnp.float32).astype(jnp.bfloat16)
    gathered = gathered.reshape(height, slot_total, rhs_count, skel_width)
    return jnp.einsum("zkrc,zkcd->zrd", gathered, fill_blocks, preferred_element_type=jnp.float32)


def pair_up(own_values, own_slots, far_values, far_slots, position):
    upper = position % 2 == 1
    lower_values = jnp.where(upper, far_values, own_values)
    upper_values = jnp.where(upper, own_values, far_values)
    lower_slots = jnp.where(upper, far_slots, own_slots)
    upper_slots = jnp.where(upper, own_slots, far_slots)
    return (jnp.stack([lower_values, upper_values]), jnp.stack([lower_slots, upper_slots]))


def body(
    right_sides,
    transform,
    inverse,
    fill_lower,
    fill_upper,
    parent_rows,
    neighbours,
    counts,
    child_slot,
):
    height = right_sides.shape[2]
    skel_width = inverse.shape[3]
    rhs_count = right_sides.shape[3]
    own_lists = neighbours[0, 0]
    own_counts = counts[0, 0]
    projected = jnp.einsum(
        "zrp,zpk->zrk", right_sides[0, 0], transform[0, 0], preferred_element_type=jnp.float32
    )
    redundant = projected[..., :skel_width].astype(jnp.bfloat16)
    local_sol = jnp.einsum(
        "zrc,zcd->zrd", redundant, inverse[0, 0], preferred_element_type=jnp.float32
    ).astype(jnp.bfloat16)
    coupled = couple(local_sol, fill_lower[0, 0], own_lists, own_counts)
    reduced = (projected[..., skel_width:] - coupled).astype(jnp.bfloat16)
    own_slots = child_slot[0, 0]
    far_values, far_slots = swapped((reduced, own_slots), "bx", 0)
    values, slot_ids = pair_up(reduced, own_slots, far_values, far_slots, lax.axis_index("bx"))
    far_values, far_slots = (
        swapped(values, "by", 0),
        swapped(shortened(slot_ids), "by", 0).astype(slot_ids.dtype),
    )
    values, slot_ids = pair_up(values, slot_ids, far_values, far_slots, lax.axis_index("by"))
    values = jnp.swapaxes(values, 0, 1)
    slot_ids = jnp.swapaxes(slot_ids, 0, 1)
    half = height // 2
    children = values.reshape(2, 2, half, 2, rhs_count, skel_width).transpose(2, 0, 1, 3, 4, 5)
    children = children.reshape(half, 8, rhs_count, skel_width)
    child_ids = slot_ids.reshape(2, 2, half, 2).transpose(2, 0, 1, 3).reshape(half, 8)
    ordinal = jnp.arange(8, dtype=jnp.int32)
    onehot = (child_ids[:, None, :] == ordinal[:, None]).astype(jnp.bfloat16)
    stacked = jnp.einsum("pjc,pcrd->prjd", onehot, children, preferred_element_type=jnp.float32)
    stacked = stacked.reshape(half, rhs_count, 8 * skel_width).astype(jnp.bfloat16)
    spread = jnp.repeat(stacked, 2, axis=0)
    skel_sol = jnp.einsum(
        "zrk,zkd->zrd", spread, parent_rows[0, 0], preferred_element_type=jnp.float32
    ).astype(jnp.bfloat16)
    backward = couple(skel_sol, fill_upper[0, 0], own_lists, own_counts)
    red_sol = (local_sol.astype(jnp.float32) - backward).astype(jnp.bfloat16)
    whole = jnp.concatenate([red_sol, skel_sol], axis=-1)
    solved = jnp.einsum("zrk,zpk->zrp", whole, transform[0, 0], preferred_element_type=jnp.float32)
    return solved.astype(jnp.bfloat16)[None, None]


def solution(mesh):
    placed = (
        P("bx", "by", None, None, None),
        P("bx", "by", None, None, None),
        P("bx", "by", None, None, None),
        P("bx", "by", None, None, None, None),
        P("bx", "by", None, None, None, None),
        P("bx", "by", None, None, None),
        P("bx", "by", None, None),
        P("bx", "by", None),
        P("bx", "by", None),
    )
    return jax.shard_map(
        body, mesh=mesh, in_specs=placed, out_specs=P("bx", "by", None, None, None), check_vma=False
    )
```

profile of v0, /device:TPU:6, one launch (start us, length us, event | category | flops | bytes accessed | tf_op | source)
XLA Modules:
  0.0 84.6 jit_solution(4993397365937001486)
XLA Ops:
  0.0 1.6 %copy-done = bf16[1,1,16,256,256]{4,3,2,1,0:T(8,128)(2,1)S(1)} copy-done((bf16[1,1,16,256,256]{4,3,2,1,0:T(8,128)(2,1)S(1)}, bf16[1,1,16,256,256]{4,3,2,1,0:T(8,128)(2,1)}, u32[]{:S(2)}) %copy-start) | copy-done | bytes 2097176
  1.6 1.4 %fusion.11 = f32[16,32,256]{2,1,0:T(8,128)S(1)} fusion(bf16[1,1,16,256,256]{4,3,2,1,0:T(8,128)(2,1)S(1)} %copy-done, bf16[1,1,16,32,256]{4,3,2,1,0:T(8,128)(2,1)} %param.9), kind=kOutput, calls=%fused_computation.15 | convolution fusion | flops 67108864 | bytes 2883584 | tf_op jit(solution)/shard_map/zrp,zpk->zrk/dot_general | solution.py:83
  3.2 5.8 %collective-permute-start.1 = (bf16[1,1,16,32,128]{4,3,2,1,0:T(8,128)(2,1)S(1)}, bf16[1,1,16,32,128]{4,3,2,1,0:T(8,128)(2,1)S(1)}, u32[]{:S(2)}, u32[]{:S(2)}) collective-permute-start(bf16[1,1,16,32,128]{4,3,2,1,0:T(8,128)(2,1)S(1)} %bitcast.159), channel_id=1, source_target_pairs={{16,0},{32,16},{48,32},{64,48},{80,64},{96,80},{112,96},{17,1},{33... | collective-permute-start | bytes 393224 | tf_op jit(solution)/shard_map/ppermute | solution.py:15
  9.0 1.9 %collective-permute-start = (bf16[1,1,16,32,128]{4,3,2,1,0:T(8,128)(2,1)S(1)}, bf16[1,1,16,32,128]{4,3,2,1,0:T(8,128)(2,1)S(1)}, u32[]{:S(2)}, u32[]{:S(2)}) collective-permute-start(bf16[1,1,16,32,128]{4,3,2,1,0:T(8,128)(2,1)S(1)} %bitcast.160), channel_id=1, source_target_pairs={{0,16},{16,32},{32,48},{48,64},{64,80},{80,96},{96,112},{1,17},{17... | collective-permute-start | bytes 393224 | tf_op jit(solution)/shard_map/ppermute | solution.py:14
  11.8 7.7 %collective-permute-done = bf16[1,1,16,32,128]{4,3,2,1,0:T(8,128)(2,1)S(1)} collective-permute-done((bf16[1,1,16,32,128]{4,3,2,1,0:T(8,128)(2,1)S(1)}, bf16[1,1,16,32,128]{4,3,2,1,0:T(8,128)(2,1)S(1)}, u32[]{:S(2)}, u32[]{:S(2)}) %collective-permute-start) | collective-permute-done | bytes 131104 | tf_op jit(solution)/shard_map/ppermute | solution.py:14
  20.3 3.3 %collective-permute-start.3 = (bf16[3,1,16,32,128]{4,3,2,1,0:T(8,128)(2,1)}, bf16[3,1,16,32,128]{4,3,2,1,0:T(8,128)(2,1)S(1)}, u32[]{:S(2)}, u32[]{:S(2)}) collective-permute-start(bf16[3,1,16,32,128]{4,3,2,1,0:T(8,128)(2,1)} %pad_maximum_fusion.1), channel_id=1, source_target_pairs={{1,0},{2,1},{3,2},{4,3},{5,4},{6,5},{7,6},{8,7},{9,8},{10,9},{11,1... | collective-permute-start | bytes 1179656 | tf_op jit(solution)/shard_map/ppermute | solution.py:15
  23.6 1.9 %collective-permute-start.2 = (bf16[3,1,16,32,128]{4,3,2,1,0:T(8,128)(2,1)}, bf16[3,1,16,32,128]{4,3,2,1,0:T(8,128)(2,1)}, u32[]{:S(2)}, u32[]{:S(2)}) collective-permute-start(bf16[3,1,16,32,128]{4,3,2,1,0:T(8,128)(2,1)} %pad_maximum_fusion.1), channel_id=1, source_target_pairs={{0,1},{1,2},{2,3},{3,4},{4,5},{5,6},{6,7},{7,8},{8,9},{9,10},{10,1... | collective-permute-start | bytes 1179656 | tf_op jit(solution)/shard_map/ppermute | solution.py:14
  25.8 3.5 %collective-permute-done.3 = bf16[3,1,16,32,128]{4,3,2,1,0:T(8,128)(2,1)S(1)} collective-permute-done((bf16[3,1,16,32,128]{4,3,2,1,0:T(8,128)(2,1)}, bf16[3,1,16,32,128]{4,3,2,1,0:T(8,128)(2,1)S(1)}, u32[]{:S(2)}, u32[]{:S(2)}) %collective-permute-start.3) | collective-permute-done | bytes 393248 | tf_op jit(solution)/shard_map/ppermute | solution.py:15
  29.2 5.9 %collective-permute-done.2 = bf16[3,1,16,32,128]{4,3,2,1,0:T(8,128)(2,1)} collective-permute-done((bf16[3,1,16,32,128]{4,3,2,1,0:T(8,128)(2,1)}, bf16[3,1,16,32,128]{4,3,2,1,0:T(8,128)(2,1)}, u32[]{:S(2)}, u32[]{:S(2)}) %collective-permute-start.2) | collective-permute-done | bytes 393248 | tf_op jit(solution)/shard_map/ppermute | solution.py:14
  35.2 1.4 %fusion.24 = bf16[3,3,18,32,128]{4,3,2,1,0:T(8,128)(2,1)S(1)} fusion(bf16[3,1,16,32,128]{4,3,2,1,0:T(8,128)(2,1)S(1)} %collective-permute-done.3, bf16[3,1,16,32,128]{4,3,2,1,0:T(8,128)(2,1)} %collective-permute-done.2, bf16[1,1,16,32,128]{4,3,2,1,0:T(8,128)(2,1)S(1)} %collective-permute-done.1, bf16[1,1,16,32,128]{4,3,2,1,0:T(8,128)(2,1)S(1)} %bitcast.162, ...), kind=kLoop, calls=%fused_computation.30 | loop fusion | flops 11943936 | bytes 2506752 | tf_op jit(solution)/shard_map/concatenate | solution.py:16
  39.1 1.6 %fusion.56 = bf16[16,32,128]{2,1,0:T(8,128)(2,1)S(1)} fusion(bf16[1,1,16,16,128,128]{5,4,3,2,1,0:T(8,128)(2,1)S(1)} %bitcast.147, f32[16,32,256]{2,1,0:T(8,128)S(1)} %fusion.11, bf16[16,16,32,128]{3,2,1,0:T(8,128)(2,1)S(1)} %bitcast.150), kind=kOutput, calls=%fused_computation.43 | convolution fusion | flops 268566528 | bytes 10878976 | tf_op jit(solution)/shard_map/zkrc,zkcd->zrd/dot_general | solution.py:55
  41.0 4.8 %collective-permute-done.4 = bf16[16,32,128]{2,1,0:T(8,128)(2,1)S(1)} collective-permute-done((bf16[16,32,128]{2,1,0:T(8,128)(2,1)S(1)}, bf16[16,32,128]{2,1,0:T(8,128)(2,1)S(1)}, u32[]{:S(2)}, u32[]{:S(2)}) %collective-permute-start.4) | collective-permute-done | bytes 131104 | tf_op jit(solution)/shard_map/ppermute | solution.py:23
  46.3 1.2 %collective-permute-done.5 = bf16[2,16,32,128]{3,2,1,0:T(8,128)(2,1)S(1)} collective-permute-done((bf16[2,16,32,128]{3,2,1,0:T(8,128)(2,1)S(1)}, bf16[2,16,32,128]{3,2,1,0:T(8,128)(2,1)S(1)}, u32[]{:S(2)}, u32[]{:S(2)}) %collective-permute-start.5) | collective-permute-done | bytes 262176 | tf_op jit(solution)/shard_map/ppermute | solution.py:23
  48.7 2.9 %fusion.66 = bf16[16,32,128]{2,1,0:T(8,128)(2,1)S(1)} fusion(bf16[16,32,1024]{2,1,0:T(8,128)(2,1)S(1)} %bitcast.158, bf16[1,1,16,1024,128]{4,3,2,1,0:T(8,128)(2,1)} %param.14), kind=kOutput, calls=%fused_computation.45 | convolution fusion | flops 134283264 | bytes 5373952 | tf_op jit(solution)/shard_map/zrk,zkd->zrd/dot_general | solution.py:111
  51.6 2.4 %collective-permute-start.9 = (bf16[1,1,16,32,128]{4,3,2,1,0:T(8,128)(2,1)S(1)}, bf16[1,1,16,32,128]{4,3,2,1,0:T(8,128)(2,1)S(1)}, u32[]{:S(2)}, u32[]{:S(2)}) collective-permute-start(bf16[1,1,16,32,128]{4,3,2,1,0:T(8,128)(2,1)S(1)} %bitcast.165), channel_id=1, source_target_pairs={{16,0},{32,16},{48,32},{64,48},{80,64},{96,80},{112,96},{17,1},{33... | collective-permute-start | bytes 393224 | tf_op jit(solution)/shard_map/ppermute | solution.py:15
  54.0 3.4 %collective-permute-start.8 = (bf16[1,1,16,32,128]{4,3,2,1,0:T(8,128)(2,1)S(1)}, bf16[1,1,16,32,128]{4,3,2,1,0:T(8,128)(2,1)S(1)}, u32[]{:S(2)}, u32[]{:S(2)}) collective-permute-start(bf16[1,1,16,32,128]{4,3,2,1,0:T(8,128)(2,1)S(1)} %bitcast.166), channel_id=1, source_target_pairs={{0,16},{16,32},{32,48},{48,64},{64,80},{80,96},{96,112},{1,17},{17... | collective-permute-start | bytes 393224 | tf_op jit(solution)/shard_map/ppermute | solution.py:14
  57.5 1.6 %collective-permute-done.9 = bf16[1,1,16,32,128]{4,3,2,1,0:T(8,128)(2,1)S(1)} collective-permute-done((bf16[1,1,16,32,128]{4,3,2,1,0:T(8,128)(2,1)S(1)}, bf16[1,1,16,32,128]{4,3,2,1,0:T(8,128)(2,1)S(1)}, u32[]{:S(2)}, u32[]{:S(2)}) %collective-permute-start.9) | collective-permute-done | bytes 131104 | tf_op jit(solution)/shard_map/ppermute | solution.py:15
  59.0 5.7 %collective-permute-done.8 = bf16[1,1,16,32,128]{4,3,2,1,0:T(8,128)(2,1)S(1)} collective-permute-done((bf16[1,1,16,32,128]{4,3,2,1,0:T(8,128)(2,1)S(1)}, bf16[1,1,16,32,128]{4,3,2,1,0:T(8,128)(2,1)S(1)}, u32[]{:S(2)}, u32[]{:S(2)}) %collective-permute-start.8) | collective-permute-done | bytes 131104 | tf_op jit(solution)/shard_map/ppermute | solution.py:14
  64.8 1.9 %collective-permute-start.11 = (bf16[3,1,16,32,128]{4,3,2,1,0:T(8,128)(2,1)S(1)}, bf16[3,1,16,32,128]{4,3,2,1,0:T(8,128)(2,1)S(1)}, u32[]{:S(2)}, u32[]{:S(2)}) collective-permute-start(bf16[3,1,16,32,128]{4,3,2,1,0:T(8,128)(2,1)S(1)} %pad_maximum_fusion.2), channel_id=1, source_target_pairs={{1,0},{2,1},{3,2},{4,3},{5,4},{6,5},{7,6},{8,7},{9,8},{10,9},{11,1... | collective-permute-start | bytes 1179656 | tf_op jit(solution)/shard_map/ppermute | solution.py:15
  66.8 2.6 %collective-permute-start.10 = (bf16[3,1,16,32,128]{4,3,2,1,0:T(8,128)(2,1)S(1)}, bf16[3,1,16,32,128]{4,3,2,1,0:T(8,128)(2,1)S(1)}, u32[]{:S(2)}, u32[]{:S(2)}) collective-permute-start(bf16[3,1,16,32,128]{4,3,2,1,0:T(8,128)(2,1)S(1)} %pad_maximum_fusion.2), channel_id=1, source_target_pairs={{0,1},{1,2},{2,3},{3,4},{4,5},{5,6},{6,7},{7,8},{8,9},{9,10},{10,1... | collective-permute-start | bytes 1179656 | tf_op jit(solution)/shard_map/ppermute | solution.py:14
  69.3 2.7 %collective-permute-done.11 = bf16[3,1,16,32,128]{4,3,2,1,0:T(8,128)(2,1)S(1)} collective-permute-done((bf16[3,1,16,32,128]{4,3,2,1,0:T(8,128)(2,1)S(1)}, bf16[3,1,16,32,128]{4,3,2,1,0:T(8,128)(2,1)S(1)}, u32[]{:S(2)}, u32[]{:S(2)}) %collective-permute-start.11) | collective-permute-done | bytes 393248 | tf_op jit(solution)/shard_map/ppermute | solution.py:15
  72.0 5.9 %collective-permute-done.10 = bf16[3,1,16,32,128]{4,3,2,1,0:T(8,128)(2,1)S(1)} collective-permute-done((bf16[3,1,16,32,128]{4,3,2,1,0:T(8,128)(2,1)S(1)}, bf16[3,1,16,32,128]{4,3,2,1,0:T(8,128)(2,1)S(1)}, u32[]{:S(2)}, u32[]{:S(2)}) %collective-permute-start.10) | collective-permute-done | bytes 393248 | tf_op jit(solution)/shard_map/ppermute | solution.py:14
  81.6 1.6 %fusion.61 = bf16[16,32,128]{2,1,0:T(8,128)(2,1)S(1)} fusion(bf16[1,1,16,16,128,128]{5,4,3,2,1,0:T(8,128)(2,1)S(1)} %bitcast.149, bf16[16,32,128]{2,1,0:T(8,128)(2,1)S(1)} %convolution_convert_fusion.3, bf16[16,16,32,128]{3,2,1,0:T(8,128)(2,1)S(1)} %bitcast.151), kind=kOutput, calls=%fused_computation.44 | convolution fusion | flops 268632064 | bytes 10747904 | tf_op jit(solution)/shard_map/zkrc,zkcd->zrd/dot_general | solution.py:55
  83.2 1.4 %fusion.33 = bf16[1,1,16,32,256]{4,3,2,1,0:T(8,128)(2,1)} fusion(bf16[1,1,16,256,256]{4,3,2,1,0:T(8,128)(2,1)S(1)} %copy-done, bf16[16,32,128]{2,1,0:T(8,128)(2,1)S(1)} %fusion.66, bf16[16,32,128]{2,1,0:T(8,128)(2,1)S(1)} %fusion.61), kind=kOutput, calls=%fused_computation.38 | convolution fusion | flops 67764224 | bytes 2621440 | tf_op jit(solution)/shard_map/zrk,zpk->zrp/dot_general | solution.py:117
  (66 shorter events, 9.9 us)
Async XLA Ops:
  0.0 1.6 %copy-start = (bf16[1,1,16,256,256]{4,3,2,1,0:T(8,128)(2,1)S(1)}, bf16[1,1,16,256,256]{4,3,2,1,0:T(8,128)(2,1)}, u32[]{:S(2)}) copy-start(bf16[1,1,16,256,256]{4,3,2,1,0:T(8,128)(2,1)} %param.10) | copy-start | bytes 6291460
  0.0 3.0 %copy-start.1 = (bf16[1,1,16,128,128]{4,3,2,1,0:T(8,128)(2,1)S(1)}, bf16[1,1,16,128,128]{4,3,2,1,0:T(8,128)(2,1)}, u32[]{:S(2)}) copy-start(bf16[1,1,16,128,128]{4,3,2,1,0:T(8,128)(2,1)} %param.11) | copy-start | bytes 1572868
  0.0 11.0 %copy-start.4 = (s32[1,1,16]{2,1,0:T(1,128)S(1)}, s32[1,1,16]{2,1,0:T(1,128)}, u32[]{:S(2)}) copy-start(s32[1,1,16]{2,1,0:T(1,128)} %param.17) | copy-start | bytes 196
  0.0 11.2 %copy-start.2 = (s32[1,1,16,16]{3,2,1,0:T(8,128)S(1)}, s32[1,1,16,16]{3,2,1,0:T(8,128)}, u32[]{:S(2)}) copy-start(s32[1,1,16,16]{3,2,1,0:T(8,128)} %param.15) | copy-start | bytes 3076
  0.0 25.5 %copy-start.3 = (s32[1,1,16]{2,1,0:T(1,128)S(1)}, s32[1,1,16]{2,1,0:T(1,128)}, u32[]{:S(2)}) copy-start(s32[1,1,16]{2,1,0:T(1,128)} %param.16) | copy-start | bytes 196
  3.2 8.5 %collective-permute-start.1 = (bf16[1,1,16,32,128]{4,3,2,1,0:T(8,128)(2,1)S(1)}, bf16[1,1,16,32,128]{4,3,2,1,0:T(8,128)(2,1)S(1)}, u32[]{:S(2)}, u32[]{:S(2)}) collective-permute-start(bf16[1,1,16,32,128]{4,3,2,1,0:T(8,128)(2,1)S(1)} %bitcast.159), channel_id=1, source_target_pairs={{16,0},{32,16},{48,32},{64,48},{80,64},{96,80},{112,96},{17,1},{33... | collective-permute-start | bytes 393224 | tf_op jit(solution)/shard_map/ppermute | solution.py:15
  9.0 10.5 %collective-permute-start = (bf16[1,1,16,32,128]{4,3,2,1,0:T(8,128)(2,1)S(1)}, bf16[1,1,16,32,128]{4,3,2,1,0:T(8,128)(2,1)S(1)}, u32[]{:S(2)}, u32[]{:S(2)}) collective-permute-start(bf16[1,1,16,32,128]{4,3,2,1,0:T(8,128)(2,1)S(1)} %bitcast.160), channel_id=1, source_target_pairs={{0,16},{16,32},{32,48},{48,64},{64,80},{80,96},{96,112},{1,17},{17... | collective-permute-start | bytes 393224 | tf_op jit(solution)/shard_map/ppermute | solution.py:14
  11.0 29.9 %collective-permute-start.6 = (s32[16]{0:T(128)S(1)}, s32[16]{0:T(128)S(1)}, u32[]{:S(2)}, u32[]{:S(2)}) collective-permute-start(s32[16]{0:T(128)S(1)} %bitcast.172), channel_id=1, source_target_pairs={{0,16},{16,0},{32,48},{48,32},{64,80},{80,64},{96,112},{112,96},{1... | collective-permute-start | bytes 200 | tf_op jit(solution)/shard_map/ppermute | solution.py:23
  20.3 8.9 %collective-permute-start.3 = (bf16[3,1,16,32,128]{4,3,2,1,0:T(8,128)(2,1)}, bf16[3,1,16,32,128]{4,3,2,1,0:T(8,128)(2,1)S(1)}, u32[]{:S(2)}, u32[]{:S(2)}) collective-permute-start(bf16[3,1,16,32,128]{4,3,2,1,0:T(8,128)(2,1)} %pad_maximum_fusion.1), channel_id=1, source_target_pairs={{1,0},{2,1},{3,2},{4,3},{5,4},{6,5},{7,6},{8,7},{9,8},{10,9},{11,1... | collective-permute-start | bytes 1179656 | tf_op jit(solution)/shard_map/ppermute | solution.py:15
  23.6 11.5 %collective-permute-start.2 = (bf16[3,1,16,32,128]{4,3,2,1,0:T(8,128)(2,1)}, bf16[3,1,16,32,128]{4,3,2,1,0:T(8,128)(2,1)}, u32[]{:S(2)}, u32[]{:S(2)}) collective-permute-start(bf16[3,1,16,32,128]{4,3,2,1,0:T(8,128)(2,1)} %pad_maximum_fusion.1), channel_id=1, source_target_pairs={{0,1},{1,2},{2,3},{3,4},{4,5},{5,6},{6,7},{7,8},{8,9},{9,10},{10,1... | collective-permute-start | bytes 1179656 | tf_op jit(solution)/shard_map/ppermute | solution.py:14
  35.1 3.5 %slice-start = ((s8[8388608]{0:T(1024)(128)(4,1)}), s8[4194304]{0:T(1024)(128)(4,1)S(1)}, s32[]{:S(2)}) async-start(s8[8388608]{0:T(1024)(128)(4,1)} %bitcast.146), calls=%async_computation | async-start | bytes 8388608
  36.8 2.4 %slice-start.1 = ((s8[8388608]{0:T(1024)(128)(4,1)}), s8[4194304]{0:T(1024)(128)(4,1)S(1)}, s32[]{:S(2)}) async-start(s8[8388608]{0:T(1024)(128)(4,1)} %bitcast.146), calls=%async_computation.1 | async-start | bytes 8388608
  40.7 5.0 %collective-permute-start.4 = (bf16[16,32,128]{2,1,0:T(8,128)(2,1)S(1)}, bf16[16,32,128]{2,1,0:T(8,128)(2,1)S(1)}, u32[]{:S(2)}, u32[]{:S(2)}) collective-permute-start(bf16[16,32,128]{2,1,0:T(8,128)(2,1)S(1)} %fusion.56), channel_id=1, source_target_pairs={{0,16},{16,0},{32,48},{48,32},{64,80},{80,64},{96,112},{112,96},{1... | collective-permute-start | bytes 393224 | tf_op jit(solution)/shard_map/ppermute | solution.py:23
  40.9 5.1 %collective-permute-start.7 = (s32[2,16]{1,0:T(2,128)S(1)}, s32[2,16]{1,0:T(2,128)S(1)}, u32[]{:S(2)}, u32[]{:S(2)}) collective-permute-start(s32[2,16]{1,0:T(2,128)S(1)} %pad_add_fusion), channel_id=1, source_target_pairs={{0,1},{1,0},{2,3},{3,2},{4,5},{5,4},{6,7},{7,6},{8,9},{9,8},{10,11... | collective-permute-start | bytes 392 | tf_op jit(solution)/shard_map/ppermute | solution.py:23
  45.9 1.6 %collective-permute-start.5 = (bf16[2,16,32,128]{3,2,1,0:T(8,128)(2,1)S(1)}, bf16[2,16,32,128]{3,2,1,0:T(8,128)(2,1)S(1)}, u32[]{:S(2)}, u32[]{:S(2)}) collective-permute-start(bf16[2,16,32,128]{3,2,1,0:T(8,128)(2,1)S(1)} %pad_maximum_fusion.3), channel_id=1, source_target_pairs={{0,1},{1,0},{2,3},{3,2},{4,5},{5,4},{6,7},{7,6},{8,9},{9,8},{10,11... | collective-permute-start | bytes 786440 | tf_op jit(solution)/shard_map/ppermute | solution.py:23
  51.6 7.4 %collective-permute-start.9 = (bf16[1,1,16,32,128]{4,3,2,1,0:T(8,128)(2,1)S(1)}, bf16[1,1,16,32,128]{4,3,2,1,0:T(8,128)(2,1)S(1)}, u32[]{:S(2)}, u32[]{:S(2)}) collective-permute-start(bf16[1,1,16,32,128]{4,3,2,1,0:T(8,128)(2,1)S(1)} %bitcast.165), channel_id=1, source_target_pairs={{16,0},{32,16},{48,32},{64,48},{80,64},{96,80},{112,96},{17,1},{33... | collective-permute-start | bytes 393224 | tf_op jit(solution)/shard_map/ppermute | solution.py:15
  54.0 10.8 %collective-permute-start.8 = (bf16[1,1,16,32,128]{4,3,2,1,0:T(8,128)(2,1)S(1)}, bf16[1,1,16,32,128]{4,3,2,1,0:T(8,128)(2,1)S(1)}, u32[]{:S(2)}, u32[]{:S(2)}) collective-permute-start(bf16[1,1,16,32,128]{4,3,2,1,0:T(8,128)(2,1)S(1)} %bitcast.166), channel_id=1, source_target_pairs={{0,16},{16,32},{32,48},{48,64},{64,80},{80,96},{96,112},{1,17},{17... | collective-permute-start | bytes 393224 | tf_op jit(solution)/shard_map/ppermute | solution.py:14
  64.8 7.2 %collective-permute-start.11 = (bf16[3,1,16,32,128]{4,3,2,1,0:T(8,128)(2,1)S(1)}, bf16[3,1,16,32,128]{4,3,2,1,0:T(8,128)(2,1)S(1)}, u32[]{:S(2)}, u32[]{:S(2)}) collective-permute-start(bf16[3,1,16,32,128]{4,3,2,1,0:T(8,128)(2,1)S(1)} %pad_maximum_fusion.2), channel_id=1, source_target_pairs={{1,0},{2,1},{3,2},{4,3},{5,4},{6,5},{7,6},{8,7},{9,8},{10,9},{11,1... | collective-permute-start | bytes 1179656 | tf_op jit(solution)/shard_map/ppermute | solution.py:15
  66.8 11.2 %collective-permute-start.10 = (bf16[3,1,16,32,128]{4,3,2,1,0:T(8,128)(2,1)S(1)}, bf16[3,1,16,32,128]{4,3,2,1,0:T(8,128)(2,1)S(1)}, u32[]{:S(2)}, u32[]{:S(2)}) collective-permute-start(bf16[3,1,16,32,128]{4,3,2,1,0:T(8,128)(2,1)S(1)} %pad_maximum_fusion.2), channel_id=1, source_target_pairs={{0,1},{1,2},{2,3},{3,4},{4,5},{5,6},{6,7},{7,8},{8,9},{9,10},{10,1... | collective-permute-start | bytes 1179656 | tf_op jit(solution)/shard_map/ppermute | solution.py:14
  78.0 2.4 %slice-start.2 = ((s8[8388608]{0:T(1024)(128)(4,1)}), s8[4194304]{0:T(1024)(128)(4,1)S(1)}, s32[]{:S(2)}) async-start(s8[8388608]{0:T(1024)(128)(4,1)} %bitcast.148), calls=%async_computation.2 | async-start | bytes 8388608
  78.5 3.1 %slice-start.3 = ((s8[8388608]{0:T(1024)(128)(4,1)}), s8[4194304]{0:T(1024)(128)(4,1)S(1)}, s32[]{:S(2)}) async-start(s8[8388608]{0:T(1024)(128)(4,1)} %bitcast.148), calls=%async_computation.3 | async-start | bytes 8388608
where the time goes:
time: 85 us; the launch traced here: 84.6 us
  waiting for transfers between devices  39.2 us (46%)
  starting transfers between devices  23.6 us (28%)
  matrix products  11.1 us (13%)
  local copies, waits for them, and re-layouts  7.45 us (9%)
  other arithmetic  2.8 us (3%)
    ppermute x4, waiting for transfers between devices, with_halo(): before = lax.ppermute(last, axis, up)  25.3 us
    ppermute x4, starting transfers between devices, with_halo(): after = lax.ppermute(initial, axis, down)  13.4 us
    ppermute x4, starting transfers between devices, with_halo(): before = lax.ppermute(last, axis, up)  9.88 us
    ppermute x4, waiting for transfers between devices, with_halo(): after = lax.ppermute(initial, axis, down)  7.86 us
    ppermute x4, waiting for transfers between devices, swapped(): return lax.ppermute(value, axis, pairs)  6.05 us
    unnamed x24, local copies, waits for them, and re-layouts  5.83 us
    dot_general x2, matrix products, couple(): jnp.einsum('zkrc,zkcd->zrd', gathered, fill_blocks, preferred_element_typ...  3.23 us
    dot_general x1, matrix products, body(): jnp.einsum('zrk,zkd->zrd', spread, parent_rows[0, 0], preferred_element_t...  2.95 us
  transfers between devices with their start and end apart: 12, of which 10 were waited for; matrix products, arithmetic and copies ran while one was open for 8% of the time, Pallas kernels for 0%

commit v1 on v0

v1 whole, which is shorter than its diff:
```python
import jax
import jax.numpy as jnp
from jax import lax
from jax.experimental import pallas as pl
from jax.experimental.pallas import tpu as pltpu
from jax.sharding import PartitionSpec as P

BF = jnp.bfloat16
F32 = jnp.float32
VM = pl.BlockSpec(memory_space=pltpu.VMEM)
SM = pl.BlockSpec(memory_space=pltpu.SMEM)


def resident(value):
    return pltpu.with_memory_space_constraint(value, pltpu.VMEM)


def even_pairs(peers):
    return [(i, i ^ 1) for i in range(peers)]


def odd_pairs(peers):
    return [(i, ((i + 1) ^ 1) - 1) for i in range(1, peers - 1)] + [(0, peers - 1), (peers - 1, 0)]


def even_swap(value, axis):
    return lax.ppermute(value, axis, even_pairs(lax.axis_size(axis)))


def odd_swap(value, axis):
    return lax.ppermute(value, axis, odd_pairs(lax.axis_size(axis)))


def first_kernel(rhs_ref, transform_ref, inverse_ref, slots_ref, skel_ref, field_ref):
    step = pl.program_id(0)
    block, rank = rhs_ref.shape[0], inverse_ref.shape[1]
    height = field_ref.shape[0] - 1

    @pl.when(step == 0)
    def _():
        rows = lax.broadcasted_iota(jnp.int32, (height, height), 0)
        cols = lax.broadcasted_iota(jnp.int32, (height, height), 1)
        column = jnp.sum(jnp.where(rows == cols, slots_ref[...], 0), axis=1, keepdims=True)
        plane = jnp.broadcast_to(column, (height, rank)).astype(F32)
        plane = jnp.concatenate([plane, jnp.zeros((field_ref.shape[1] - height, rank), F32)], axis=0)
        field_ref[height] = plane.astype(BF)

    for i in range(block):
        projected = jnp.dot(rhs_ref[i], transform_ref[i], preferred_element_type=F32)
        skel_ref[i] = projected[:, rank:]
        local = jnp.dot(projected[:, :rank].astype(BF), inverse_ref[i], preferred_element_type=F32)
        field_ref[step * block + i] = local.astype(BF)


def first(right_sides, transform, inverse, slots):
    height, rhs_count, points = right_sides.shape
    rank = inverse.shape[1]
    block = 4
    return pl.pallas_call(
        first_kernel,
        grid=(height // block,),
        in_specs=[
            pl.BlockSpec((block, rhs_count, points), lambda i: (i, 0, 0)),
            pl.BlockSpec((block, points, points), lambda i: (i, 0, 0)),
            pl.BlockSpec((block, rank, rank), lambda i: (i, 0, 0)),
            pl.BlockSpec((1, height), lambda i: (0, 0)),
        ],
        out_specs=[
            pl.BlockSpec((block, rhs_count, rank), lambda i: (i, 0, 0)),
            pl.BlockSpec((height + 1, rhs_count, rank), lambda i: (0, 0, 0)),
        ],
        out_shape=[
            jax.ShapeDtypeStruct((height, rhs_count, rank), F32),
            jax.ShapeDtypeStruct((height + 1, rhs_count, rank), BF),
        ],
        compiler_params=pltpu.CompilerParams(vmem_limit_bytes=8 << 20),
        name="first",
    )(right_sides, transform, inverse, slots)


def fill_table(table_ref, parts):
    planes = parts[0].shape[0]
    for i, part in enumerate(parts):
        table_ref[i * planes : (i + 1) * planes] = part[...]
    table_ref[len(parts) * planes] = jnp.zeros(table_ref.shape[1:], BF)


def coupling(table_ref, where_ref, fill_ref, z):
    slots, rank = fill_ref.shape[1], fill_ref.shape[2]
    rows = jnp.concatenate([table_ref[where_ref[z, k]] for k in range(slots)], axis=1)
    blocks = fill_ref[z].reshape(slots * rank, fill_ref.shape[3])
    return jnp.dot(rows, blocks, preferred_element_type=F32)


def lower_kernel(where_ref, own_ref, even_ref, odd_ref, skel_ref, fill_ref, out_ref, table_ref):
    fill_table(table_ref, (own_ref, even_ref, odd_ref))

    def box(z, _):
        out_ref[z] = (skel_ref[z] - coupling(table_ref, where_ref, fill_ref, z)).astype(BF)
        return _

    lax.fori_loop(0, out_ref.shape[0], box, 0, unroll=2)


def lower(where, own, even, odd, skel, fill):
    height, rhs_count, rank = skel.shape
    return pl.pallas_call(
        lower_kernel,
        in_specs=[SM, VM, VM, VM, VM, VM],
        out_specs=VM,
        out_shape=jax.ShapeDtypeStruct((height, rhs_count, rank), BF),
        scratch_shapes=[pltpu.VMEM((3 * own.shape[0] + 1, rhs_count, rank), BF)],
        compiler_params=pltpu.CompilerParams(vmem_limit_bytes=8 << 20),
        name="lower",
    )(where, resident(own), resident(even), resident(odd), resident(skel), resident(fill))


def parent_kernel(where_ref, own_ref, far_ref, rows_ref, out_ref, table_ref):
    planes = own_ref.shape[0]
    table_ref[0:planes] = own_ref[...]
    table_ref[planes : 2 * planes] = far_ref[...]

    def parent(i, _):
        stacked = jnp.concatenate([table_ref[where_ref[i, s]] for s in range(8)], axis=1)
        for e in range(2):
            z = 2 * i + e
            out_ref[z] = jnp.dot(stacked, rows_ref[z], preferred_element_type=F32).astype(BF)
        return _

    lax.fori_loop(0, out_ref.shape[0] // 2, parent, 0, unroll=2)


def parent(where, own, far, rows):
    height, rhs_count, rank = rows.shape[0], own.shape[1], own.shape[2]
    return pl.pallas_call(
        parent_kernel,
        in_specs=[SM, VM, VM, VM],
        out_specs=VM,
        out_shape=jax.ShapeDtypeStruct((height, rhs_count, rank), BF),
        scratch_shapes=[pltpu.VMEM((2 * own.shape[0], rhs_count, rank), BF)],
        compiler_params=pltpu.CompilerParams(vmem_limit_bytes=8 << 20),
        name="parent",
    )(where, resident(own), resident(far), resident(rows))


def upper_kernel(where_ref, own_ref, even_ref, odd_ref, skel_ref, local_ref, fill_ref, transform_ref, out_ref, table_ref):
    fill_table(table_ref, (own_ref, even_ref, odd_ref))
    last = (((1,), (1,)), ((), ()))

    def box(z, _):
        backward = coupling(table_ref, where_ref, fill_ref, z)
        red = (local_ref[z].astype(F32) - backward).astype(BF)
        whole = jnp.concatenate([red, skel_ref[z]], axis=1)
        solved = lax.dot_general(whole, transform_ref[z], last, preferred_element_type=F32)
        out_ref[z] = solved.astype(BF)
        return _

    lax.fori_loop(0, out_ref.shape[0], box, 0, unroll=2)


def upper(where, own, even, odd, skel, local, fill, transform):
    height, rhs_count, rank = skel.shape
    points = transform.shape[1]
    return pl.pallas_call(
        upper_kernel,
        in_specs=[SM, VM, VM, VM, VM, VM, VM, VM],
        out_specs=VM,
        out_shape=jax.ShapeDtypeStruct((height, rhs_count, points), BF),
        scratch_shapes=[pltpu.VMEM((3 * own.shape[0] + 1, rhs_count, rank), BF)],
        compiler_params=pltpu.CompilerParams(vmem_limit_bytes=8 << 20),
        name="upper",
    )(
        where,
        resident(own),
        resident(even),
        resident(odd),
        resident(skel),
        resident(local),
        resident(fill),
        resident(transform),
    )


def halo(field):
    even = even_swap(field, "bx")
    odd = odd_swap(field, "bx")
    own = jnp.concatenate([field, even, odd], axis=0)
    return own, even_swap(own, "by"), odd_swap(own, "by")


def places(neighbours, counts, planes):
    height, slots = neighbours.shape
    step_x = neighbours // 9 - 1
    step_y = neighbours // 3 % 3 - 1
    step_z = neighbours % 3 - 1

    def source(step, axis):
        toward_even = 1 - 2 * (lax.axis_index(axis) % 2)
        return jnp.where(step == 0, 0, jnp.where(step == toward_even, 1, 2))

    column = source(step_y, "by") * 3 + source(step_x, "bx")
    height_at = jnp.arange(height, dtype=jnp.int32)[:, None] + step_z
    active = jnp.arange(slots, dtype=jnp.int32)[None, :] < counts[:, None]
    return jnp.where(active, column * planes + height_at, 9 * planes)


def body(right_sides, transform, inverse, fill_lower, fill_upper, parent_rows, neighbours, counts, child_slot):
    right_sides, transform, inverse = right_sides[0, 0], transform[0, 0], inverse[0, 0]
    height = right_sides.shape[0]
    skel, field = first(right_sides, transform, inverse, child_slot[0])
    planes = height + 1
    own, even, odd = halo(field)
    slots = jnp.stack([own[height, :height, 0], own[planes + height, :height, 0], even[height, :height, 0], even[planes + height, :height, 0]])
    slots = slots.astype(jnp.int32).reshape(4, height // 2, 2)
    ordinal = jnp.arange(8, dtype=jnp.int32)
    index = jnp.arange(4 * height, dtype=jnp.int32).reshape(4, height // 2, 2)
    hit = slots[..., None] == ordinal
    where_child = jnp.sum(jnp.where(hit, index[..., None], 0), axis=(0, 2))
    where = places(neighbours[0, 0], counts[0, 0], planes)
    reduced = lower(where, own, even, odd, skel, fill_lower[0, 0])
    pair = jnp.concatenate([reduced, even_swap(reduced, "bx")], axis=0)
    skel_sol = parent(where_child, pair, even_swap(pair, "by"), parent_rows[0, 0])
    where = jnp.where(where == 9 * planes, 9 * height, where - where // planes)
    own, even, odd = halo(skel_sol)
    solved = upper(where, own, even, odd, skel_sol, field, fill_upper[0, 0], transform)
    return solved[None, None]


def solution(mesh):
    wide = P("bx", "by", None, None, None)
    placed = (wide, wide, wide, P("bx", "by", None, None, None, None), P("bx", "by", None, None, None, None), wide)
    placed = placed + (P("bx", "by", None, None), P("bx", "by", None), P("bx", "by", None))
    return jax.shard_map(body, mesh=mesh, in_specs=placed, out_specs=wide, check_vma=False)
```

time: 85 us -> 74.7 us (0.88)
  the two profiles are of different devices: /device:TPU:6 before, /device:TPU:0 now
where the time goes in v1:
time: 74.7 us; the launch traced here: 74.3 us
  waiting for transfers between devices  25.6 us (34%)
  starting transfers between devices  18.8 us (25%)
  local copies, waits for them, and re-layouts  15 us (20%)
  Pallas kernels  13.7 us (18%)
  other arithmetic  0.97 us (1%)
    ppermute x4, waiting for transfers between devices, odd_swap(): return lax.ppermute(value, axis, odd_pairs(lax.axis_size(axis)))  20.5 us
    ppermute x4, starting transfers between devices, odd_swap(): return lax.ppermute(value, axis, odd_pairs(lax.axis_size(axis)))  16.8 us
    unnamed x20, local copies, waits for them, and re-layouts  13.2 us
    pallas_call x1, Pallas kernels, upper(): pl.pallas_call(upper_kernel, in_specs=[SM, VM, VM, VM, VM, VM, VM, VM], o...  5.44 us
    ppermute x6, waiting for transfers between devices, even_swap(): return lax.ppermute(value, axis, even_pairs(lax.axis_size(axis)))  5.11 us
    pallas_call x1, Pallas kernels, lower(): pl.pallas_call(lower_kernel, in_specs=[SM, VM, VM, VM, VM, VM], out_specs...  3.51 us
    pallas_call x1, Pallas kernels, first(): pl.pallas_call(first_kernel, grid=(height // block,), in_specs=[pl.BlockS...  2.99 us
    ppermute x6, starting transfers between devices, even_swap(): return lax.ppermute(value, axis, even_pairs(lax.axis_size(axis)))  2.03 us
  transfers between devices with their start and end apart: 10, of which 7 were waited for; matrix products, arithmetic and copies ran while one was open for 4% of the time, Pallas kernels for 0%

profile of v1, /device:TPU:0, one launch (start us, length us, event | category | flops | bytes accessed | tf_op | source)
XLA Modules:
  0.0 74.3 jit_solution(4395816959639044539)
XLA Ops:
  0.0 1.6 %copy-done.2 = bf16[1,1,16,256,256]{4,3,2,1,0:T(8,128)(2,1)S(1)} copy-done((bf16[1,1,16,256,256]{4,3,2,1,0:T(8,128)(2,1)S(1)}, bf16[1,1,16,256,256]{4,3,2,1,0:T(8,128)(2,1)}, u32[]{:S(2)}) %copy-start.2) | copy-done | bytes 2097176
  1.6 1.0 %copy-done.5 = bf16[1,1,16,128,128]{4,3,2,1,0:T(8,128)(2,1)S(1)} copy-done((bf16[1,1,16,128,128]{4,3,2,1,0:T(8,128)(2,1)S(1)}, bf16[1,1,16,128,128]{4,3,2,1,0:T(8,128)(2,1)}, u32[]{:S(2)}) %copy-start.5) | copy-done | bytes 524312
  2.6 0.9 %copy-done.6 = bf16[1,1,16,32,256]{4,3,2,1,0:T(8,128)(2,1)S(1)} copy-done((bf16[1,1,16,32,256]{4,3,2,1,0:T(8,128)(2,1)S(1)}, bf16[1,1,16,32,256]{4,3,2,1,0:T(8,128)(2,1)}, u32[]{:S(2)}) %copy-start.6) | copy-done | bytes 262168
  3.6 0.7 copy-done.7
  4.2 3.0 %first.1 = (f32[16,32,128]{2,1,0:T(8,128)S(1)}, bf16[17,32,128]{2,1,0:T(8,128)(2,1)S(1)}) custom-call(bf16[16,32,256]{2,1,0:T(8,128)(2,1)S(1)} %bitcast.50, bf16[16,256,256]{2,1,0:T(8,128)(2,1)S(1)} %bitcast.46, bf16[16,128,128]{2,1,0:T(8,128)(2,1)S(1)} %bitcast.49, s32[1,16]{1,0:T(1,128)S(1)} %bitcast.51), custom_call_target="tpu_custom_call" | custom-call | tf_op jit(solution)/shard_map/first/pallas_call | solution.py:59
  7.2 1.7 %collective-permute-start = (bf16[17,32,128]{2,1,0:T(8,128)(2,1)S(1)}, bf16[17,32,128]{2,1,0:T(8,128)(2,1)S(1)}, u32[]{:S(2)}, u32[]{:S(2)}) collective-permute-start(bf16[17,32,128]{2,1,0:T(8,128)(2,1)S(1)} %get-tuple-element.7.local_ref), channel_id=1, source_target_pairs={{0,16},{16,0},{32,48},{48,32},{64,80},{80,64},{96,112},{112,96},{1... | collective-permute-start | bytes 417800 | tf_op jit(solution)/shard_map/ppermute | solution.py:27
  8.9 4.6 %collective-permute-start.1 = (bf16[17,32,128]{2,1,0:T(8,128)(2,1)S(1)}, bf16[17,32,128]{2,1,0:T(8,128)(2,1)S(1)}, u32[]{:S(2)}, u32[]{:S(2)}) collective-permute-start(bf16[17,32,128]{2,1,0:T(8,128)(2,1)S(1)} %get-tuple-element.7.local_ref), channel_id=1, source_target_pairs={{16,32},{32,16},{48,64},{64,48},{80,96},{96,80},{0,112},{112,0},{1... | collective-permute-start | bytes 417800 | tf_op jit(solution)/shard_map/ppermute | solution.py:31
  13.6 4.0 %collective-permute-done.1 = bf16[17,32,128]{2,1,0:T(8,128)(2,1)S(1)} collective-permute-done((bf16[17,32,128]{2,1,0:T(8,128)(2,1)S(1)}, bf16[17,32,128]{2,1,0:T(8,128)(2,1)S(1)}, u32[]{:S(2)}, u32[]{:S(2)}) %collective-permute-start.1) | collective-permute-done | bytes 139296 | tf_op jit(solution)/shard_map/ppermute | solution.py:31
  17.8 5.1 %collective-permute-start.3 = (bf16[51,32,128]{2,1,0:T(8,128)(2,1)S(1)}, bf16[51,32,128]{2,1,0:T(8,128)(2,1)}, u32[]{:S(2)}, u32[]{:S(2)}) collective-permute-start(bf16[51,32,128]{2,1,0:T(8,128)(2,1)S(1)} %constant_dynamic-update-slice_fusion.own_ref), channel_id=1, source_target_pairs={{1,2},{2,1},{3,4},{4,3},{5,6},{6,5},{7,8},{8,7},{9,10},{10,9},{11,... | collective-permute-start | bytes 1253384 | tf_op jit(solution)/shard_map/ppermute | solution.py:31
  23.0 0.8 %fusion.8 = (s32[16,16]{1,0:T(8,128)S(1)}, s32[16,16]{1,0:T(8,128)S(1)}) fusion(s32[]{:T(128)S(6)} %sub.37, s32[1,1,16,16]{3,2,1,0:T(8,128)} %param.15, s32[]{:T(128)S(6)} %sub.34, s32[16]{0:T(128)} %bitcast.52), kind=kLoop, calls=%fused_computation.17 | loop fusion | flops 13568 | bytes 3144 | tf_op jit(solution)/shard_map/jit(_where)/select_n | solution.py:223
  23.8 4.9 %collective-permute-done.3.odd_ref = bf16[51,32,128]{2,1,0:T(8,128)(2,1)} collective-permute-done((bf16[51,32,128]{2,1,0:T(8,128)(2,1)S(1)}, bf16[51,32,128]{2,1,0:T(8,128)(2,1)}, u32[]{:S(2)}, u32[]{:S(2)}) %collective-permute-start.3) | collective-permute-done | bytes 417824 | tf_op jit(solution)/shard_map/ppermute | solution.py:31
  28.7 3.4 %copy-done = bf16[1,1,16,16,128,128]{5,4,3,2,1,0:T(8,128)(2,1)S(1)} copy-done((bf16[1,1,16,16,128,128]{5,4,3,2,1,0:T(8,128)(2,1)S(1)}, bf16[1,1,16,16,128,128]{5,4,3,2,1,0:T(8,128)(2,1)}, u32[]{:S(2)}) %copy-start) | copy-done | bytes 8388632
  32.1 3.5 %lower.1 = bf16[16,32,128]{2,1,0:T(8,128)(2,1)S(1)} custom-call(s32[16,16]{1,0:T(8,128)S(1)} %get-tuple-element.12.where_ref, bf16[51,32,128]{2,1,0:T(8,128)(2,1)S(1)} %constant_dynamic-update-slice_fusion.own_ref, bf16[51,32,128]{2,1,0:T(8,128)(2,1)S(1)} %collective-permute-done.2.even_ref, bf16[51,32,128]{2,1,0:T(8,128)(2,1)} %collective-permute-done.3.odd_ref, ...), custom_call_target="tpu_custom_call" | custom-call | tf_op jit(solution)/shard_map/lower/pallas_call | solution.py:107
  35.9 0.8 %slice_reduce_fusion.2 = bf16[16]{0:T(256)(128)(2,1)S(1)} fusion(bf16[17,32,128]{2,1,0:T(8,128)(2,1)} %copy-done.8), kind=kLoop, calls=%fused_computation.35 | loop fusion | bytes 64 | tf_op jit(solution)/shard_map/slice | solution.py:213
  36.9 3.8 %collective-permute-done.4 = bf16[16,32,128]{2,1,0:T(8,128)(2,1)S(1)} collective-permute-done((bf16[16,32,128]{2,1,0:T(8,128)(2,1)S(1)}, bf16[16,32,128]{2,1,0:T(8,128)(2,1)S(1)}, u32[]{:S(2)}, u32[]{:S(2)}) %collective-permute-start.4) | collective-permute-done | bytes 131104 | tf_op jit(solution)/shard_map/ppermute | solution.py:27
  41.4 0.9 %collective-permute-done.5.far_ref = bf16[32,32,128]{2,1,0:T(8,128)(2,1)S(1)} collective-permute-done((bf16[32,32,128]{2,1,0:T(8,128)(2,1)S(1)}, bf16[32,32,128]{2,1,0:T(8,128)(2,1)S(1)}, u32[]{:S(2)}, u32[]{:S(2)}) %collective-permute-start.5) | collective-permute-done | bytes 262176 | tf_op jit(solution)/shard_map/ppermute | solution.py:27
  42.3 2.2 %copy-done.4 = bf16[1,1,16,1024,128]{4,3,2,1,0:T(8,128)(2,1)S(1)} copy-done((bf16[1,1,16,1024,128]{4,3,2,1,0:T(8,128)(2,1)S(1)}, bf16[1,1,16,1024,128]{4,3,2,1,0:T(8,128)(2,1)}, u32[]{:S(2)}) %copy-start.4) | copy-done | bytes 4194328
  44.5 1.7 %parent.1.skel_ref = bf16[16,32,128]{2,1,0:T(8,128)(2,1)S(1)} custom-call(s32[8,8]{1,0:T(8,128)S(1)} %select_reduce_fusion.where_ref, bf16[32,32,128]{2,1,0:T(8,128)(2,1)S(1)} %pad_maximum_fusion.1.own_ref, bf16[32,32,128]{2,1,0:T(8,128)(2,1)S(1)} %collective-permute-done.5.far_ref, bf16[16,1024,128]{2,1,0:T(8,128)(2,1)S(1)} %bitcast.48), custom_call_target="tpu_custom_call" | custom-call | tf_op jit(solution)/shard_map/parent/pallas_call | solution.py:135
  46.2 4.4 %collective-permute-start.7 = (bf16[16,32,128]{2,1,0:T(8,128)(2,1)S(1)}, bf16[16,32,128]{2,1,0:T(8,128)(2,1)S(1)}, u32[]{:S(2)}, u32[]{:S(2)}) collective-permute-start(bf16[16,32,128]{2,1,0:T(8,128)(2,1)S(1)} %parent.1.skel_ref), channel_id=1, source_target_pairs={{16,32},{32,16},{48,64},{64,48},{80,96},{96,80},{0,112},{112,0},{1... | collective-permute-start | bytes 393224 | tf_op jit(solution)/shard_map/ppermute | solution.py:31
  50.6 4.8 %collective-permute-done.7 = bf16[16,32,128]{2,1,0:T(8,128)(2,1)S(1)} collective-permute-done((bf16[16,32,128]{2,1,0:T(8,128)(2,1)S(1)}, bf16[16,32,128]{2,1,0:T(8,128)(2,1)S(1)}, u32[]{:S(2)}, u32[]{:S(2)}) %collective-permute-start.7) | collective-permute-done | bytes 131104 | tf_op jit(solution)/shard_map/ppermute | solution.py:31
  56.0 2.6 %collective-permute-start.9 = (bf16[48,32,128]{2,1,0:T(8,128)(2,1)S(1)}, bf16[48,32,128]{2,1,0:T(8,128)(2,1)S(1)}, u32[]{:S(2)}, u32[]{:S(2)}) collective-permute-start(bf16[48,32,128]{2,1,0:T(8,128)(2,1)S(1)} %pad_maximum_fusion.own_ref), channel_id=1, source_target_pairs={{1,2},{2,1},{3,4},{4,3},{5,6},{6,5},{7,8},{8,7},{9,10},{10,9},{11,... | collective-permute-start | bytes 1179656 | tf_op jit(solution)/shard_map/ppermute | solution.py:31
  58.7 6.8 %collective-permute-done.9.odd_ref = bf16[48,32,128]{2,1,0:T(8,128)(2,1)S(1)} collective-permute-done((bf16[48,32,128]{2,1,0:T(8,128)(2,1)S(1)}, bf16[48,32,128]{2,1,0:T(8,128)(2,1)S(1)}, u32[]{:S(2)}, u32[]{:S(2)}) %collective-permute-start.9) | collective-permute-done | bytes 393248 | tf_op jit(solution)/shard_map/ppermute | solution.py:31
  65.4 3.4 %copy-done.1 = bf16[1,1,16,16,128,128]{5,4,3,2,1,0:T(8,128)(2,1)S(1)} copy-done((bf16[1,1,16,16,128,128]{5,4,3,2,1,0:T(8,128)(2,1)S(1)}, bf16[1,1,16,16,128,128]{5,4,3,2,1,0:T(8,128)(2,1)}, u32[]{:S(2)}) %copy-start.1) | copy-done | bytes 8388632
  68.8 5.4 %upper.1 = bf16[16,32,256]{2,1,0:T(8,128)(2,1)} custom-call(s32[16,16]{1,0:T(8,128)S(1)} %get-tuple-element.11.where_ref, bf16[48,32,128]{2,1,0:T(8,128)(2,1)S(1)} %pad_maximum_fusion.own_ref, bf16[48,32,128]{2,1,0:T(8,128)(2,1)S(1)} %collective-permute-done.8.even_ref, bf16[48,32,128]{2,1,0:T(8,128)(2,1)S(1)} %collective-permute-done.9.odd_ref, ...), custom_call_target="tpu_custom_call" | custom-call | tf_op jit(solution)/shard_map/upper/pallas_call | solution.py:164
  (39 shorter events, 2.1 us)
Async XLA Ops:
  0.0 1.6 %copy-start.2 = (bf16[1,1,16,256,256]{4,3,2,1,0:T(8,128)(2,1)S(1)}, bf16[1,1,16,256,256]{4,3,2,1,0:T(8,128)(2,1)}, u32[]{:S(2)}) copy-start(bf16[1,1,16,256,256]{4,3,2,1,0:T(8,128)(2,1)} %param.10) | copy-start | bytes 6291460
  1.6 1.0 %copy-start.5 = (bf16[1,1,16,128,128]{4,3,2,1,0:T(8,128)(2,1)S(1)}, bf16[1,1,16,128,128]{4,3,2,1,0:T(8,128)(2,1)}, u32[]{:S(2)}) copy-start(bf16[1,1,16,128,128]{4,3,2,1,0:T(8,128)(2,1)} %param.11) | copy-start | bytes 1572868
  2.6 0.9 %copy-start.6 = (bf16[1,1,16,32,256]{4,3,2,1,0:T(8,128)(2,1)S(1)}, bf16[1,1,16,32,256]{4,3,2,1,0:T(8,128)(2,1)}, u32[]{:S(2)}) copy-start(bf16[1,1,16,32,256]{4,3,2,1,0:T(8,128)(2,1)} %param.9) | copy-start | bytes 786436
  3.6 0.7 copy-start.7
  4.2 61.2 %copy-start.3 = (bf16[1,1,16,256,256]{4,3,2,1,0:T(8,128)(2,1)S(1)}, bf16[1,1,16,256,256]{4,3,2,1,0:T(8,128)(2,1)}, u32[]{:S(2)}) copy-start(bf16[1,1,16,256,256]{4,3,2,1,0:T(8,128)(2,1)} %param.10) | copy-start | bytes 6291460
  7.2 6.3 %collective-permute-start = (bf16[17,32,128]{2,1,0:T(8,128)(2,1)S(1)}, bf16[17,32,128]{2,1,0:T(8,128)(2,1)S(1)}, u32[]{:S(2)}, u32[]{:S(2)}) collective-permute-start(bf16[17,32,128]{2,1,0:T(8,128)(2,1)S(1)} %get-tuple-element.7.local_ref), channel_id=1, source_target_pairs={{0,16},{16,0},{32,48},{48,32},{64,80},{80,64},{96,112},{112,96},{1... | collective-permute-start | bytes 417800 | tf_op jit(solution)/shard_map/ppermute | solution.py:27
  8.9 8.7 %collective-permute-start.1 = (bf16[17,32,128]{2,1,0:T(8,128)(2,1)S(1)}, bf16[17,32,128]{2,1,0:T(8,128)(2,1)S(1)}, u32[]{:S(2)}, u32[]{:S(2)}) collective-permute-start(bf16[17,32,128]{2,1,0:T(8,128)(2,1)S(1)} %get-tuple-element.7.local_ref), channel_id=1, source_target_pairs={{16,32},{32,16},{48,64},{64,48},{80,96},{96,80},{0,112},{112,0},{1... | collective-permute-start | bytes 417800 | tf_op jit(solution)/shard_map/ppermute | solution.py:31
  13.6 4.1 %copy-start.8 = (bf16[17,32,128]{2,1,0:T(8,128)(2,1)}, bf16[17,32,128]{2,1,0:T(8,128)(2,1)S(1)}, u32[]{:S(2)}) copy-start(bf16[17,32,128]{2,1,0:T(8,128)(2,1)S(1)} %collective-permute-done) | copy-start | bytes 417796
  17.7 6.1 %collective-permute-start.2 = (bf16[51,32,128]{2,1,0:T(8,128)(2,1)S(1)}, bf16[51,32,128]{2,1,0:T(8,128)(2,1)S(1)}, u32[]{:S(2)}, u32[]{:S(2)}) collective-permute-start(bf16[51,32,128]{2,1,0:T(8,128)(2,1)S(1)} %constant_dynamic-update-slice_fusion.own_ref), channel_id=1, source_target_pairs={{0,1},{1,0},{2,3},{3,2},{4,5},{5,4},{6,7},{7,6},{8,9},{9,8},{10,11... | collective-permute-start | bytes 1253384 | tf_op jit(solution)/shard_map/ppermute | solution.py:27
  17.8 10.9 %collective-permute-start.3 = (bf16[51,32,128]{2,1,0:T(8,128)(2,1)S(1)}, bf16[51,32,128]{2,1,0:T(8,128)(2,1)}, u32[]{:S(2)}, u32[]{:S(2)}) collective-permute-start(bf16[51,32,128]{2,1,0:T(8,128)(2,1)S(1)} %constant_dynamic-update-slice_fusion.own_ref), channel_id=1, source_target_pairs={{1,2},{2,1},{3,4},{4,3},{5,6},{6,5},{7,8},{8,7},{9,10},{10,9},{11,... | collective-permute-start | bytes 1253384 | tf_op jit(solution)/shard_map/ppermute | solution.py:31
  28.7 3.4 %copy-start = (bf16[1,1,16,16,128,128]{5,4,3,2,1,0:T(8,128)(2,1)S(1)}, bf16[1,1,16,16,128,128]{5,4,3,2,1,0:T(8,128)(2,1)}, u32[]{:S(2)}) copy-start(bf16[1,1,16,16,128,128]{5,4,3,2,1,0:T(8,128)(2,1)} %param.12) | copy-start | bytes 25165828
  35.6 5.0 %collective-permute-start.4 = (bf16[16,32,128]{2,1,0:T(8,128)(2,1)S(1)}, bf16[16,32,128]{2,1,0:T(8,128)(2,1)S(1)}, u32[]{:S(2)}, u32[]{:S(2)}) collective-permute-start(bf16[16,32,128]{2,1,0:T(8,128)(2,1)S(1)} %lower.1), channel_id=1, source_target_pairs={{0,16},{16,0},{32,48},{48,32},{64,80},{80,64},{96,112},{112,96},{1... | collective-permute-start | bytes 393224 | tf_op jit(solution)/shard_map/ppermute | solution.py:27
  40.7 1.6 %collective-permute-start.5 = (bf16[32,32,128]{2,1,0:T(8,128)(2,1)S(1)}, bf16[32,32,128]{2,1,0:T(8,128)(2,1)S(1)}, u32[]{:S(2)}, u32[]{:S(2)}) collective-permute-start(bf16[32,32,128]{2,1,0:T(8,128)(2,1)S(1)} %pad_maximum_fusion.1.own_ref), channel_id=1, source_target_pairs={{0,1},{1,0},{2,3},{3,2},{4,5},{5,4},{6,7},{7,6},{8,9},{9,8},{10,11... | collective-permute-start | bytes 786440 | tf_op jit(solution)/shard_map/ppermute | solution.py:27
  42.3 2.2 %copy-start.4 = (bf16[1,1,16,1024,128]{4,3,2,1,0:T(8,128)(2,1)S(1)}, bf16[1,1,16,1024,128]{4,3,2,1,0:T(8,128)(2,1)}, u32[]{:S(2)}) copy-start(bf16[1,1,16,1024,128]{4,3,2,1,0:T(8,128)(2,1)} %param.14) | copy-start | bytes 12582916
  46.2 9.2 %collective-permute-start.7 = (bf16[16,32,128]{2,1,0:T(8,128)(2,1)S(1)}, bf16[16,32,128]{2,1,0:T(8,128)(2,1)S(1)}, u32[]{:S(2)}, u32[]{:S(2)}) collective-permute-start(bf16[16,32,128]{2,1,0:T(8,128)(2,1)S(1)} %parent.1.skel_ref), channel_id=1, source_target_pairs={{16,32},{32,16},{48,64},{64,48},{80,96},{96,80},{0,112},{112,0},{1... | collective-permute-start | bytes 393224 | tf_op jit(solution)/shard_map/ppermute | solution.py:31
  50.6 5.3 %collective-permute-start.6 = (bf16[16,32,128]{2,1,0:T(8,128)(2,1)S(1)}, bf16[16,32,128]{2,1,0:T(8,128)(2,1)S(1)}, u32[]{:S(2)}, u32[]{:S(2)}) collective-permute-start(bf16[16,32,128]{2,1,0:T(8,128)(2,1)S(1)} %parent.1.skel_ref), channel_id=1, source_target_pairs={{0,16},{16,0},{32,48},{48,32},{64,80},{80,64},{96,112},{112,96},{1... | collective-permute-start | bytes 393224 | tf_op jit(solution)/shard_map/ppermute | solution.py:27
  55.9 2.7 %collective-permute-start.8 = (bf16[48,32,128]{2,1,0:T(8,128)(2,1)S(1)}, bf16[48,32,128]{2,1,0:T(8,128)(2,1)S(1)}, u32[]{:S(2)}, u32[]{:S(2)}) collective-permute-start(bf16[48,32,128]{2,1,0:T(8,128)(2,1)S(1)} %pad_maximum_fusion.own_ref), channel_id=1, source_target_pairs={{0,1},{1,0},{2,3},{3,2},{4,5},{5,4},{6,7},{7,6},{8,9},{9,8},{10,11... | collective-permute-start | bytes 1179656 | tf_op jit(solution)/shard_map/ppermute | solution.py:27
  56.0 9.4 %collective-permute-start.9 = (bf16[48,32,128]{2,1,0:T(8,128)(2,1)S(1)}, bf16[48,32,128]{2,1,0:T(8,128)(2,1)S(1)}, u32[]{:S(2)}, u32[]{:S(2)}) collective-permute-start(bf16[48,32,128]{2,1,0:T(8,128)(2,1)S(1)} %pad_maximum_fusion.own_ref), channel_id=1, source_target_pairs={{1,2},{2,1},{3,4},{4,3},{5,6},{6,5},{7,8},{8,7},{9,10},{10,9},{11,... | collective-permute-start | bytes 1179656 | tf_op jit(solution)/shard_map/ppermute | solution.py:31
  65.4 3.4 %copy-start.1 = (bf16[1,1,16,16,128,128]{5,4,3,2,1,0:T(8,128)(2,1)S(1)}, bf16[1,1,16,16,128,128]{5,4,3,2,1,0:T(8,128)(2,1)}, u32[]{:S(2)}) copy-start(bf16[1,1,16,16,128,128]{5,4,3,2,1,0:T(8,128)(2,1)} %param.13) | copy-start | bytes 25165828

commit v2 on v1

v2 whole, which is shorter than its diff:
```python
import functools

import jax
import jax.numpy as jnp
from jax import lax
from jax.experimental import pallas as pl
from jax.experimental.pallas import tpu as pltpu
from jax.sharding import PartitionSpec as P

BF = jnp.bfloat16
F32 = jnp.float32
VM = pl.BlockSpec(memory_space=pltpu.VMEM)
SM = pl.BlockSpec(memory_space=pltpu.SMEM)
HB = pl.BlockSpec(memory_space=pltpu.HBM)
AN = pl.BlockSpec(memory_space=pl.ANY)


def resident(value):
    return pltpu.with_memory_space_constraint(value, pltpu.VMEM)


def far_memory(value):
    return pltpu.with_memory_space_constraint(value, pltpu.HBM)


def scalars(value):
    return pltpu.with_memory_space_constraint(value, pltpu.SMEM)


def call(kernel, name, ins, outs, scratch=(), moved=0, flops=0):
    return pl.pallas_call(
        kernel,
        in_specs=ins,
        out_specs=[SM if getattr(o, "memory_space", None) == pltpu.SMEM else VM for o in outs],
        out_shape=list(outs),
        scratch_shapes=list(scratch),
        compiler_params=pltpu.CompilerParams(vmem_limit_bytes=4 << 20),
        cost_estimate=pl.CostEstimate(flops=flops, bytes_accessed=moved, transcendentals=0),
        name=name,
    )


def even_pairs(peers):
    return [(i, i ^ 1) for i in range(peers)]


def odd_pairs(peers):
    return [(i, ((i + 1) ^ 1) - 1) for i in range(1, peers - 1)] + [(0, peers - 1), (peers - 1, 0)]


def even_swap(value, axis):
    return lax.ppermute(value, axis, even_pairs(lax.axis_size(axis)))


def odd_swap(value, axis):
    return lax.ppermute(value, axis, odd_pairs(lax.axis_size(axis)))


def first_kernel(rhs_hbm, transform_hbm, inverse_hbm, slots_hbm, skel_ref, field_ref, transform_ref, rhs_ref, inverse_ref, slots_ref, sems):
    height, rank = inverse_ref.shape[0], inverse_ref.shape[1]
    bounds = (0, height * 3 // 8, height * 3 // 4, height)
    chunks = [slice(i, j) for i, j in zip(bounds[:-1], bounds[1:])]
    loads = [pltpu.make_async_copy(transform_hbm.at[c], transform_ref.at[c], sems.at[i]) for i, c in enumerate(chunks)]
    rhs_load = pltpu.make_async_copy(rhs_hbm, rhs_ref, sems.at[3])
    inverse_load = pltpu.make_async_copy(inverse_hbm, inverse_ref, sems.at[4])
    small = pltpu.make_async_copy(slots_hbm, slots_ref, sems.at[5])
    for copy in (rhs_load, *loads, inverse_load, small):
        copy.start()
    rhs_load.wait()
    redundant = []
    for c, load in zip(chunks, loads):
        load.wait()
        boxes = range(c.start, c.stop)
        projected = [jnp.dot(rhs_ref[z], transform_ref[z], preferred_element_type=F32) for z in boxes]
        for z, rows in zip(boxes, projected):
            skel_ref[z] = rows[:, rank:]
            redundant.append(rows[:, :rank].astype(BF))
    inverse_load.wait()
    for z in range(height):
        field_ref[z] = jnp.dot(redundant[z], inverse_ref[z], preferred_element_type=F32).astype(BF)
    small.wait()
    rows = lax.broadcasted_iota(jnp.int32, (height, height), 0)
    cols = lax.broadcasted_iota(jnp.int32, (height, height), 1)
    column = jnp.sum(jnp.where(rows == cols, slots_ref[...], 0), axis=1, keepdims=True)
    plane = jnp.broadcast_to(column, (height, rank)).astype(F32)
    plane = jnp.concatenate([plane, jnp.zeros((field_ref.shape[1] - height, rank), F32)], axis=0)
    field_ref[height] = plane.astype(BF)


def first(right_sides, transform, inverse, slots):
    height, rhs_count, points = right_sides.shape
    rank = inverse.shape[1]
    return call(
        first_kernel,
        "first",
        [HB, HB, HB, HB],
        [
            pltpu.VMEM((height, rhs_count, rank), F32),
            pltpu.VMEM((height + 1, rhs_count, rank), BF),
            pltpu.VMEM(transform.shape, BF),
        ],
        [
            pltpu.VMEM(right_sides.shape, BF),
            pltpu.VMEM(inverse.shape, BF),
            pltpu.VMEM(slots.shape, jnp.int32),
            pltpu.SemaphoreType.DMA((6,)),
        ],
    )(far_memory(right_sides), far_memory(transform), far_memory(inverse), far_memory(slots))


def fetch_kernel(value_hbm, after_ref, out_ref, token_ref, sem):
    copy = pltpu.make_async_copy(value_hbm, out_ref, sem)
    copy.start()
    token_ref[...] = jnp.zeros_like(token_ref)
    copy.wait()


def fetch(value, after):
    return call(
        fetch_kernel,
        "fetch",
        [HB, AN],
        [pltpu.VMEM(value.shape, value.dtype), pltpu.VMEM((8, 128), F32)],
        [pltpu.SemaphoreType.DMA],
        moved=2 * value.size * value.dtype.itemsize,
    )(far_memory(value), after)


def places_kernel(lists_hbm, counts_hbm, after_ref, out_ref, lists_ref, counts_ref, found_ref, sems, *, planes):
    height, slots = lists_ref.shape
    loads = [pltpu.make_async_copy(lists_hbm, lists_ref, sems.at[0]), pltpu.make_async_copy(counts_hbm, counts_ref, sems.at[1])]
    for load in loads:
        load.start()
    for load in loads:
        load.wait()
    codes = lists_ref[...]
    one = jnp.int32(1)
    step_x = jnp.where(codes >= 9, one, 0) + jnp.where(codes >= 18, one, 0)
    rest = codes - 9 * step_x
    step_y = jnp.where(rest >= 3, one, 0) + jnp.where(rest >= 6, one, 0)
    step_z = rest - 3 * step_y

    def source(step, axis):
        even_side = 2 - 2 * (lax.axis_index(axis) % 2)
        return jnp.where(step == 1, 0, jnp.where(step == even_side, one, 2))

    level = lax.broadcasted_iota(jnp.int32, (height, height), 0)
    lane = lax.broadcasted_iota(jnp.int32, (height, height), 1)
    counts = jnp.sum(jnp.where(level == lane, counts_ref[...], 0), axis=1, keepdims=True)
    active = lax.broadcasted_iota(jnp.int32, (height, slots), 1) < counts
    column = source(step_y, "by") * 3 + source(step_x, "bx")
    level = lax.broadcasted_iota(jnp.int32, (height, slots), 0) + step_z - 1
    for i, size in enumerate(planes):
        found_ref[i * height : (i + 1) * height] = jnp.where(active, column * size + level, 9 * size)
    copy = pltpu.make_async_copy(found_ref, out_ref, sems.at[2])
    copy.start()
    copy.wait()


def places(neighbours, counts, planes, after):
    height, slots = neighbours.shape
    rows = len(planes) * height
    return call(
        functools.partial(places_kernel, planes=planes),
        "places",
        [HB, HB, AN],
        [pltpu.SMEM((rows, slots), jnp.int32)],
        [
            pltpu.VMEM(neighbours.shape, jnp.int32),
            pltpu.VMEM(counts.shape, jnp.int32),
            pltpu.VMEM((rows, slots), jnp.int32),
            pltpu.SemaphoreType.DMA((3,)),
        ],
        moved=1 << 20,
    )(far_memory(neighbours), far_memory(counts), after)[0]


def pack_kernel(*refs):
    out_ref = refs[-1]
    planes = refs[0].shape[0]
    for i in range(out_ref.shape[0] // planes):
        out_ref[i * planes : (i + 1) * planes] = refs[i][...]


def pack(parts, after):
    planes, rows, cols = parts[0].shape
    shape = pltpu.VMEM((len(parts) * planes, rows, cols), BF)
    return call(pack_kernel, "pack", [VM] * len(parts) + [AN] * len(after), [shape])(*map(resident, parts), *after)[0]


def fill_table(table_ref, parts):
    planes = parts[0].shape[0]
    for i, part in enumerate(parts):
        table_ref[i * planes : (i + 1) * planes] = part[...]
    table_ref[len(parts) * planes] = jnp.zeros(table_ref.shape[1:], BF)


def coupling(table_ref, where_ref, base, fill_ref, z):
    slots, rank = fill_ref.shape[1], fill_ref.shape[2]
    rows = jnp.concatenate([table_ref[where_ref[base + z, k]] for k in range(slots)], axis=1)
    blocks = fill_ref[z].reshape(slots * rank, fill_ref.shape[3])
    return jnp.dot(rows, blocks, preferred_element_type=F32)


def lower_kernel(where_ref, own_ref, even_ref, odd_ref, skel_ref, fill_ref, after_ref, out_ref, child_ref, table_ref, child_vmem, sem):
    height, planes = out_ref.shape[0], own_ref.shape[0] // 3
    lane = lax.broadcasted_iota(jnp.int32, child_vmem.shape, 1)
    level = lax.broadcasted_iota(jnp.int32, child_vmem.shape, 0)
    found = jnp.zeros(child_vmem.shape, jnp.int32)
    columns = (own_ref[height], own_ref[planes + height], even_ref[height], even_ref[planes + height])
    for i, column in enumerate(columns):
        slots = column.astype(F32)[:height].astype(jnp.int32)
        found = found + jnp.where(slots == lane, i * height + level, 0)
    child_vmem[...] = found
    copy = pltpu.make_async_copy(child_vmem, child_ref, sem)
    copy.start()
    fill_table(table_ref, (own_ref, even_ref, odd_ref))
    for z in range(height):
        out_ref[z] = (skel_ref[z] - coupling(table_ref, where_ref, 0, fill_ref, z)).astype(BF)
    copy.wait()


def lower(where, own, even, odd, skel, fill, after):
    height, rhs_count, rank = skel.shape
    return call(
        lower_kernel,
        "lower",
        [SM, VM, VM, VM, VM, VM, AN],
        [pltpu.VMEM((height, rhs_count, rank), BF), pltpu.SMEM((height, rank), jnp.int32)],
        [
            pltpu.VMEM((3 * own.shape[0] + 1, rhs_count, rank), BF),
            pltpu.VMEM((height, rank), jnp.int32),
            pltpu.SemaphoreType.DMA,
        ],
    )(scalars(where), resident(own), resident(even), resident(odd), resident(skel), resident(fill), after)


def parent_kernel(child_ref, own_ref, far_ref, rows_ref, out_ref, table_ref):
    planes = own_ref.shape[0]
    table_ref[0:planes] = own_ref[...]
    table_ref[planes : 2 * planes] = far_ref[...]
    for i in range(out_ref.shape[0] // 2):
        places = [child_ref[2 * i, s] + child_ref[2 * i + 1, s] for s in range(8)]
        stacked = jnp.concatenate([table_ref[place] for place in places], axis=1)
        for z in (2 * i, 2 * i + 1):
            out_ref[z] = jnp.dot(stacked, rows_ref[z], preferred_element_type=F32).astype(BF)


def parent(child, own, far, rows):
    height, rhs_count, rank = rows.shape[0], own.shape[1], own.shape[2]
    return call(
        parent_kernel,
        "parent",
        [SM, VM, VM, VM],
        [pltpu.VMEM((height, rhs_count, rank), BF)],
        [pltpu.VMEM((2 * own.shape[0], rhs_count, rank), BF)],
    )(scalars(child), resident(own), resident(far), resident(rows))[0]


def upper_kernel(where_ref, own_ref, even_ref, odd_ref, skel_ref, local_ref, fill_ref, transform_ref, out_ref, table_ref):
    fill_table(table_ref, (own_ref, even_ref, odd_ref))
    last = (((1,), (1,)), ((), ()))
    height = out_ref.shape[0]
    for z in range(height):
        backward = coupling(table_ref, where_ref, height, fill_ref, z)
        red = (local_ref[z].astype(F32) - backward).astype(BF)
        whole = jnp.concatenate([red, skel_ref[z]], axis=1)
        solved = lax.dot_general(whole, transform_ref[z], last, preferred_element_type=F32)
        out_ref[z] = solved.astype(BF)


def upper(where, own, even, odd, skel, local, fill, transform):
    height, rhs_count, rank = skel.shape
    points = transform.shape[1]
    operands = (own, even, odd, skel, local, fill, transform)
    return call(
        upper_kernel,
        "upper",
        [SM, VM, VM, VM, VM, VM, VM, VM],
        [jax.ShapeDtypeStruct((height, rhs_count, points), BF)],
        [pltpu.VMEM((3 * own.shape[0] + 1, rhs_count, rank), BF)],
    )(scalars(where), *map(resident, operands))[0]


def halo(field, after):
    odd = odd_swap(field, "bx")
    even = even_swap(field, "bx")
    own = pack([field, even, odd], after)
    return own, even_swap(own, "by"), odd_swap(own, "by")


def body(right_sides, transform, inverse, fill_lower, fill_upper, parent_rows, neighbours, counts, child_slot):
    right_sides, transform, inverse = right_sides[0, 0], transform[0, 0], inverse[0, 0]
    height = right_sides.shape[0]
    skel, field, transform = first(right_sides, transform, inverse, child_slot[0])
    planes = height + 1
    fill_lower, token = fetch(fill_lower[0, 0], field)
    own, even, odd = halo(field, [token])
    where = places(neighbours[0, 0], counts[0], (planes, height), own)
    parent_rows, token = fetch(parent_rows[0, 0], own)
    reduced, child = lower(where, own, even, odd, skel, fill_lower, token)
    fill_upper, token = fetch(fill_upper[0, 0], reduced)
    pair = pack([reduced, even_swap(reduced, "bx")], [token])
    skel_sol = parent(child, pair, even_swap(pair, "by"), parent_rows)
    own, even, odd = halo(skel_sol, [])
    solved = upper(where, own, even, odd, skel_sol, field, fill_upper, transform)
    return solved[None, None]


def solution(mesh):
    wide = P("bx", "by", None, None, None)
    placed = (wide, wide, wide, P("bx", "by", None, None, None, None), P("bx", "by", None, None, None, None), wide)
    placed = placed + (P("bx", "by", None, None), P("bx", "by", None), P("bx", "by", None))
    return jax.shard_map(body, mesh=mesh, in_specs=placed, out_specs=wide, check_vma=False)
```

time: 74.7 us -> 54.8 us (0.73)
  local copies, waits for them, and re-layouts: 15 us -> 0 us
  Pallas kernels: 13.7 us -> 19.4 us
  waiting for transfers between devices: 25.6 us -> 20.5 us
  starting transfers between devices: 18.8 us -> 14.6 us
  other arithmetic: 0.97 us -> 0 us
    unnamed x20 -> x0, local copies, waits for them, and re-layouts: 13.2 us -> none
    pallas_call x4 -> x11, Pallas kernels: 13.7 us -> 19.4 us  [the longest x3 8.98 us: fetch(): call(fetch_kernel, 'fetch', [HB, AN], [pltpu.VMEM(value.shape, value.dtyp...]
    ppermute x4, waiting for transfers between devices: 20.5 us -> 16.2 us  [odd_swap(): return lax.ppermute(value, axis, odd_pairs(lax.axis_size(axis)))]
    ppermute x4, starting transfers between devices: 16.8 us -> 14.1 us  [odd_swap(): return lax.ppermute(value, axis, odd_pairs(lax.axis_size(axis)))]
    ppermute x6, starting transfers between devices: 2.03 us -> 0.49 us  [even_swap(): return lax.ppermute(value, axis, even_pairs(lax.axis_size(axis)))]
    slice x3 -> x0, local copies, waits for them, and re-layouts: 1.04 us -> none  [the longest x1 0.81 us: body(): own[planes + height, :height, 0]]
    ppermute x6, waiting for transfers between devices: 5.11 us -> 4.24 us  [even_swap(): return lax.ppermute(value, axis, even_pairs(lax.axis_size(axis)))]
    select_n x1 -> x0, other arithmetic: 0.79 us -> none  [body(): where = jnp.where(where == 9 * planes, 9 * height, where - where // planes)]
  transfers between devices with their start and end apart: 10 -> 10, of which waited for: 7 -> 7; matrix products, arithmetic and copies ran while one was open for 4% -> 0% of each run, Pallas kernels for 0% -> 19%
where the time goes in v2:
time: 54.8 us; the launch traced here: 54.6 us
  waiting for transfers between devices  20.5 us (37%)
  Pallas kernels  19.4 us (35%)
  starting transfers between devices  14.6 us (27%)
    ppermute x4, waiting for transfers between devices, odd_swap(): return lax.ppermute(value, axis, odd_pairs(lax.axis_size(axis)))  16.2 us
    ppermute x4, starting transfers between devices, odd_swap(): return lax.ppermute(value, axis, odd_pairs(lax.axis_size(axis)))  14.1 us
    pallas_call x3, Pallas kernels, fetch(): call(fetch_kernel, 'fetch', [HB, AN], [pltpu.VMEM(value.shape, value.dtyp...  8.98 us
    ppermute x6, waiting for transfers between devices, even_swap(): return lax.ppermute(value, axis, even_pairs(lax.axis_size(axis)))  4.24 us
    pallas_call x1, Pallas kernels, upper(): call(upper_kernel, 'upper', [SM, VM, VM, VM, VM, VM, VM, VM], [jax.ShapeD...  3.49 us
    pallas_call x1, Pallas kernels, first(): call(first_kernel, 'first', [HB, HB, HB, HB], [pltpu.VMEM((height, rhs_co...  2.3 us
    pallas_call x1, Pallas kernels, lower(): call(lower_kernel, 'lower', [SM, VM, VM, VM, VM, VM, AN], [pltpu.VMEM((he...  2.19 us
    pallas_call x1, Pallas kernels, places(): call(functools.partial(places_kernel, planes=planes), 'places', [HB, HB,...  1.61 us
  transfers between devices with their start and end apart: 10, of which 7 were waited for; matrix products, arithmetic and copies ran while one was open for 0% of the time, Pallas kernels for 19%

profile of v2, /device:TPU:0, one launch (start us, length us, event | category | flops | bytes accessed | tf_op | source)
XLA Modules:
  0.0 54.6 jit_solution(6732419267664356098)
XLA Ops:
  0.0 2.3 %first.1 = (f32[16,32,128]{2,1,0:T(8,128)S(1)}, bf16[17,32,128]{2,1,0:T(8,128)(2,1)S(1)}, bf16[16,256,256]{2,1,0:T(8,128)(2,1)S(1)}) custom-call(bf16[16,32,256]{2,1,0:T(8,128)(2,1)} %bitcast.15, bf16[16,256,256]{2,1,0:T(8,128)(2,1)} %bitcast.13, bf16[16,128,128]{2,1,0:T(8,128)(2,1)} %bitcast.14, s32[1,16]{1,0:T(1,128)} %bitcast.17), custom_call_target="tpu_custom_call" | custom-call | tf_op jit(solution)/shard_map/first/pallas_call | solution.py:93
  2.3 5.6 %collective-permute-start.1 = (bf16[17,32,128]{2,1,0:T(8,128)(2,1)S(1)}, bf16[17,32,128]{2,1,0:T(8,128)(2,1)S(1)}, u32[]{:S(2)}, u32[]{:S(2)}) collective-permute-start(bf16[17,32,128]{2,1,0:T(8,128)(2,1)S(1)} %get-tuple-element.16.after_ref.refs_0_.local_ref), channel_id=1, source_target_pairs={{16,32},{32,16},{48,64},{64,48},{80,96},{96,80},{0,112},{112,0},{1... | collective-permute-start | bytes 417800 | tf_op jit(solution)/shard_map/ppermute | solution.py:56
  7.9 0.0 collective-permute-start
  7.9 3.4 %fetch.3 = (bf16[16,16,128,128]{3,2,1,0:T(8,128)(2,1)S(1)}, f32[8,128]{1,0:T(8,128)S(1)}) custom-call(bf16[16,16,128,128]{3,2,1,0:T(8,128)(2,1)} %bitcast.10, bf16[17,32,128]{2,1,0:T(8,128)(2,1)S(1)} %get-tuple-element.16.after_ref.refs_0_.local_ref), custom_call_target="tpu_custom_call" | custom-call | bytes 16777216 | tf_op jit(solution)/shard_map/fetch/pallas_call | solution.py:119
  11.3 0.3 collective-permute-done.1.refs_2_
  11.6 1.5 %collective-permute-done.refs_1_ = bf16[17,32,128]{2,1,0:T(8,128)(2,1)S(1)} collective-permute-done((bf16[17,32,128]{2,1,0:T(8,128)(2,1)S(1)}, bf16[17,32,128]{2,1,0:T(8,128)(2,1)S(1)}, u32[]{:S(2)}, u32[]{:S(2)}) %collective-permute-start) | collective-permute-done | bytes 139296 | tf_op jit(solution)/shard_map/ppermute | solution.py:52
  13.1 2.4 %collective-permute-start.3 = (bf16[51,32,128]{2,1,0:T(8,128)(2,1)S(1)}, bf16[51,32,128]{2,1,0:T(8,128)(2,1)S(1)}, u32[]{:S(2)}, u32[]{:S(2)}) collective-permute-start(bf16[51,32,128]{2,1,0:T(8,128)(2,1)S(1)} %pack.3.after_ref.own_ref), channel_id=1, source_target_pairs={{1,2},{2,1},{3,4},{4,3},{5,6},{6,5},{7,8},{8,7},{9,10},{10,9},{11,... | collective-permute-start | bytes 1253384 | tf_op jit(solution)/shard_map/ppermute | solution.py:56
  15.5 2.2 %fetch.4 = (bf16[16,1024,128]{2,1,0:T(8,128)(2,1)S(1)}, f32[8,128]{1,0:T(8,128)S(1)}) custom-call(bf16[16,1024,128]{2,1,0:T(8,128)(2,1)} %bitcast.12, bf16[51,32,128]{2,1,0:T(8,128)(2,1)S(1)} %pack.3.after_ref.own_ref), custom_call_target="tpu_custom_call" | custom-call | bytes 8388608 | tf_op jit(solution)/shard_map/fetch/pallas_call | solution.py:119
  17.7 1.6 %places.1.where_ref = s32[32,16]{1,0:T(8,128)S(4)} custom-call(s32[16,16]{1,0:T(8,128)} %bitcast.16, s32[1,16]{1,0:T(1,128)} %bitcast.18, bf16[51,32,128]{2,1,0:T(8,128)(2,1)S(1)} %pack.3.after_ref.own_ref), custom_call_target="tpu_custom_call" | custom-call | bytes 1048576 | tf_op jit(solution)/shard_map/places/pallas_call | solution.py:163
  19.3 3.4 %collective-permute-done.3.odd_ref = bf16[51,32,128]{2,1,0:T(8,128)(2,1)S(1)} collective-permute-done((bf16[51,32,128]{2,1,0:T(8,128)(2,1)S(1)}, bf16[51,32,128]{2,1,0:T(8,128)(2,1)S(1)}, u32[]{:S(2)}, u32[]{:S(2)}) %collective-permute-start.3) | collective-permute-done | bytes 417824 | tf_op jit(solution)/shard_map/ppermute | solution.py:56
  22.8 0.0 collective-permute-done.2.even_ref
  22.8 2.2 %lower.1 = (bf16[16,32,128]{2,1,0:T(8,128)(2,1)S(1)}, s32[16,128]{1,0:T(8,128)S(4)}) custom-call(s32[32,16]{1,0:T(8,128)S(4)} %places.1.where_ref, bf16[51,32,128]{2,1,0:T(8,128)(2,1)S(1)} %pack.3.after_ref.own_ref, bf16[51,32,128]{2,1,0:T(8,128)(2,1)S(1)} %collective-permute-done.2.even_ref, bf16[51,32,128]{2,1,0:T(8,128)(2,1)S(1)} %collective-permute-done.3.odd_ref, ...), custom_call_target="tpu_custom_call" | custom-call | tf_op jit(solution)/shard_map/lower/pallas_call | solution.py:225
  25.0 0.4 collective-permute-start.4
  25.4 3.4 %fetch.5 = (bf16[16,16,128,128]{3,2,1,0:T(8,128)(2,1)S(1)}, f32[8,128]{1,0:T(8,128)S(1)}) custom-call(bf16[16,16,128,128]{3,2,1,0:T(8,128)(2,1)} %bitcast.11, bf16[16,32,128]{2,1,0:T(8,128)(2,1)S(1)} %get-tuple-element.22.after_ref.refs_0_), custom_call_target="tpu_custom_call" | custom-call | bytes 16777216 | tf_op jit(solution)/shard_map/fetch/pallas_call | solution.py:119
  28.8 1.3 %collective-permute-done.4.refs_1_ = bf16[16,32,128]{2,1,0:T(8,128)(2,1)S(1)} collective-permute-done((bf16[16,32,128]{2,1,0:T(8,128)(2,1)S(1)}, bf16[16,32,128]{2,1,0:T(8,128)(2,1)S(1)}, u32[]{:S(2)}, u32[]{:S(2)}) %collective-permute-start.4) | collective-permute-done | bytes 131104 | tf_op jit(solution)/shard_map/ppermute | solution.py:52
  30.0 0.1 collective-permute-start.5
  30.1 1.5 %collective-permute-done.5.far_ref = bf16[32,32,128]{2,1,0:T(8,128)(2,1)S(1)} collective-permute-done((bf16[32,32,128]{2,1,0:T(8,128)(2,1)S(1)}, bf16[32,32,128]{2,1,0:T(8,128)(2,1)S(1)}, u32[]{:S(2)}, u32[]{:S(2)}) %collective-permute-start.5) | collective-permute-done | bytes 262176 | tf_op jit(solution)/shard_map/ppermute | solution.py:52
  31.7 0.7 %parent.1.refs_0_.skel_ref = bf16[16,32,128]{2,1,0:T(8,128)(2,1)S(1)} custom-call(s32[16,128]{1,0:T(8,128)S(4)} %get-tuple-element.21.child_ref, bf16[32,32,128]{2,1,0:T(8,128)(2,1)S(1)} %pack.4.own_ref, bf16[32,32,128]{2,1,0:T(8,128)(2,1)S(1)} %collective-permute-done.5.far_ref, bf16[16,1024,128]{2,1,0:T(8,128)(2,1)S(1)} %get-tuple-element.24.rows_ref), custom_call_target="tpu_custom_call" | custom-call | tf_op jit(solution)/shard_map/parent/pallas_call | solution.py:251
  32.4 4.0 %collective-permute-start.7 = (bf16[16,32,128]{2,1,0:T(8,128)(2,1)S(1)}, bf16[16,32,128]{2,1,0:T(8,128)(2,1)S(1)}, u32[]{:S(2)}, u32[]{:S(2)}) collective-permute-start(bf16[16,32,128]{2,1,0:T(8,128)(2,1)S(1)} %parent.1.refs_0_.skel_ref), channel_id=1, source_target_pairs={{16,32},{32,16},{48,64},{64,48},{80,96},{96,80},{0,112},{112,0},{1... | collective-permute-start | bytes 393224 | tf_op jit(solution)/shard_map/ppermute | solution.py:56
  36.4 0.0 collective-permute-start.6
  36.4 5.3 %collective-permute-done.7.refs_2_ = bf16[16,32,128]{2,1,0:T(8,128)(2,1)S(1)} collective-permute-done((bf16[16,32,128]{2,1,0:T(8,128)(2,1)S(1)}, bf16[16,32,128]{2,1,0:T(8,128)(2,1)S(1)}, u32[]{:S(2)}, u32[]{:S(2)}) %collective-permute-start.7) | collective-permute-done | bytes 131104 | tf_op jit(solution)/shard_map/ppermute | solution.py:56
  41.7 2.1 %collective-permute-start.9 = (bf16[48,32,128]{2,1,0:T(8,128)(2,1)S(1)}, bf16[48,32,128]{2,1,0:T(8,128)(2,1)S(1)}, u32[]{:S(2)}, u32[]{:S(2)}) collective-permute-start(bf16[48,32,128]{2,1,0:T(8,128)(2,1)S(1)} %pack.5.own_ref), channel_id=1, source_target_pairs={{1,2},{2,1},{3,4},{4,3},{5,6},{6,5},{7,8},{8,7},{9,10},{10,9},{11,... | collective-permute-start | bytes 1179656 | tf_op jit(solution)/shard_map/ppermute | solution.py:56
  43.8 7.3 %collective-permute-done.9.odd_ref = bf16[48,32,128]{2,1,0:T(8,128)(2,1)S(1)} collective-permute-done((bf16[48,32,128]{2,1,0:T(8,128)(2,1)S(1)}, bf16[48,32,128]{2,1,0:T(8,128)(2,1)S(1)}, u32[]{:S(2)}, u32[]{:S(2)}) %collective-permute-start.9) | collective-permute-done | bytes 393248 | tf_op jit(solution)/shard_map/ppermute | solution.py:56
  51.1 3.5 %upper.1 = bf16[16,32,256]{2,1,0:T(8,128)(2,1)} custom-call(s32[32,16]{1,0:T(8,128)S(4)} %places.1.where_ref, bf16[48,32,128]{2,1,0:T(8,128)(2,1)S(1)} %pack.5.own_ref, bf16[48,32,128]{2,1,0:T(8,128)(2,1)S(1)} %collective-permute-done.8.even_ref, bf16[48,32,128]{2,1,0:T(8,128)(2,1)S(1)} %collective-permute-done.9.odd_ref, ...), custom_call_target="tpu_custom_call" | custom-call | tf_op jit(solution)/shard_map/upper/pallas_call | solution.py:276
  (7 shorter events, 0.1 us)
Async XLA Ops:
  2.3 9.3 %collective-permute-start.1 = (bf16[17,32,128]{2,1,0:T(8,128)(2,1)S(1)}, bf16[17,32,128]{2,1,0:T(8,128)(2,1)S(1)}, u32[]{:S(2)}, u32[]{:S(2)}) collective-permute-start(bf16[17,32,128]{2,1,0:T(8,128)(2,1)S(1)} %get-tuple-element.16.after_ref.refs_0_.local_ref), channel_id=1, source_target_pairs={{16,32},{32,16},{48,64},{64,48},{80,96},{96,80},{0,112},{112,0},{1... | collective-permute-start | bytes 417800 | tf_op jit(solution)/shard_map/ppermute | solution.py:56
  7.9 5.1 %collective-permute-start = (bf16[17,32,128]{2,1,0:T(8,128)(2,1)S(1)}, bf16[17,32,128]{2,1,0:T(8,128)(2,1)S(1)}, u32[]{:S(2)}, u32[]{:S(2)}) collective-permute-start(bf16[17,32,128]{2,1,0:T(8,128)(2,1)S(1)} %get-tuple-element.16.after_ref.refs_0_.local_ref), channel_id=1, source_target_pairs={{0,16},{16,0},{32,48},{48,32},{64,80},{80,64},{96,112},{112,96},{1... | collective-permute-start | bytes 417800 | tf_op jit(solution)/shard_map/ppermute | solution.py:52
  13.1 9.7 %collective-permute-start.3 = (bf16[51,32,128]{2,1,0:T(8,128)(2,1)S(1)}, bf16[51,32,128]{2,1,0:T(8,128)(2,1)S(1)}, u32[]{:S(2)}, u32[]{:S(2)}) collective-permute-start(bf16[51,32,128]{2,1,0:T(8,128)(2,1)S(1)} %pack.3.after_ref.own_ref), channel_id=1, source_target_pairs={{1,2},{2,1},{3,4},{4,3},{5,6},{6,5},{7,8},{8,7},{9,10},{10,9},{11,... | collective-permute-start | bytes 1253384 | tf_op jit(solution)/shard_map/ppermute | solution.py:56
  15.5 7.3 %collective-permute-start.2 = (bf16[51,32,128]{2,1,0:T(8,128)(2,1)S(1)}, bf16[51,32,128]{2,1,0:T(8,128)(2,1)S(1)}, u32[]{:S(2)}, u32[]{:S(2)}) collective-permute-start(bf16[51,32,128]{2,1,0:T(8,128)(2,1)S(1)} %pack.3.after_ref.own_ref), channel_id=1, source_target_pairs={{0,1},{1,0},{2,3},{3,2},{4,5},{5,4},{6,7},{7,6},{8,9},{9,8},{10,11... | collective-permute-start | bytes 1253384 | tf_op jit(solution)/shard_map/ppermute | solution.py:52
  25.0 5.0 %collective-permute-start.4 = (bf16[16,32,128]{2,1,0:T(8,128)(2,1)S(1)}, bf16[16,32,128]{2,1,0:T(8,128)(2,1)S(1)}, u32[]{:S(2)}, u32[]{:S(2)}) collective-permute-start(bf16[16,32,128]{2,1,0:T(8,128)(2,1)S(1)} %get-tuple-element.22.after_ref.refs_0_), channel_id=1, source_target_pairs={{0,16},{16,0},{32,48},{48,32},{64,80},{80,64},{96,112},{112,96},{1... | collective-permute-start | bytes 393224 | tf_op jit(solution)/shard_map/ppermute | solution.py:52
  30.0 1.6 %collective-permute-start.5 = (bf16[32,32,128]{2,1,0:T(8,128)(2,1)S(1)}, bf16[32,32,128]{2,1,0:T(8,128)(2,1)S(1)}, u32[]{:S(2)}, u32[]{:S(2)}) collective-permute-start(bf16[32,32,128]{2,1,0:T(8,128)(2,1)S(1)} %pack.4.own_ref), channel_id=1, source_target_pairs={{0,1},{1,0},{2,3},{3,2},{4,5},{5,4},{6,7},{7,6},{8,9},{9,8},{10,11... | collective-permute-start | bytes 786440 | tf_op jit(solution)/shard_map/ppermute | solution.py:52
  32.4 9.2 %collective-permute-start.7 = (bf16[16,32,128]{2,1,0:T(8,128)(2,1)S(1)}, bf16[16,32,128]{2,1,0:T(8,128)(2,1)S(1)}, u32[]{:S(2)}, u32[]{:S(2)}) collective-permute-start(bf16[16,32,128]{2,1,0:T(8,128)(2,1)S(1)} %parent.1.refs_0_.skel_ref), channel_id=1, source_target_pairs={{16,32},{32,16},{48,64},{64,48},{80,96},{96,80},{0,112},{112,0},{1... | collective-permute-start | bytes 393224 | tf_op jit(solution)/shard_map/ppermute | solution.py:56
  36.4 5.3 %collective-permute-start.6 = (bf16[16,32,128]{2,1,0:T(8,128)(2,1)S(1)}, bf16[16,32,128]{2,1,0:T(8,128)(2,1)S(1)}, u32[]{:S(2)}, u32[]{:S(2)}) collective-permute-start(bf16[16,32,128]{2,1,0:T(8,128)(2,1)S(1)} %parent.1.refs_0_.skel_ref), channel_id=1, source_target_pairs={{0,16},{16,0},{32,48},{48,32},{64,80},{80,64},{96,112},{112,96},{1... | collective-permute-start | bytes 393224 | tf_op jit(solution)/shard_map/ppermute | solution.py:52
  41.7 9.4 %collective-permute-start.9 = (bf16[48,32,128]{2,1,0:T(8,128)(2,1)S(1)}, bf16[48,32,128]{2,1,0:T(8,128)(2,1)S(1)}, u32[]{:S(2)}, u32[]{:S(2)}) collective-permute-start(bf16[48,32,128]{2,1,0:T(8,128)(2,1)S(1)} %pack.5.own_ref), channel_id=1, source_target_pairs={{1,2},{2,1},{3,4},{4,3},{5,6},{6,5},{7,8},{8,7},{9,10},{10,9},{11,... | collective-permute-start | bytes 1179656 | tf_op jit(solution)/shard_map/ppermute | solution.py:56
  43.8 7.3 %collective-permute-start.8 = (bf16[48,32,128]{2,1,0:T(8,128)(2,1)S(1)}, bf16[48,32,128]{2,1,0:T(8,128)(2,1)S(1)}, u32[]{:S(2)}, u32[]{:S(2)}) collective-permute-start(bf16[48,32,128]{2,1,0:T(8,128)(2,1)S(1)} %pack.5.own_ref), channel_id=1, source_target_pairs={{0,1},{1,0},{2,3},{3,2},{4,5},{5,4},{6,7},{7,6},{8,9},{9,8},{10,11... | collective-permute-start | bytes 1179656 | tf_op jit(solution)/shard_map/ppermute | solution.py:52

commit v3 on v2

v3 whole, which is shorter than its diff:
```python
import functools
import math

import jax
import jax.numpy as jnp
from jax import lax
from jax.experimental import pallas as pl
from jax.experimental.pallas import tpu as pltpu
from jax.sharding import PartitionSpec as P

BF = jnp.bfloat16
F32 = jnp.float32
VM = pl.BlockSpec(memory_space=pltpu.VMEM)
SM = pl.BlockSpec(memory_space=pltpu.SMEM)
HB = pl.BlockSpec(memory_space=pltpu.HBM)
AN = pl.BlockSpec(memory_space=pl.ANY)
TOKEN = pltpu.VMEM((8, 128), F32)


def resident(value):
    return pltpu.with_memory_space_constraint(value, pltpu.VMEM)


def far_memory(value):
    return pltpu.with_memory_space_constraint(value, pltpu.HBM)


def scalars(value):
    return pltpu.with_memory_space_constraint(value, pltpu.SMEM)


def call(kernel, name, ins, outs, scratch=(), moved=0, flops=0):
    return pl.pallas_call(
        kernel,
        in_specs=ins,
        out_specs=[pl.BlockSpec(memory_space=o.memory_space) for o in outs],
        out_shape=list(outs),
        scratch_shapes=list(scratch),
        compiler_params=pltpu.CompilerParams(vmem_limit_bytes=4 << 20),
        cost_estimate=pl.CostEstimate(flops=flops, bytes_accessed=moved, transcendentals=0),
        name=name,
    )


def even_pairs(peers):
    return [(i, i ^ 1) for i in range(peers)]


def odd_pairs(peers):
    return [(i, ((i + 1) ^ 1) - 1) for i in range(1, peers - 1)] + [(0, peers - 1), (peers - 1, 0)]


def even_swap(value, axis):
    return lax.ppermute(value, axis, even_pairs(lax.axis_size(axis)))


def odd_swap(value, axis):
    return lax.ppermute(value, axis, odd_pairs(lax.axis_size(axis)))


def find_places(codes, counts, planes, out_ref):
    height, slots = codes.shape
    one = jnp.int32(1)
    step_x = jnp.where(codes >= 9, one, 0) + jnp.where(codes >= 18, one, 0)
    rest = codes - 9 * step_x
    step_y = jnp.where(rest >= 3, one, 0) + jnp.where(rest >= 6, one, 0)
    step_z = rest - 3 * step_y

    def source(step, axis):
        even_side = 2 - 2 * (lax.axis_index(axis) % 2)
        return jnp.where(step == 1, 0, jnp.where(step == even_side, one, 2))

    active = lax.broadcasted_iota(jnp.int32, (height, slots), 1) < upright(counts)
    column = source(step_y, "by") * 3 + source(step_x, "bx")
    level = lax.broadcasted_iota(jnp.int32, (height, slots), 0) + step_z - 1
    for i, size in enumerate(planes):
        out_ref[i * height : (i + 1) * height] = jnp.where(active, column * size + level, 9 * size)


def upright(row):
    size = row.shape[1]
    level = lax.broadcasted_iota(jnp.int32, (size, size), 0)
    lane = lax.broadcasted_iota(jnp.int32, (size, size), 1)
    return jnp.sum(jnp.where(level == lane, row, 0), axis=1, keepdims=True)


def places_kernel(lists_hbm, counts_hbm, after_ref, out_ref, token_ref, lists_ref, counts_ref, found_ref, sems, *, planes):
    loads = [pltpu.make_async_copy(lists_hbm, lists_ref, sems.at[0]), pltpu.make_async_copy(counts_hbm, counts_ref, sems.at[1])]
    for load in loads:
        load.start()
    for load in loads:
        load.wait()
    find_places(lists_ref[...], counts_ref[...], planes, found_ref)
    copy = pltpu.make_async_copy(found_ref, out_ref, sems.at[2])
    copy.start()
    token_ref[...] = jnp.zeros_like(token_ref)
    copy.wait()


def places(lists, counts, planes, after):
    found = (len(planes) * lists.shape[0], lists.shape[1])
    return call(
        functools.partial(places_kernel, planes=planes),
        "places",
        [HB, HB, AN],
        [pltpu.SMEM(found, jnp.int32), TOKEN],
        [
            pltpu.VMEM(lists.shape, jnp.int32),
            pltpu.VMEM(counts.shape, jnp.int32),
            pltpu.VMEM(found, jnp.int32),
            pltpu.SemaphoreType.DMA((3,)),
        ],
        moved=4 << 20,
    )(far_memory(lists), far_memory(counts), after)


def first_kernel(*refs):
    rhs_hbm, transform_hbm, inverse_hbm, slots_hbm, skel_ref, field_ref, transform_ref = refs[:7]
    rhs_ref, inverse_ref, slots_ref, sems = refs[7:]
    height, rank = inverse_ref.shape[0], inverse_ref.shape[1]
    bounds = (0, height * 3 // 8, height * 3 // 4, height)
    chunks = [slice(i, j) for i, j in zip(bounds[:-1], bounds[1:])]
    loads = [pltpu.make_async_copy(transform_hbm.at[c], transform_ref.at[c], sems.at[i]) for i, c in enumerate(chunks)]
    rhs_load = pltpu.make_async_copy(rhs_hbm, rhs_ref, sems.at[3])
    inverse_load = pltpu.make_async_copy(inverse_hbm, inverse_ref, sems.at[4])
    slots_load = pltpu.make_async_copy(slots_hbm, slots_ref, sems.at[5])
    for copy in (rhs_load, *loads, inverse_load, slots_load):
        copy.start()
    rhs_load.wait()
    redundant = []
    for c, load in zip(chunks, loads):
        load.wait()
        boxes = range(c.start, c.stop)
        projected = [jnp.dot(rhs_ref[z], transform_ref[z], preferred_element_type=F32) for z in boxes]
        for z, rows in zip(boxes, projected):
            skel_ref[z] = rows[:, rank:]
            redundant.append(rows[:, :rank].astype(BF))
    inverse_load.wait()
    for z in range(height):
        field_ref[z] = jnp.dot(redundant[z], inverse_ref[z], preferred_element_type=F32).astype(BF)
    slots_load.wait()
    plane = jnp.broadcast_to(upright(slots_ref[...]), (height, rank)).astype(F32)
    plane = jnp.concatenate([plane, jnp.zeros((field_ref.shape[1] - height, rank), F32)], axis=0)
    field_ref[height] = plane.astype(BF)


def first(right_sides, transform, inverse, slots):
    height, rhs_count, points = right_sides.shape
    rank = inverse.shape[1]
    operands = (right_sides, transform, inverse, slots)
    return call(
        first_kernel,
        "first",
        [HB] * 4,
        [
            pltpu.VMEM((height, rhs_count, rank), F32),
            pltpu.VMEM((height + 1, rhs_count, rank), BF),
            pltpu.VMEM(transform.shape, BF),
        ],
        [
            pltpu.VMEM(right_sides.shape, BF),
            pltpu.VMEM(inverse.shape, BF),
            pltpu.VMEM(slots.shape, jnp.int32),
            pltpu.SemaphoreType.DMA((6,)),
        ],
    )(*map(far_memory, operands))


def fetch_kernel(value_hbm, after_ref, out_ref, token_ref, sem, *, start):
    copy = pltpu.make_async_copy(value_hbm.at[start : start + out_ref.shape[0]], out_ref, sem)
    copy.start()
    token_ref[...] = jnp.zeros_like(token_ref)
    copy.wait()


def fetch(value, after, start, stop):
    shape = (stop - start, *value.shape[1:])
    return call(
        functools.partial(fetch_kernel, start=start),
        "fetch",
        [HB, AN],
        [pltpu.VMEM(shape, value.dtype), TOKEN],
        [pltpu.SemaphoreType.DMA],
        moved=4 * math.prod(shape),
    )(far_memory(value), after)


def pack_kernel(*refs):
    out_ref = refs[-1]
    planes = refs[0].shape[0]
    for i in range(out_ref.shape[0] // planes):
        out_ref[i * planes : (i + 1) * planes] = refs[i][...]


def pack(parts, after):
    planes, rows, cols = parts[0].shape
    shape = pltpu.VMEM((len(parts) * planes, rows, cols), BF)
    return call(pack_kernel, "pack", [VM] * len(parts) + [AN] * len(after), [shape])(*map(resident, parts), *after)[0]


def fill_table(table_ref, parts):
    at = 0
    for part in parts:
        table_ref[at : at + part.shape[0]] = part[...]
        at += part.shape[0]
    table_ref[at] = jnp.zeros(table_ref.shape[1:], BF)


def coupling(table_ref, where_ref, row, fill_ref, z):
    slots, rank = fill_ref.shape[1], fill_ref.shape[2]
    rows = jnp.concatenate([table_ref[where_ref[row, k]] for k in range(slots)], axis=1)
    blocks = fill_ref[z].reshape(slots * rank, fill_ref.shape[3])
    return jnp.dot(rows, blocks, preferred_element_type=F32)


def lower_kernel(*refs):
    parts, refs = refs[1:7], refs[:1] + refs[7:]
    where_ref, skel_ref, fill_ref, after_ref, out_ref, child_ref, table_ref, child_vmem, sem = refs
    height, planes = out_ref.shape[0], parts[1].shape[0]
    lane = lax.broadcasted_iota(jnp.int32, child_vmem.shape, 1)
    level = lax.broadcasted_iota(jnp.int32, child_vmem.shape, 0)
    found = jnp.zeros(child_vmem.shape, jnp.int32)
    columns = [part[at] for part in (parts[0], parts[2]) for at in (height, planes + height)]
    for i, column in enumerate(columns):
        slots = column.astype(F32)[:height].astype(jnp.int32)
        found = found + jnp.where(slots == lane, i * height + level, 0)
    child_vmem[...] = found
    copy = pltpu.make_async_copy(child_vmem, child_ref, sem)
    copy.start()
    fill_table(table_ref, parts)
    for z in range(height):
        out_ref[z] = (skel_ref[z] - coupling(table_ref, where_ref, z, fill_ref, z)).astype(BF)
    copy.wait()


def lower(where, parts, skel, fill, after):
    height, rhs_count, rank = skel.shape
    planes = sum(part.shape[0] for part in parts) + 1
    return call(
        lower_kernel,
        "lower",
        [SM] + [VM] * 8 + [AN],
        [pltpu.VMEM((height, rhs_count, rank), BF), pltpu.SMEM((height, rank), jnp.int32)],
        [
            pltpu.VMEM((planes, rhs_count, rank), BF),
            pltpu.VMEM((height, rank), jnp.int32),
            pltpu.SemaphoreType.DMA,
        ],
    )(scalars(where), *map(resident, (*parts, skel, fill)), after)


def parent_kernel(child_ref, own_ref, far_ref, rows_ref, out_ref, table_ref):
    planes = own_ref.shape[0]
    table_ref[0:planes] = own_ref[...]
    table_ref[planes : 2 * planes] = far_ref[...]
    for i in range(out_ref.shape[0] // 2):
        places = [child_ref[2 * i, s] + child_ref[2 * i + 1, s] for s in range(8)]
        stacked = jnp.concatenate([table_ref[place] for place in places], axis=1)
        for z in (2 * i, 2 * i + 1):
            out_ref[z] = jnp.dot(stacked, rows_ref[z], preferred_element_type=F32).astype(BF)


def parent(child, own, far, rows):
    height, rhs_count, rank = rows.shape[0], own.shape[1], own.shape[2]
    return call(
        parent_kernel,
        "parent",
        [SM, VM, VM, VM],
        [pltpu.VMEM((height, rhs_count, rank), BF)],
        [pltpu.VMEM((2 * own.shape[0], rhs_count, rank), BF)],
    )(scalars(child), resident(own), resident(far), resident(rows))[0]


LAST = (((1,), (1,)), ((), ()))


def half_kernel(skel_ref, transform_ref, out_ref, token_ref):
    rank = skel_ref.shape[2]
    for z in range(out_ref.shape[0]):
        out_ref[z] = lax.dot_general(skel_ref[z], transform_ref[z, :, rank:], LAST, preferred_element_type=F32)
    token_ref[...] = jnp.zeros_like(token_ref)


def half(skel, transform):
    height, rhs_count, rank = skel.shape
    shape = pltpu.VMEM((height, rhs_count, transform.shape[1]), F32)
    return call(half_kernel, "half", [VM, VM], [shape, TOKEN], moved=4 << 20)(resident(skel), resident(transform))


def upper_kernel(*refs):
    parts, refs = refs[1:7], refs[:1] + refs[7:]
    where_ref, base_ref, local_ref, low_ref, high_ref, transform_ref, out_hbm, table_ref, red_ref, out_ref, sems = refs
    fill_table(table_ref, parts)
    height, rank = out_ref.shape[0], local_ref.shape[2]
    for z in range(height):
        fill_ref, at = (low_ref, z) if z < low_ref.shape[0] else (high_ref, z - low_ref.shape[0])
        backward = coupling(table_ref, where_ref, height + z, fill_ref, at)
        red_ref[z] = (local_ref[z].astype(F32) - backward).astype(BF)
    copies = []
    block = height // sems.shape[0]
    for z in range(height):
        solved = lax.dot_general(red_ref[z], transform_ref[z, :, :rank], LAST, preferred_element_type=F32)
        out_ref[z] = (solved + base_ref[z]).astype(BF)
        if (z + 1) % block == 0:
            part = slice(z + 1 - block, z + 1)
            copies.append(pltpu.make_async_copy(out_ref.at[part], out_hbm.at[part], sems.at[z // block]))
            copies[-1].start()
    for copy in copies:
        copy.wait()


def upper(where, parts, base, local, low, high, transform):
    height, rhs_count, points = base.shape
    rank = local.shape[2]
    planes = sum(part.shape[0] for part in parts) + 1
    return call(
        upper_kernel,
        "upper",
        [SM] + [VM] * 11,
        [pltpu.HBM((height, rhs_count, points), BF)],
        [
            pltpu.VMEM((planes, rhs_count, rank), BF),
            pltpu.VMEM((height, rhs_count, rank), BF),
            pltpu.VMEM((height, rhs_count, points), BF),
            pltpu.SemaphoreType.DMA((2,)),
        ],
    )(scalars(where), *map(resident, (*parts, base, local, low, high, transform)))[0]


def halo(field, before, between):
    odd = odd_swap(field, "bx")
    even = even_swap(field, "bx")
    near = pack([field, even], before)
    tokens = between(near)
    if tokens:
        odd = pack([odd], tokens)
    parts = [near, odd]
    for swap in (even_swap, odd_swap):
        parts += [swap(near, "by"), swap(odd, "by")]
    return parts


def body(right_sides, transform, inverse, fill_lower, fill_upper, parent_rows, neighbours, counts, child_slot):
    height = right_sides.shape[2]
    skel, field, transform = first(right_sides[0, 0], transform[0, 0], inverse[0, 0], child_slot[0])
    found = []

    def between(near):
        found.extend(places(neighbours[0, 0], counts[0], (height + 1, height), near))
        return found[1:]

    parts = halo(field, [], between)
    where = found[0]
    fill, _ = fetch(fill_lower[0, 0], parts[1], 0, height)
    reduced, child = lower(where, parts, skel, fill, field)
    rows, rows_token = fetch(parent_rows[0, 0], reduced, 0, height)
    low, low_token = fetch(fill_upper[0, 0], reduced, 0, height // 2)
    pair = pack([reduced, even_swap(reduced, "bx")], [rows_token, low_token])
    skel_sol = parent(child, pair, even_swap(pair, "by"), rows)
    base, base_token = half(skel_sol, transform)
    high = []

    def between(near):
        value, token = fetch(fill_upper[0, 0], near, height // 2, height)
        high.append(value)
        return [token]

    parts = halo(skel_sol, [base_token], between)
    solved = upper(where, parts, base, field, low, high[0], transform)
    return solved[None, None]


def solution(mesh):
    wide = P("bx", "by", None, None, None)
    placed = (wide, wide, wide, P("bx", "by", None, None, None, None), P("bx", "by", None, None, None, None), wide)
    placed = placed + (P("bx", "by", None, None), P("bx", "by", None), P("bx", "by", None))
    return jax.shard_map(body, mesh=mesh, in_specs=placed, out_specs=wide, check_vma=False)
```

time: 54.8 us -> 50.3 us (0.918)
  waiting for transfers between devices: 20.5 us -> 6.35 us
  starting transfers between devices: 14.6 us -> 22.9 us
  Pallas kernels: 19.4 us -> 20.6 us
    ppermute x4 -> x6, waiting for transfers between devices: 16.2 us -> 4.61 us  [odd_swap(): return lax.ppermute(value, axis, odd_pairs(lax.axis_size(axis)))]
    ppermute x4 -> x6, starting transfers between devices: 14.1 us -> 19.1 us  [odd_swap(): return lax.ppermute(value, axis, odd_pairs(lax.axis_size(axis)))]
    ppermute x6 -> x8, starting transfers between devices: 0.49 us -> 3.83 us  [even_swap(): return lax.ppermute(value, axis, even_pairs(lax.axis_size(axis)))]
    ppermute x6 -> x8, waiting for transfers between devices: 4.24 us -> 1.74 us  [even_swap(): return lax.ppermute(value, axis, even_pairs(lax.axis_size(axis)))]
    pallas_call x6 -> x8, Pallas kernels: 17 us -> 18.1 us  [the longest x4 10.6 us: fetch(): call(functools.partial(fetch_kernel, start=start), 'fetch', [HB, AN], [pl...]
  transfers between devices with their start and end apart: 10 -> 14, of which waited for: 7 -> 4; matrix products, arithmetic and copies ran while one was open for 0% -> 0% of each run, Pallas kernels for 19% -> 25%
where the time goes in v3:
time: 50.3 us; the launch traced here: 50 us
  starting transfers between devices  22.9 us (46%)
  Pallas kernels  20.6 us (41%)
  waiting for transfers between devices  6.35 us (13%)
    ppermute x6, starting transfers between devices, odd_swap(): return lax.ppermute(value, axis, odd_pairs(lax.axis_size(axis)))  19.1 us
    pallas_call x4, Pallas kernels, fetch(): call(functools.partial(fetch_kernel, start=start), 'fetch', [HB, AN], [pl...  10.6 us
    ppermute x6, waiting for transfers between devices, odd_swap(): return lax.ppermute(value, axis, odd_pairs(lax.axis_size(axis)))  4.61 us
    ppermute x8, starting transfers between devices, even_swap(): return lax.ppermute(value, axis, even_pairs(lax.axis_size(axis)))  3.83 us
    pallas_call x1, Pallas kernels, upper(): call(upper_kernel, 'upper', [SM] + [VM] * 11, [pltpu.HBM((height, rhs_cou...  2.62 us
    pallas_call x1, Pallas kernels, first(): call(first_kernel, 'first', [HB] * 4, [pltpu.VMEM((height, rhs_count, ran...  2.3 us
    pallas_call x1, Pallas kernels, lower(): call(lower_kernel, 'lower', [SM] + [VM] * 8 + [AN], [pltpu.VMEM((height,...  2.19 us
    ppermute x8, waiting for transfers between devices, even_swap(): return lax.ppermute(value, axis, even_pairs(lax.axis_size(axis)))  1.74 us
  transfers between devices with their start and end apart: 14, of which 4 were waited for; matrix products, arithmetic and copies ran while one was open for 0% of the time, Pallas kernels for 25%

profile of v3, /device:TPU:0, one launch (start us, length us, event | category | flops | bytes accessed | tf_op | source)
XLA Modules:
  0.0 50.0 jit_solution(5003882006747755371)
XLA Ops:
  0.0 2.3 %first.1 = (f32[16,32,128]{2,1,0:T(8,128)S(1)}, bf16[17,32,128]{2,1,0:T(8,128)(2,1)S(1)}, bf16[16,256,256]{2,1,0:T(8,128)(2,1)S(1)}) custom-call(bf16[16,32,256]{2,1,0:T(8,128)(2,1)} %bitcast.16, bf16[16,256,256]{2,1,0:T(8,128)(2,1)} %bitcast.14, bf16[16,128,128]{2,1,0:T(8,128)(2,1)} %bitcast.15, s32[1,16]{1,0:T(1,128)} %bitcast.18), custom_call_target="tpu_custom_call" | custom-call | tf_op jit(solution)/shard_map/first/pallas_call | solution.py:151
  2.3 1.7 %collective-permute-start = (bf16[17,32,128]{2,1,0:T(8,128)(2,1)S(1)}, bf16[17,32,128]{2,1,0:T(8,128)(2,1)S(1)}, u32[]{:S(2)}, u32[]{:S(2)}) collective-permute-start(bf16[17,32,128]{2,1,0:T(8,128)(2,1)S(1)} %get-tuple-element.21.refs_0_.refs_9_.refs_8_), channel_id=1, source_target_pairs={{0,16},{16,0},{32,48},{48,32},{64,80},{80,64},{96,112},{112,96},{1... | collective-permute-start | bytes 417800 | tf_op jit(solution)/shard_map/ppermute | solution.py:54
  4.0 4.6 %collective-permute-start.1 = (bf16[17,32,128]{2,1,0:T(8,128)(2,1)S(1)}, bf16[17,32,128]{2,1,0:T(8,128)(2,1)S(1)}, u32[]{:S(2)}, u32[]{:S(2)}) collective-permute-start(bf16[17,32,128]{2,1,0:T(8,128)(2,1)S(1)} %get-tuple-element.21.refs_0_.refs_9_.refs_8_), channel_id=1, source_target_pairs={{16,32},{32,16},{48,64},{64,48},{80,96},{96,80},{0,112},{112,0},{1... | collective-permute-start | bytes 417800 | tf_op jit(solution)/shard_map/ppermute | solution.py:58
  8.7 3.0 %collective-permute-start.4 = (bf16[34,32,128]{2,1,0:T(8,128)(2,1)S(1)}, bf16[34,32,128]{2,1,0:T(8,128)(2,1)S(1)}, u32[]{:S(2)}, u32[]{:S(2)}) collective-permute-start(bf16[34,32,128]{2,1,0:T(8,128)(2,1)S(1)} %pack.5.after_ref.refs_1_), channel_id=1, source_target_pairs={{1,2},{2,1},{3,4},{4,3},{5,6},{6,5},{7,8},{8,7},{9,10},{10,9},{11,... | collective-permute-start | bytes 835592 | tf_op jit(solution)/shard_map/ppermute | solution.py:58
  11.7 1.6 %places.1 = (s32[32,16]{1,0:T(8,128)S(4)}, f32[8,128]{1,0:T(8,128)S(1)}) custom-call(s32[16,16]{1,0:T(8,128)} %bitcast.17, s32[1,16]{1,0:T(1,128)} %bitcast.19, bf16[34,32,128]{2,1,0:T(8,128)(2,1)S(1)} %pack.5.after_ref.refs_1_), custom_call_target="tpu_custom_call" | custom-call | bytes 4194304 | tf_op jit(solution)/shard_map/places/pallas_call | solution.py:102
  13.4 2.7 %collective-permute-start.5 = (bf16[17,32,128]{2,1,0:T(8,128)(2,1)S(1)}, bf16[17,32,128]{2,1,0:T(8,128)(2,1)S(1)}, u32[]{:S(2)}, u32[]{:S(2)}) collective-permute-start(bf16[17,32,128]{2,1,0:T(8,128)(2,1)S(1)} %pack.6.after_ref.refs_2_), channel_id=1, source_target_pairs={{1,2},{2,1},{3,4},{4,3},{5,6},{6,5},{7,8},{8,7},{9,10},{10,9},{11,... | collective-permute-start | bytes 417800 | tf_op jit(solution)/shard_map/ppermute | solution.py:58
  16.1 4.0 %fetch.4 = (bf16[16,16,128,128]{3,2,1,0:T(8,128)(2,1)S(1)}, f32[8,128]{1,0:T(8,128)}) custom-call(bf16[16,16,128,128]{3,2,1,0:T(8,128)(2,1)} %bitcast.12, bf16[17,32,128]{2,1,0:T(8,128)(2,1)S(1)} %pack.6.after_ref.refs_2_), custom_call_target="tpu_custom_call" | custom-call | bytes 16777216 | tf_op jit(solution)/shard_map/fetch/pallas_call | solution.py:178
  20.1 0.2 collective-permute-done.5.refs_6_
  20.3 2.2 %lower.1 = (bf16[16,32,128]{2,1,0:T(8,128)(2,1)S(1)}, s32[16,128]{1,0:T(8,128)S(4)}) custom-call(s32[32,16]{1,0:T(8,128)S(4)} %get-tuple-element.22.refs_0_, bf16[34,32,128]{2,1,0:T(8,128)(2,1)S(1)} %pack.5.after_ref.refs_1_, bf16[17,32,128]{2,1,0:T(8,128)(2,1)S(1)} %pack.6.after_ref.refs_2_, bf16[34,32,128]{2,1,0:T(8,128)(2,1)S(1)} %collective-permute-done.2.refs_3_, ...), custom_call_target="tpu_custom_call" | custom-call | tf_op jit(solution)/shard_map/lower/pallas_call | solution.py:239
  22.5 1.2 %collective-permute-start.6 = (bf16[16,32,128]{2,1,0:T(8,128)(2,1)S(1)}, bf16[16,32,128]{2,1,0:T(8,128)(2,1)S(1)}, u32[]{:S(2)}, u32[]{:S(2)}) collective-permute-start(bf16[16,32,128]{2,1,0:T(8,128)(2,1)S(1)} %get-tuple-element.27.after_ref.refs_0_), channel_id=1, source_target_pairs={{0,16},{16,0},{32,48},{48,32},{64,80},{80,64},{96,112},{112,96},{1... | collective-permute-start | bytes 393224 | tf_op jit(solution)/shard_map/ppermute | solution.py:54
  23.7 2.2 %fetch.6 = (bf16[8,16,128,128]{3,2,1,0:T(8,128)(2,1)S(1)}, f32[8,128]{1,0:T(8,128)S(1)}) custom-call(bf16[16,16,128,128]{3,2,1,0:T(8,128)(2,1)} %bitcast.10, bf16[16,32,128]{2,1,0:T(8,128)(2,1)S(1)} %get-tuple-element.27.after_ref.refs_0_), custom_call_target="tpu_custom_call" | custom-call | bytes 8388608 | tf_op jit(solution)/shard_map/fetch/pallas_call | solution.py:178
  25.9 2.2 %fetch.5 = (bf16[16,1024,128]{2,1,0:T(8,128)(2,1)S(1)}, f32[8,128]{1,0:T(8,128)S(1)}) custom-call(bf16[16,1024,128]{2,1,0:T(8,128)(2,1)} %bitcast.13, bf16[16,32,128]{2,1,0:T(8,128)(2,1)S(1)} %get-tuple-element.27.after_ref.refs_0_), custom_call_target="tpu_custom_call" | custom-call | bytes 8388608 | tf_op jit(solution)/shard_map/fetch/pallas_call | solution.py:178
  28.1 0.2 collective-permute-done.6.refs_1_
  28.3 0.1 collective-permute-start.7
  28.4 1.5 %collective-permute-done.7.far_ref = bf16[32,32,128]{2,1,0:T(8,128)(2,1)S(1)} collective-permute-done((bf16[32,32,128]{2,1,0:T(8,128)(2,1)S(1)}, bf16[32,32,128]{2,1,0:T(8,128)(2,1)S(1)}, u32[]{:S(2)}, u32[]{:S(2)}) %collective-permute-start.7) | collective-permute-done | bytes 262176 | tf_op jit(solution)/shard_map/ppermute | solution.py:54
  30.0 0.8 %parent.1.skel_ref.refs_0_ = bf16[16,32,128]{2,1,0:T(8,128)(2,1)S(1)} custom-call(s32[16,128]{1,0:T(8,128)S(4)} %get-tuple-element.26.child_ref, bf16[32,32,128]{2,1,0:T(8,128)(2,1)S(1)} %pack.7.own_ref, bf16[32,32,128]{2,1,0:T(8,128)(2,1)S(1)} %collective-permute-done.7.far_ref, bf16[16,1024,128]{2,1,0:T(8,128)(2,1)S(1)} %get-tuple-element.30.rows_ref), custom_call_target="tpu_custom_call" | custom-call | tf_op jit(solution)/shard_map/parent/pallas_call | solution.py:265
  30.7 0.8 %collective-permute-start.8 = (bf16[16,32,128]{2,1,0:T(8,128)(2,1)S(1)}, bf16[16,32,128]{2,1,0:T(8,128)(2,1)S(1)}, u32[]{:S(2)}, u32[]{:S(2)}) collective-permute-start(bf16[16,32,128]{2,1,0:T(8,128)(2,1)S(1)} %parent.1.skel_ref.refs_0_), channel_id=1, source_target_pairs={{0,16},{16,0},{32,48},{48,32},{64,80},{80,64},{96,112},{112,96},{1... | collective-permute-start | bytes 393224 | tf_op jit(solution)/shard_map/ppermute | solution.py:54
  31.6 4.7 %collective-permute-start.9 = (bf16[16,32,128]{2,1,0:T(8,128)(2,1)S(1)}, bf16[16,32,128]{2,1,0:T(8,128)(2,1)S(1)}, u32[]{:S(2)}, u32[]{:S(2)}) collective-permute-start(bf16[16,32,128]{2,1,0:T(8,128)(2,1)S(1)} %parent.1.skel_ref.refs_0_), channel_id=1, source_target_pairs={{16,32},{32,16},{48,64},{64,48},{80,96},{96,80},{0,112},{112,0},{1... | collective-permute-start | bytes 393224 | tf_op jit(solution)/shard_map/ppermute | solution.py:58
  36.2 0.4 half.1
  36.7 1.8 %collective-permute-start.12 = (bf16[32,32,128]{2,1,0:T(8,128)(2,1)S(1)}, bf16[32,32,128]{2,1,0:T(8,128)(2,1)S(1)}, u32[]{:S(2)}, u32[]{:S(2)}) collective-permute-start(bf16[32,32,128]{2,1,0:T(8,128)(2,1)S(1)} %pack.8.after_ref.refs_1_), channel_id=1, source_target_pairs={{1,2},{2,1},{3,4},{4,3},{5,6},{6,5},{7,8},{8,7},{9,10},{10,9},{11,... | collective-permute-start | bytes 786440 | tf_op jit(solution)/shard_map/ppermute | solution.py:58
  38.5 2.2 %fetch.7 = (bf16[8,16,128,128]{3,2,1,0:T(8,128)(2,1)S(1)}, f32[8,128]{1,0:T(8,128)S(1)}) custom-call(bf16[16,16,128,128]{3,2,1,0:T(8,128)(2,1)} %bitcast.11, bf16[32,32,128]{2,1,0:T(8,128)(2,1)S(1)} %pack.8.after_ref.refs_1_), custom_call_target="tpu_custom_call" | custom-call | bytes 8388608 | tf_op jit(solution)/shard_map/fetch/pallas_call | solution.py:178
  40.7 2.2 %collective-permute-start.13 = (bf16[16,32,128]{2,1,0:T(8,128)(2,1)S(1)}, bf16[16,32,128]{2,1,0:T(8,128)(2,1)S(1)}, u32[]{:S(2)}, u32[]{:S(2)}) collective-permute-start(bf16[16,32,128]{2,1,0:T(8,128)(2,1)S(1)} %pack.9.refs_2_), channel_id=1, source_target_pairs={{1,2},{2,1},{3,4},{4,3},{5,6},{6,5},{7,8},{8,7},{9,10},{10,9},{11,... | collective-permute-start | bytes 393224 | tf_op jit(solution)/shard_map/ppermute | solution.py:58
  43.0 4.4 %collective-permute-done.13.refs_6_ = bf16[16,32,128]{2,1,0:T(8,128)(2,1)S(1)} collective-permute-done((bf16[16,32,128]{2,1,0:T(8,128)(2,1)S(1)}, bf16[16,32,128]{2,1,0:T(8,128)(2,1)S(1)}, u32[]{:S(2)}, u32[]{:S(2)}) %collective-permute-start.13) | collective-permute-done | bytes 131104 | tf_op jit(solution)/shard_map/ppermute | solution.py:58
  47.3 2.6 %upper.1 = bf16[16,32,256]{2,1,0:T(8,128)(2,1)} custom-call(s32[32,16]{1,0:T(8,128)S(4)} %get-tuple-element.22.refs_0_, bf16[32,32,128]{2,1,0:T(8,128)(2,1)S(1)} %pack.8.after_ref.refs_1_, bf16[16,32,128]{2,1,0:T(8,128)(2,1)S(1)} %pack.9.refs_2_, bf16[32,32,128]{2,1,0:T(8,128)(2,1)S(1)} %collective-permute-done.10.refs_3_, ...), custom_call_target="tpu_custom_call" | custom-call | tf_op jit(solution)/shard_map/upper/pallas_call | solution.py:316
  (19 shorter events, 0.1 us)
Async XLA Ops:
  2.3 6.4 %collective-permute-start = (bf16[17,32,128]{2,1,0:T(8,128)(2,1)S(1)}, bf16[17,32,128]{2,1,0:T(8,128)(2,1)S(1)}, u32[]{:S(2)}, u32[]{:S(2)}) collective-permute-start(bf16[17,32,128]{2,1,0:T(8,128)(2,1)S(1)} %get-tuple-element.21.refs_0_.refs_9_.refs_8_), channel_id=1, source_target_pairs={{0,16},{16,0},{32,48},{48,32},{64,80},{80,64},{96,112},{112,96},{1... | collective-permute-start | bytes 417800 | tf_op jit(solution)/shard_map/ppermute | solution.py:54
  4.0 9.3 %collective-permute-start.1 = (bf16[17,32,128]{2,1,0:T(8,128)(2,1)S(1)}, bf16[17,32,128]{2,1,0:T(8,128)(2,1)S(1)}, u32[]{:S(2)}, u32[]{:S(2)}) collective-permute-start(bf16[17,32,128]{2,1,0:T(8,128)(2,1)S(1)} %get-tuple-element.21.refs_0_.refs_9_.refs_8_), channel_id=1, source_target_pairs={{16,32},{32,16},{48,64},{64,48},{80,96},{96,80},{0,112},{112,0},{1... | collective-permute-start | bytes 417800 | tf_op jit(solution)/shard_map/ppermute | solution.py:58
  8.7 11.6 %collective-permute-start.4 = (bf16[34,32,128]{2,1,0:T(8,128)(2,1)S(1)}, bf16[34,32,128]{2,1,0:T(8,128)(2,1)S(1)}, u32[]{:S(2)}, u32[]{:S(2)}) collective-permute-start(bf16[34,32,128]{2,1,0:T(8,128)(2,1)S(1)} %pack.5.after_ref.refs_1_), channel_id=1, source_target_pairs={{1,2},{2,1},{3,4},{4,3},{5,6},{6,5},{7,8},{8,7},{9,10},{10,9},{11,... | collective-permute-start | bytes 835592 | tf_op jit(solution)/shard_map/ppermute | solution.py:58
  11.7 8.6 %collective-permute-start.2 = (bf16[34,32,128]{2,1,0:T(8,128)(2,1)S(1)}, bf16[34,32,128]{2,1,0:T(8,128)(2,1)S(1)}, u32[]{:S(2)}, u32[]{:S(2)}) collective-permute-start(bf16[34,32,128]{2,1,0:T(8,128)(2,1)S(1)} %pack.5.after_ref.refs_1_), channel_id=1, source_target_pairs={{0,1},{1,0},{2,3},{3,2},{4,5},{5,4},{6,7},{7,6},{8,9},{9,8},{10,11... | collective-permute-start | bytes 835592 | tf_op jit(solution)/shard_map/ppermute | solution.py:54
  13.4 6.9 %collective-permute-start.5 = (bf16[17,32,128]{2,1,0:T(8,128)(2,1)S(1)}, bf16[17,32,128]{2,1,0:T(8,128)(2,1)S(1)}, u32[]{:S(2)}, u32[]{:S(2)}) collective-permute-start(bf16[17,32,128]{2,1,0:T(8,128)(2,1)S(1)} %pack.6.after_ref.refs_2_), channel_id=1, source_target_pairs={{1,2},{2,1},{3,4},{4,3},{5,6},{6,5},{7,8},{8,7},{9,10},{10,9},{11,... | collective-permute-start | bytes 417800 | tf_op jit(solution)/shard_map/ppermute | solution.py:58
  16.1 4.2 %collective-permute-start.3 = (bf16[17,32,128]{2,1,0:T(8,128)(2,1)S(1)}, bf16[17,32,128]{2,1,0:T(8,128)(2,1)S(1)}, u32[]{:S(2)}, u32[]{:S(2)}) collective-permute-start(bf16[17,32,128]{2,1,0:T(8,128)(2,1)S(1)} %pack.6.after_ref.refs_2_), channel_id=1, source_target_pairs={{0,1},{1,0},{2,3},{3,2},{4,5},{5,4},{6,7},{7,6},{8,9},{9,8},{10,11... | collective-permute-start | bytes 417800 | tf_op jit(solution)/shard_map/ppermute | solution.py:54
  22.5 5.8 %collective-permute-start.6 = (bf16[16,32,128]{2,1,0:T(8,128)(2,1)S(1)}, bf16[16,32,128]{2,1,0:T(8,128)(2,1)S(1)}, u32[]{:S(2)}, u32[]{:S(2)}) collective-permute-start(bf16[16,32,128]{2,1,0:T(8,128)(2,1)S(1)} %get-tuple-element.27.after_ref.refs_0_), channel_id=1, source_target_pairs={{0,16},{16,0},{32,48},{48,32},{64,80},{80,64},{96,112},{112,96},{1... | collective-permute-start | bytes 393224 | tf_op jit(solution)/shard_map/ppermute | solution.py:54
  28.3 1.6 %collective-permute-start.7 = (bf16[32,32,128]{2,1,0:T(8,128)(2,1)S(1)}, bf16[32,32,128]{2,1,0:T(8,128)(2,1)S(1)}, u32[]{:S(2)}, u32[]{:S(2)}) collective-permute-start(bf16[32,32,128]{2,1,0:T(8,128)(2,1)S(1)} %pack.7.own_ref), channel_id=1, source_target_pairs={{0,1},{1,0},{2,3},{3,2},{4,5},{5,4},{6,7},{7,6},{8,9},{9,8},{10,11... | collective-permute-start | bytes 786440 | tf_op jit(solution)/shard_map/ppermute | solution.py:54
  30.7 6.0 %collective-permute-start.8 = (bf16[16,32,128]{2,1,0:T(8,128)(2,1)S(1)}, bf16[16,32,128]{2,1,0:T(8,128)(2,1)S(1)}, u32[]{:S(2)}, u32[]{:S(2)}) collective-permute-start(bf16[16,32,128]{2,1,0:T(8,128)(2,1)S(1)} %parent.1.skel_ref.refs_0_), channel_id=1, source_target_pairs={{0,16},{16,0},{32,48},{48,32},{64,80},{80,64},{96,112},{112,96},{1... | collective-permute-start | bytes 393224 | tf_op jit(solution)/shard_map/ppermute | solution.py:54
  31.6 9.2 %collective-permute-start.9 = (bf16[16,32,128]{2,1,0:T(8,128)(2,1)S(1)}, bf16[16,32,128]{2,1,0:T(8,128)(2,1)S(1)}, u32[]{:S(2)}, u32[]{:S(2)}) collective-permute-start(bf16[16,32,128]{2,1,0:T(8,128)(2,1)S(1)} %parent.1.skel_ref.refs_0_), channel_id=1, source_target_pairs={{16,32},{32,16},{48,64},{64,48},{80,96},{96,80},{0,112},{112,0},{1... | collective-permute-start | bytes 393224 | tf_op jit(solution)/shard_map/ppermute | solution.py:58
  36.7 10.6 %collective-permute-start.12 = (bf16[32,32,128]{2,1,0:T(8,128)(2,1)S(1)}, bf16[32,32,128]{2,1,0:T(8,128)(2,1)S(1)}, u32[]{:S(2)}, u32[]{:S(2)}) collective-permute-start(bf16[32,32,128]{2,1,0:T(8,128)(2,1)S(1)} %pack.8.after_ref.refs_1_), channel_id=1, source_target_pairs={{1,2},{2,1},{3,4},{4,3},{5,6},{6,5},{7,8},{8,7},{9,10},{10,9},{11,... | collective-permute-start | bytes 786440 | tf_op jit(solution)/shard_map/ppermute | solution.py:58
  38.5 8.8 %collective-permute-start.10 = (bf16[32,32,128]{2,1,0:T(8,128)(2,1)S(1)}, bf16[32,32,128]{2,1,0:T(8,128)(2,1)S(1)}, u32[]{:S(2)}, u32[]{:S(2)}) collective-permute-start(bf16[32,32,128]{2,1,0:T(8,128)(2,1)S(1)} %pack.8.after_ref.refs_1_), channel_id=1, source_target_pairs={{0,1},{1,0},{2,3},{3,2},{4,5},{5,4},{6,7},{7,6},{8,9},{9,8},{10,11... | collective-permute-start | bytes 786440 | tf_op jit(solution)/shard_map/ppermute | solution.py:54
  40.7 6.6 %collective-permute-start.13 = (bf16[16,32,128]{2,1,0:T(8,128)(2,1)S(1)}, bf16[16,32,128]{2,1,0:T(8,128)(2,1)S(1)}, u32[]{:S(2)}, u32[]{:S(2)}) collective-permute-start(bf16[16,32,128]{2,1,0:T(8,128)(2,1)S(1)} %pack.9.refs_2_), channel_id=1, source_target_pairs={{1,2},{2,1},{3,4},{4,3},{5,6},{6,5},{7,8},{8,7},{9,10},{10,9},{11,... | collective-permute-start | bytes 393224 | tf_op jit(solution)/shard_map/ppermute | solution.py:58
  43.0 4.4 %collective-permute-start.11 = (bf16[16,32,128]{2,1,0:T(8,128)(2,1)S(1)}, bf16[16,32,128]{2,1,0:T(8,128)(2,1)S(1)}, u32[]{:S(2)}, u32[]{:S(2)}) collective-permute-start(bf16[16,32,128]{2,1,0:T(8,128)(2,1)S(1)} %pack.9.refs_2_), channel_id=1, source_target_pairs={{0,1},{1,0},{2,3},{3,2},{4,5},{5,4},{6,7},{7,6},{8,9},{9,8},{10,11... | collective-permute-start | bytes 393224 | tf_op jit(solution)/shard_map/ppermute | solution.py:54

commit v4 on v3

--- a/solution.py
+++ b/solution.py
@@ -70,11 +70,21 @@
         even_side = 2 - 2 * (lax.axis_index(axis) % 2)
         return jnp.where(step == 1, 0, jnp.where(step == even_side, one, 2))
 
-    active = lax.broadcasted_iota(jnp.int32, (height, slots), 1) < upright(counts)
+    lane = lax.broadcasted_iota(jnp.int32, (height, slots), 1)
     column = source(step_y, "by") * 3 + source(step_x, "bx")
     level = lax.broadcasted_iota(jnp.int32, (height, slots), 0) + step_z - 1
+    active = lane < upright(counts)
+    early = active & (column != 5) & (column != 8)
+    table_column = column - jnp.where(column > 5, one, 0)
     for i, size in enumerate(planes):
-        out_ref[i * height : (i + 1) * height] = jnp.where(active, column * size + level, 9 * size)
+        out_ref[i * height : (i + 1) * height] = jnp.where(early, table_column * size + level, 7 * size)
+    late = jnp.full((height, slots), -one)
+    for i, late_column in enumerate((5, 8)):
+        for step in range(3):
+            hit = active & (column == late_column) & (step_z == step)
+            slot = jnp.sum(jnp.where(hit, lane + 1, 0), axis=1, keepdims=True) - 1
+            late = jnp.where(lane == 3 * i + step, slot, late)
+    out_ref[len(planes) * height :] = late
 
 
 def upright(row):
@@ -84,34 +94,38 @@
     return jnp.sum(jnp.where(level == lane, row, 0), axis=1, keepdims=True)
 
 
-def places_kernel(lists_hbm, counts_hbm, after_ref, out_ref, token_ref, lists_ref, counts_ref, found_ref, sems, *, planes):
+def places_kernel(lists_hbm, counts_hbm, value_hbm, after_ref, out_ref, token_ref, value_ref, *scratch, planes):
+    lists_ref, counts_ref, found_ref, sems = scratch
     loads = [pltpu.make_async_copy(lists_hbm, lists_ref, sems.at[0]), pltpu.make_async_copy(counts_hbm, counts_ref, sems.at[1])]
+    value_load = pltpu.make_async_copy(value_hbm.at[0 : value_ref.shape[0]], value_ref, sems.at[3])
     for load in loads:
         load.start()
+    value_load.start()
     for load in loads:
         load.wait()
     find_places(lists_ref[...], counts_ref[...], planes, found_ref)
     copy = pltpu.make_async_copy(found_ref, out_ref, sems.at[2])
     copy.start()
     token_ref[...] = jnp.zeros_like(token_ref)
+    value_load.wait()
     copy.wait()
 
 
-def places(lists, counts, planes, after):
-    found = (len(planes) * lists.shape[0], lists.shape[1])
+def places(lists, counts, planes, value, boxes, after):
+    found = ((len(planes) + 1) * lists.shape[0], lists.shape[1])
     return call(
         functools.partial(places_kernel, planes=planes),
         "places",
-        [HB, HB, AN],
-        [pltpu.SMEM(found, jnp.int32), TOKEN],
+        [HB, HB, HB, AN],
+        [pltpu.SMEM(found, jnp.int32), TOKEN, pltpu.VMEM((boxes, *value.shape[1:]), BF)],
         [
             pltpu.VMEM(lists.shape, jnp.int32),
             pltpu.VMEM(counts.shape, jnp.int32),
             pltpu.VMEM(found, jnp.int32),
-            pltpu.SemaphoreType.DMA((3,)),
+            pltpu.SemaphoreType.DMA((4,)),
         ],
         moved=4 << 20,
-    )(far_memory(lists), far_memory(counts), after)
+    )(far_memory(lists), far_memory(counts), far_memory(value), after)
 
 
 def first_kernel(*refs):
@@ -206,17 +220,34 @@
     table_ref[at] = jnp.zeros(table_ref.shape[1:], BF)
 
 
-def coupling(table_ref, where_ref, row, fill_ref, z):
-    slots, rank = fill_ref.shape[1], fill_ref.shape[2]
+def coupling(table_ref, where_ref, row, blocks_ref):
+    slots, rank = blocks_ref.shape[0], blocks_ref.shape[1]
     rows = jnp.concatenate([table_ref[where_ref[row, k]] for k in range(slots)], axis=1)
-    blocks = fill_ref[z].reshape(slots * rank, fill_ref.shape[3])
-    return jnp.dot(rows, blocks, preferred_element_type=F32)
-
-
-def lower_kernel(*refs):
-    parts, refs = refs[1:7], refs[:1] + refs[7:]
-    where_ref, skel_ref, fill_ref, after_ref, out_ref, child_ref, table_ref, child_vmem, sem = refs
-    height, planes = out_ref.shape[0], parts[1].shape[0]
+    return jnp.dot(rows, blocks_ref[...].reshape(slots * rank, rank), preferred_element_type=F32)
+
+
+def late_coupling(columns, where_ref, row, blocks_ref, z, height):
+    rows, blocks = [], []
+    for i, column_ref in enumerate(columns):
+        for step in range(3):
+            if 0 <= z + step - 1 < height:
+                slot = where_ref[row, 3 * i + step]
+                plane = column_ref[z + step - 1]
+                rows.append(jnp.where(slot >= 0, plane, jnp.zeros_like(plane)))
+                blocks.append(blocks_ref[jnp.maximum(slot, 0)])
+    return jnp.dot(jnp.concatenate(rows, axis=1), jnp.concatenate(blocks, axis=0), preferred_element_type=F32)
+
+
+def early_lower_kernel(*refs):
+    where_ref, parts, refs = refs[0], [refs[i] for i in (4, 3, 2, 1)], refs[5:]
+    skel_ref, low_ref, fill_hbm, out_ref, child_ref, high_ref, table_ref, child_vmem, sems = refs
+    height, planes, done = out_ref.shape[0], parts[1].shape[0], low_ref.shape[0]
+    block = high_ref.shape[0] // (sems.shape[0] - 1)
+    loads = []
+    for i in range(sems.shape[0] - 1):
+        source = fill_hbm.at[done + i * block : done + (i + 1) * block]
+        loads.append(pltpu.make_async_copy(source, high_ref.at[i * block : (i + 1) * block], sems.at[i]))
+        loads[-1].start()
     lane = lax.broadcasted_iota(jnp.int32, child_vmem.shape, 1)
     level = lax.broadcasted_iota(jnp.int32, child_vmem.shape, 0)
     found = jnp.zeros(child_vmem.shape, jnp.int32)
@@ -225,28 +256,49 @@
         slots = column.astype(F32)[:height].astype(jnp.int32)
         found = found + jnp.where(slots == lane, i * height + level, 0)
     child_vmem[...] = found
-    copy = pltpu.make_async_copy(child_vmem, child_ref, sem)
+    copy = pltpu.make_async_copy(child_vmem, child_ref, sems.at[len(loads)])
     copy.start()
     fill_table(table_ref, parts)
     for z in range(height):
-        out_ref[z] = (skel_ref[z] - coupling(table_ref, where_ref, z, fill_ref, z)).astype(BF)
+        if z >= done and (z - done) % block == 0:
+            loads[(z - done) // block].wait()
+        blocks_ref = low_ref.at[z] if z < done else high_ref.at[z - done]
+        out_ref[z] = skel_ref[z] - coupling(table_ref, where_ref, z, blocks_ref)
     copy.wait()
 
 
-def lower(where, parts, skel, fill, after):
+def early_lower(where, parts, skel, low, fill):
     height, rhs_count, rank = skel.shape
     planes = sum(part.shape[0] for part in parts) + 1
     return call(
-        lower_kernel,
-        "lower",
-        [SM] + [VM] * 8 + [AN],
-        [pltpu.VMEM((height, rhs_count, rank), BF), pltpu.SMEM((height, rank), jnp.int32)],
+        early_lower_kernel,
+        "early_lower",
+        [SM] + [VM] * 6 + [HB],
+        [
+            pltpu.VMEM((height, rhs_count, rank), F32),
+            pltpu.SMEM((height, rank), jnp.int32),
+            pltpu.VMEM((height - low.shape[0], *fill.shape[1:]), BF),
+        ],
         [
             pltpu.VMEM((planes, rhs_count, rank), BF),
             pltpu.VMEM((height, rank), jnp.int32),
-            pltpu.SemaphoreType.DMA,
+            pltpu.SemaphoreType.DMA((5,)),
         ],
-    )(scalars(where), *map(resident, (*parts, skel, fill)), after)
+        moved=16 << 20,
+    )(scalars(where), *map(resident, (*parts[::-1], skel, low)), far_memory(fill))
+
+
+def late_lower_kernel(where_ref, odd_ref, even_ref, base_ref, low_ref, high_ref, out_ref):
+    height, done = out_ref.shape[0], low_ref.shape[0]
+    for z in range(height):
+        blocks_ref = low_ref.at[z] if z < done else high_ref.at[z - done]
+        out_ref[z] = (base_ref[z] - late_coupling((even_ref, odd_ref), where_ref, 2 * height + z, blocks_ref, z, height)).astype(BF)
+
+
+def late_lower(where, columns, base, low, high):
+    shape = pltpu.VMEM(base.shape, BF)
+    operands = (*columns[::-1], base, low, high)
+    return call(late_lower_kernel, "late_lower", [SM] + [VM] * 5, [shape])(scalars(where), *map(resident, operands))[0]
 
 
 def parent_kernel(child_ref, own_ref, far_ref, rows_ref, out_ref, table_ref):
@@ -287,20 +339,40 @@
     return call(half_kernel, "half", [VM, VM], [shape, TOKEN], moved=4 << 20)(resident(skel), resident(transform))
 
 
-def upper_kernel(*refs):
-    parts, refs = refs[1:7], refs[:1] + refs[7:]
-    where_ref, base_ref, local_ref, low_ref, high_ref, transform_ref, out_hbm, table_ref, red_ref, out_ref, sems = refs
+def early_upper_kernel(*refs):
+    where_ref, parts, refs = refs[0], [refs[i] for i in (4, 3, 2, 1)], refs[5:]
+    local_ref, low_ref, high_ref, out_ref, table_ref = refs
     fill_table(table_ref, parts)
-    height, rank = out_ref.shape[0], local_ref.shape[2]
-    for z in range(height):
-        fill_ref, at = (low_ref, z) if z < low_ref.shape[0] else (high_ref, z - low_ref.shape[0])
-        backward = coupling(table_ref, where_ref, height + z, fill_ref, at)
-        red_ref[z] = (local_ref[z].astype(F32) - backward).astype(BF)
+    height, done = out_ref.shape[0], low_ref.shape[0]
+    for z in range(height):
+        blocks_ref = low_ref.at[z] if z < done else high_ref.at[z - done]
+        out_ref[z] = local_ref[z].astype(F32) - coupling(table_ref, where_ref, height + z, blocks_ref)
+
+
+def early_upper(where, parts, local, low, high):
+    height, rhs_count, rank = parts[1].shape
+    planes = sum(part.shape[0] for part in parts) + 1
+    return call(
+        early_upper_kernel,
+        "early_upper",
+        [SM] + [VM] * 7,
+        [pltpu.VMEM((height, rhs_count, rank), F32)],
+        [pltpu.VMEM((planes, rhs_count, rank), BF)],
+        moved=16 << 20,
+    )(scalars(where), *map(resident, (*parts[::-1], local, low, high)))[0]
+
+
+def late_upper_kernel(where_ref, odd_ref, even_ref, base_ref, solved_ref, low_ref, high_ref, transform_ref, out_hbm, red_ref, out_ref, sems):
+    height, rank, done = base_ref.shape[0], base_ref.shape[2], low_ref.shape[0]
+    for z in range(height):
+        blocks_ref = low_ref.at[z] if z < done else high_ref.at[z - done]
+        backward = late_coupling((even_ref, odd_ref), where_ref, 2 * height + z, blocks_ref, z, height)
+        red_ref[z] = (base_ref[z] - backward).astype(BF)
     copies = []
     block = height // sems.shape[0]
     for z in range(height):
         solved = lax.dot_general(red_ref[z], transform_ref[z, :, :rank], LAST, preferred_element_type=F32)
-        out_ref[z] = (solved + base_ref[z]).astype(BF)
+        out_ref[z] = (solved + solved_ref[z]).astype(BF)
         if (z + 1) % block == 0:
             part = slice(z + 1 - block, z + 1)
             copies.append(pltpu.make_async_copy(out_ref.at[part], out_hbm.at[part], sems.at[z // block]))
@@ -309,22 +381,15 @@
         copy.wait()
 
 
-def upper(where, parts, base, local, low, high, transform):
-    height, rhs_count, points = base.shape
-    rank = local.shape[2]
-    planes = sum(part.shape[0] for part in parts) + 1
-    return call(
-        upper_kernel,
-        "upper",
-        [SM] + [VM] * 11,
-        [pltpu.HBM((height, rhs_count, points), BF)],
-        [
-            pltpu.VMEM((planes, rhs_count, rank), BF),
-            pltpu.VMEM((height, rhs_count, rank), BF),
-            pltpu.VMEM((height, rhs_count, points), BF),
-            pltpu.SemaphoreType.DMA((2,)),
-        ],
-    )(scalars(where), *map(resident, (*parts, base, local, low, high, transform)))[0]
+def late_upper(where, columns, base, solved, low, high, transform):
+    operands = (*columns[::-1], base, solved, low, high, transform)
+    return call(
+        late_upper_kernel,
+        "late_upper",
+        [SM] + [VM] * 7,
+        [pltpu.HBM(solved.shape, BF)],
+        [pltpu.VMEM(base.shape, BF), pltpu.VMEM(solved.shape, BF), pltpu.SemaphoreType.DMA((2,))],
+    )(scalars(where), *map(resident, operands))[0]
 
 
 def halo(field, before, between):
@@ -332,12 +397,11 @@
     even = even_swap(field, "bx")
     near = pack([field, even], before)
     tokens = between(near)
-    if tokens:
-        odd = pack([odd], tokens)
-    parts = [near, odd]
-    for swap in (even_swap, odd_swap):
-        parts += [swap(near, "by"), swap(odd, "by")]
-    return parts
+    odd = pack([odd], tokens)
+    for _ in range(3):
+        odd = pack([odd], [])
+    early = [near, odd, even_swap(near, "by"), odd_swap(near, "by")]
+    return early, [even_swap(odd, "by"), odd_swap(odd, "by")]
 
 
 def body(right_sides, transform, inverse, fill_lower, fill_upper, parent_rows, neighbours, counts, child_slot):
@@ -346,18 +410,18 @@
     found = []
 
     def between(near):
-        found.extend(places(neighbours[0, 0], counts[0], (height + 1, height), near))
-        return found[1:]
-
-    parts = halo(field, [], between)
-    where = found[0]
-    fill, _ = fetch(fill_lower[0, 0], parts[1], 0, height)
-    reduced, child = lower(where, parts, skel, fill, field)
+        found.extend(places(neighbours[0, 0], counts[0], (height + 1, height), fill_lower[0, 0], height // 4, near))
+        return found[1:2]
+
+    early, late = halo(field, [], between)
+    where, _, low = found
+    base, child, high = early_lower(where, early, skel, low, fill_lower[0, 0])
+    reduced = late_lower(where, late, base, low, high)
     rows, rows_token = fetch(parent_rows[0, 0], reduced, 0, height)
     low, low_token = fetch(fill_upper[0, 0], reduced, 0, height // 2)
     pair = pack([reduced, even_swap(reduced, "bx")], [rows_token, low_token])
     skel_sol = parent(child, pair, even_swap(pair, "by"), rows)
-    base, base_token = half(skel_sol, transform)
+    solved, solved_token = half(skel_sol, transform)
     high = []
 
     def between(near):
@@ -365,8 +429,9 @@
         high.append(value)
         return [token]
 
-    parts = halo(skel_sol, [base_token], between)
-    solved = upper(where, parts, base, field, low, high[0], transform)
+    early, late = halo(skel_sol, [solved_token], between)
+    base = early_upper(where, early, field, low, high[0])
+    solved = late_upper(where, late, base, solved, low, high[0], transform)
     return solved[None, None]
 
 

time: 50.3 us -> 49.5 us (0.984)
  waiting for transfers between devices: 6.35 us -> 10.7 us
  starting transfers between devices: 22.9 us -> 18.9 us
  Pallas kernels: 20.6 us -> 19.5 us
    pallas_call x4 -> x3, Pallas kernels: 10.6 us -> 6.6 us  [fetch(): call(functools.partial(fetch_kernel, start=start), 'fetch', [HB, AN], [pl...]
    ppermute x6, starting transfers between devices: 19.1 us -> 15.4 us  [odd_swap(): return lax.ppermute(value, axis, odd_pairs(lax.axis_size(axis)))]
    ppermute x6, waiting for transfers between devices: 4.61 us -> 7.84 us  [odd_swap(): return lax.ppermute(value, axis, odd_pairs(lax.axis_size(axis)))]
    pallas_call x2 -> x4, Pallas kernels: 4.81 us -> 7.4 us  [the longest x1 3.64 us: early_lower(): call(early_lower_kernel, 'early_lower', [SM] + [VM] * 6 + [HB], [pltpu.VM...]
    ppermute x8, waiting for transfers between devices: 1.74 us -> 2.88 us  [even_swap(): return lax.ppermute(value, axis, even_pairs(lax.axis_size(axis)))]
  transfers between devices with their start and end apart: 14 -> 14, of which waited for: 4 -> 7; matrix products, arithmetic and copies ran while one was open for 0% -> 0% of each run, Pallas kernels for 25% -> 29%
where the time goes in v4:
time: 49.5 us; the launch traced here: 49.3 us
  Pallas kernels  19.5 us (39%)
  starting transfers between devices  18.9 us (38%)
  waiting for transfers between devices  10.7 us (22%)
    ppermute x6, starting transfers between devices, odd_swap(): return lax.ppermute(value, axis, odd_pairs(lax.axis_size(axis)))  15.4 us
    ppermute x6, waiting for transfers between devices, odd_swap(): return lax.ppermute(value, axis, odd_pairs(lax.axis_size(axis)))  7.84 us
    pallas_call x3, Pallas kernels, fetch(): call(functools.partial(fetch_kernel, start=start), 'fetch', [HB, AN], [pl...  6.6 us
    pallas_call x1, Pallas kernels, early_lower(): call(early_lower_kernel, 'early_lower', [SM] + [VM] * 6 + [HB], [pltpu.VM...  3.64 us
    ppermute x8, starting transfers between devices, even_swap(): return lax.ppermute(value, axis, even_pairs(lax.axis_size(axis)))  3.49 us
    ppermute x8, waiting for transfers between devices, even_swap(): return lax.ppermute(value, axis, even_pairs(lax.axis_size(axis)))  2.88 us
    pallas_call x1, Pallas kernels, first(): call(first_kernel, 'first', [HB] * 4, [pltpu.VMEM((height, rhs_count, ran...  2.3 us
    pallas_call x1, Pallas kernels, places(): call(functools.partial(places_kernel, planes=planes), 'places', [HB, HB,...  1.86 us
  transfers between devices with their start and end apart: 14, of which 7 were waited for; matrix products, arithmetic and copies ran while one was open for 0% of the time, Pallas kernels for 29%

profile of v4, /device:TPU:0, one launch (start us, length us, event | category | flops | bytes accessed | tf_op | source)
XLA Modules:
  0.0 49.3 jit_solution(1203633037019288527)
XLA Ops:
  0.0 2.3 %first.1 = (f32[16,32,128]{2,1,0:T(8,128)S(1)}, bf16[17,32,128]{2,1,0:T(8,128)(2,1)S(1)}, bf16[16,256,256]{2,1,0:T(8,128)(2,1)S(1)}) custom-call(bf16[16,32,256]{2,1,0:T(8,128)(2,1)} %bitcast.17, bf16[16,256,256]{2,1,0:T(8,128)(2,1)} %bitcast.15, bf16[16,128,128]{2,1,0:T(8,128)(2,1)} %bitcast.16, s32[1,16]{1,0:T(1,128)} %bitcast.19), custom_call_target="tpu_custom_call" | custom-call | tf_op jit(solution)/shard_map/first/pallas_call | solution.py:165
  2.3 1.7 %collective-permute-start = (bf16[17,32,128]{2,1,0:T(8,128)(2,1)S(1)}, bf16[17,32,128]{2,1,0:T(8,128)(2,1)S(1)}, u32[]{:S(2)}, u32[]{:S(2)}) collective-permute-start(bf16[17,32,128]{2,1,0:T(8,128)(2,1)S(1)} %get-tuple-element.22.refs_0_.refs_5_), channel_id=1, source_target_pairs={{0,16},{16,0},{32,48},{48,32},{64,80},{80,64},{96,112},{112,96},{1... | collective-permute-start | bytes 417800 | tf_op jit(solution)/shard_map/ppermute | solution.py:54
  4.0 4.6 %collective-permute-start.3 = (bf16[17,32,128]{2,1,0:T(8,128)(2,1)S(1)}, bf16[17,32,128]{2,1,0:T(8,128)(2,1)S(1)}, u32[]{:S(2)}, u32[]{:S(2)}) collective-permute-start(bf16[17,32,128]{2,1,0:T(8,128)(2,1)S(1)} %get-tuple-element.22.refs_0_.refs_5_), channel_id=1, source_target_pairs={{16,32},{32,16},{48,64},{64,48},{80,96},{96,80},{0,112},{112,0},{1... | collective-permute-start | bytes 417800 | tf_op jit(solution)/shard_map/ppermute | solution.py:58
  8.7 3.0 %collective-permute-start.1 = (bf16[34,32,128]{2,1,0:T(8,128)(2,1)S(1)}, bf16[34,32,128]{2,1,0:T(8,128)(2,1)S(1)}, u32[]{:S(2)}, u32[]{:S(2)}) collective-permute-start(bf16[34,32,128]{2,1,0:T(8,128)(2,1)S(1)} %pack.11.after_ref.refs_4_), channel_id=1, source_target_pairs={{1,2},{2,1},{3,4},{4,3},{5,6},{6,5},{7,8},{8,7},{9,10},{10,9},{11,... | collective-permute-start | bytes 835592 | tf_op jit(solution)/shard_map/ppermute | solution.py:58
  11.7 1.9 %places.1 = (s32[48,16]{1,0:T(8,128)S(4)}, f32[8,128]{1,0:T(8,128)S(1)}, bf16[4,16,128,128]{3,2,1,0:T(8,128)(2,1)S(1)}) custom-call(s32[16,16]{1,0:T(8,128)} %bitcast.18, s32[1,16]{1,0:T(1,128)} %bitcast.20, bf16[16,16,128,128]{3,2,1,0:T(8,128)(2,1)} %bitcast.10, bf16[34,32,128]{2,1,0:T(8,128)(2,1)S(1)} %pack.11.after_ref.refs_4_), custom_call_target="tpu_custom_call" | custom-call | bytes 4194304 | tf_op jit(solution)/shard_map/places/pallas_call | solution.py:116
  13.7 2.5 %collective-permute-start.4 = (bf16[17,32,128]{2,1,0:T(8,128)(2,1)S(1)}, bf16[17,32,128]{2,1,0:T(8,128)(2,1)S(1)}, u32[]{:S(2)}, u32[]{:S(2)}) collective-permute-start(bf16[17,32,128]{2,1,0:T(8,128)(2,1)S(1)} %pack.15.refs_3_), channel_id=1, source_target_pairs={{1,2},{2,1},{3,4},{4,3},{5,6},{6,5},{7,8},{8,7},{9,10},{10,9},{11,... | collective-permute-start | bytes 417800 | tf_op jit(solution)/shard_map/ppermute | solution.py:58
  16.2 2.7 %collective-permute-done.1.refs_1_ = bf16[34,32,128]{2,1,0:T(8,128)(2,1)S(1)} collective-permute-done((bf16[34,32,128]{2,1,0:T(8,128)(2,1)S(1)}, bf16[34,32,128]{2,1,0:T(8,128)(2,1)S(1)}, u32[]{:S(2)}, u32[]{:S(2)}) %collective-permute-start.1) | collective-permute-done | bytes 278560 | tf_op jit(solution)/shard_map/ppermute | solution.py:58
  18.8 3.6 %early_lower.1 = (f32[16,32,128]{2,1,0:T(8,128)S(1)}, s32[16,128]{1,0:T(8,128)S(4)}, bf16[12,16,128,128]{3,2,1,0:T(8,128)(2,1)S(1)}) custom-call(s32[48,16]{1,0:T(8,128)S(4)} %get-tuple-element.23.refs_0_.where_ref, bf16[34,32,128]{2,1,0:T(8,128)(2,1)S(1)} %collective-permute-done.1.refs_1_, bf16[34,32,128]{2,1,0:T(8,128)(2,1)S(1)} %collective-permute-done.2.refs_2_, ...), custom_call_target="tpu_custom_call" | custom-call | bytes 16777216 | tf_op jit(solution)/shard_map/early_lower/pallas_call | solution.py:273
  22.5 0.6 %late_lower.1.after_ref.refs_0_ = bf16[16,32,128]{2,1,0:T(8,128)(2,1)S(1)} custom-call(s32[48,16]{1,0:T(8,128)S(4)} %get-tuple-element.23.refs_0_.where_ref, bf16[17,32,128]{2,1,0:T(8,128)(2,1)S(1)} %collective-permute-done.4.odd_ref, bf16[17,32,128]{2,1,0:T(8,128)(2,1)S(1)} %collective-permute-done.5.even_ref, ...), custom_call_target="tpu_custom_call" | custom-call | tf_op jit(solution)/shard_map/late_lower/pallas_call | solution.py:301
  23.2 2.2 %fetch.3 = (bf16[16,1024,128]{2,1,0:T(8,128)(2,1)S(1)}, f32[8,128]{1,0:T(8,128)S(1)}) custom-call(bf16[16,1024,128]{2,1,0:T(8,128)(2,1)} %bitcast.14, bf16[16,32,128]{2,1,0:T(8,128)(2,1)S(1)} %late_lower.1.after_ref.refs_0_), custom_call_target="tpu_custom_call" | custom-call | bytes 8388608 | tf_op jit(solution)/shard_map/fetch/pallas_call | solution.py:192
  25.4 2.2 %fetch.4 = (bf16[8,16,128,128]{3,2,1,0:T(8,128)(2,1)S(1)}, f32[8,128]{1,0:T(8,128)S(1)}) custom-call(bf16[16,16,128,128]{3,2,1,0:T(8,128)(2,1)} %bitcast.12, bf16[16,32,128]{2,1,0:T(8,128)(2,1)S(1)} %late_lower.1.after_ref.refs_0_), custom_call_target="tpu_custom_call" | custom-call | bytes 8388608 | tf_op jit(solution)/shard_map/fetch/pallas_call | solution.py:192
  28.3 1.5 %collective-permute-done.7.far_ref = bf16[32,32,128]{2,1,0:T(8,128)(2,1)S(1)} collective-permute-done((bf16[32,32,128]{2,1,0:T(8,128)(2,1)S(1)}, bf16[32,32,128]{2,1,0:T(8,128)(2,1)S(1)}, u32[]{:S(2)}, u32[]{:S(2)}) %collective-permute-start.7) | collective-permute-done | bytes 262176 | tf_op jit(solution)/shard_map/ppermute | solution.py:54
  29.8 0.7 %parent.1.skel_ref.refs_0_ = bf16[16,32,128]{2,1,0:T(8,128)(2,1)S(1)} custom-call(s32[16,128]{1,0:T(8,128)S(4)} %get-tuple-element.27.child_ref, bf16[32,32,128]{2,1,0:T(8,128)(2,1)S(1)} %pack.16.own_ref, bf16[32,32,128]{2,1,0:T(8,128)(2,1)S(1)} %collective-permute-done.7.far_ref, bf16[16,1024,128]{2,1,0:T(8,128)(2,1)S(1)} %get-tuple-element.32.rows_ref), custom_call_target="tpu_custom_call" | custom-call | tf_op jit(solution)/shard_map/parent/pallas_call | solution.py:317
  30.5 1.6 %collective-permute-start.9 = (bf16[16,32,128]{2,1,0:T(8,128)(2,1)S(1)}, bf16[16,32,128]{2,1,0:T(8,128)(2,1)S(1)}, u32[]{:S(2)}, u32[]{:S(2)}) collective-permute-start(bf16[16,32,128]{2,1,0:T(8,128)(2,1)S(1)} %parent.1.skel_ref.refs_0_), channel_id=1, source_target_pairs={{0,16},{16,0},{32,48},{48,32},{64,80},{80,64},{96,112},{112,96},{1... | collective-permute-start | bytes 393224 | tf_op jit(solution)/shard_map/ppermute | solution.py:54
  32.1 2.8 %collective-permute-start.8 = (bf16[16,32,128]{2,1,0:T(8,128)(2,1)S(1)}, bf16[16,32,128]{2,1,0:T(8,128)(2,1)S(1)}, u32[]{:S(2)}, u32[]{:S(2)}) collective-permute-start(bf16[16,32,128]{2,1,0:T(8,128)(2,1)S(1)} %parent.1.skel_ref.refs_0_), channel_id=1, source_target_pairs={{16,32},{32,16},{48,64},{64,48},{80,96},{96,80},{0,112},{112,0},{1... | collective-permute-start | bytes 393224 | tf_op jit(solution)/shard_map/ppermute | solution.py:58
  35.4 0.8 %collective-permute-done.9.refs_1_ = bf16[16,32,128]{2,1,0:T(8,128)(2,1)S(1)} collective-permute-done((bf16[16,32,128]{2,1,0:T(8,128)(2,1)S(1)}, bf16[16,32,128]{2,1,0:T(8,128)(2,1)S(1)}, u32[]{:S(2)}, u32[]{:S(2)}) %collective-permute-start.9) | collective-permute-done | bytes 131104 | tf_op jit(solution)/shard_map/ppermute | solution.py:54
  36.2 1.0 %collective-permute-start.12 = (bf16[32,32,128]{2,1,0:T(8,128)(2,1)S(1)}, bf16[32,32,128]{2,1,0:T(8,128)(2,1)S(1)}, u32[]{:S(2)}, u32[]{:S(2)}) collective-permute-start(bf16[32,32,128]{2,1,0:T(8,128)(2,1)S(1)} %pack.17.after_ref.refs_4_), channel_id=1, source_target_pairs={{1,2},{2,1},{3,4},{4,3},{5,6},{6,5},{7,8},{8,7},{9,10},{10,9},{11,... | collective-permute-start | bytes 786440 | tf_op jit(solution)/shard_map/ppermute | solution.py:58
  37.2 2.2 %fetch.5 = (bf16[8,16,128,128]{3,2,1,0:T(8,128)(2,1)S(1)}, f32[8,128]{1,0:T(8,128)S(1)}) custom-call(bf16[16,16,128,128]{3,2,1,0:T(8,128)(2,1)} %bitcast.13, bf16[32,32,128]{2,1,0:T(8,128)(2,1)S(1)} %pack.17.after_ref.refs_4_), custom_call_target="tpu_custom_call" | custom-call | bytes 8388608 | tf_op jit(solution)/shard_map/fetch/pallas_call | solution.py:192
  39.4 1.6 %collective-permute-done.8.refs_0_ = bf16[16,32,128]{2,1,0:T(8,128)(2,1)S(1)} collective-permute-done((bf16[16,32,128]{2,1,0:T(8,128)(2,1)S(1)}, bf16[16,32,128]{2,1,0:T(8,128)(2,1)S(1)}, u32[]{:S(2)}, u32[]{:S(2)}) %collective-permute-start.8) | collective-permute-done | bytes 131104 | tf_op jit(solution)/shard_map/ppermute | solution.py:58
  41.0 1.4 %collective-permute-start.10 = (bf16[16,32,128]{2,1,0:T(8,128)(2,1)S(1)}, bf16[16,32,128]{2,1,0:T(8,128)(2,1)S(1)}, u32[]{:S(2)}, u32[]{:S(2)}) collective-permute-start(bf16[16,32,128]{2,1,0:T(8,128)(2,1)S(1)} %pack.21.refs_3_), channel_id=1, source_target_pairs={{1,2},{2,1},{3,4},{4,3},{5,6},{6,5},{7,8},{8,7},{9,10},{10,9},{11,... | collective-permute-start | bytes 393224 | tf_op jit(solution)/shard_map/ppermute | solution.py:58
  42.5 1.7 %collective-permute-done.12.refs_1_ = bf16[32,32,128]{2,1,0:T(8,128)(2,1)S(1)} collective-permute-done((bf16[32,32,128]{2,1,0:T(8,128)(2,1)S(1)}, bf16[32,32,128]{2,1,0:T(8,128)(2,1)S(1)}, u32[]{:S(2)}, u32[]{:S(2)}) %collective-permute-start.12) | collective-permute-done | bytes 262176 | tf_op jit(solution)/shard_map/ppermute | solution.py:58
  44.2 1.6 %early_upper.1.base_ref = f32[16,32,128]{2,1,0:T(8,128)S(1)} custom-call(s32[48,16]{1,0:T(8,128)S(4)} %get-tuple-element.23.refs_0_.where_ref, bf16[32,32,128]{2,1,0:T(8,128)(2,1)S(1)} %collective-permute-done.12.refs_1_, bf16[32,32,128]{2,1,0:T(8,128)(2,1)S(1)} %collective-permute-done.13.refs_2_, bf16[16,32,128]{2,1,0:T(8,128)(2,1)S(1)} %pack.21.refs_3_, ...), custom_call_target="tpu_custom_call" | custom-call | bytes 16777216 | tf_op jit(solution)/shard_map/early_upper/pallas_call | solution.py:355
  45.7 1.9 %collective-permute-done.10.odd_ref = bf16[16,32,128]{2,1,0:T(8,128)(2,1)S(1)} collective-permute-done((bf16[16,32,128]{2,1,0:T(8,128)(2,1)S(1)}, bf16[16,32,128]{2,1,0:T(8,128)(2,1)S(1)}, u32[]{:S(2)}, u32[]{:S(2)}) %collective-permute-start.10) | collective-permute-done | bytes 131104 | tf_op jit(solution)/shard_map/ppermute | solution.py:58
  47.6 1.6 %late_upper.1 = bf16[16,32,256]{2,1,0:T(8,128)(2,1)} custom-call(s32[48,16]{1,0:T(8,128)S(4)} %get-tuple-element.23.refs_0_.where_ref, bf16[16,32,128]{2,1,0:T(8,128)(2,1)S(1)} %collective-permute-done.10.odd_ref, bf16[16,32,128]{2,1,0:T(8,128)(2,1)S(1)} %collective-permute-done.11.even_ref, f32[16,32,128]{2,1,0:T(8,128)S(1)} %early_upper.1.base_ref, ...), custom_call_target="tpu_custom_call" | custom-call | tf_op jit(solution)/shard_map/late_upper/pallas_call | solution.py:386
  (26 shorter events, 1.3 us)
Async XLA Ops:
  2.3 6.4 %collective-permute-start = (bf16[17,32,128]{2,1,0:T(8,128)(2,1)S(1)}, bf16[17,32,128]{2,1,0:T(8,128)(2,1)S(1)}, u32[]{:S(2)}, u32[]{:S(2)}) collective-permute-start(bf16[17,32,128]{2,1,0:T(8,128)(2,1)S(1)} %get-tuple-element.22.refs_0_.refs_5_), channel_id=1, source_target_pairs={{0,16},{16,0},{32,48},{48,32},{64,80},{80,64},{96,112},{112,96},{1... | collective-permute-start | bytes 417800 | tf_op jit(solution)/shard_map/ppermute | solution.py:54
  4.0 9.6 %collective-permute-start.3 = (bf16[17,32,128]{2,1,0:T(8,128)(2,1)S(1)}, bf16[17,32,128]{2,1,0:T(8,128)(2,1)S(1)}, u32[]{:S(2)}, u32[]{:S(2)}) collective-permute-start(bf16[17,32,128]{2,1,0:T(8,128)(2,1)S(1)} %get-tuple-element.22.refs_0_.refs_5_), channel_id=1, source_target_pairs={{16,32},{32,16},{48,64},{64,48},{80,96},{96,80},{0,112},{112,0},{1... | collective-permute-start | bytes 417800 | tf_op jit(solution)/shard_map/ppermute | solution.py:58
  8.7 10.1 %collective-permute-start.1 = (bf16[34,32,128]{2,1,0:T(8,128)(2,1)S(1)}, bf16[34,32,128]{2,1,0:T(8,128)(2,1)S(1)}, u32[]{:S(2)}, u32[]{:S(2)}) collective-permute-start(bf16[34,32,128]{2,1,0:T(8,128)(2,1)S(1)} %pack.11.after_ref.refs_4_), channel_id=1, source_target_pairs={{1,2},{2,1},{3,4},{4,3},{5,6},{6,5},{7,8},{8,7},{9,10},{10,9},{11,... | collective-permute-start | bytes 835592 | tf_op jit(solution)/shard_map/ppermute | solution.py:58
  11.7 7.1 %collective-permute-start.2 = (bf16[34,32,128]{2,1,0:T(8,128)(2,1)S(1)}, bf16[34,32,128]{2,1,0:T(8,128)(2,1)S(1)}, u32[]{:S(2)}, u32[]{:S(2)}) collective-permute-start(bf16[34,32,128]{2,1,0:T(8,128)(2,1)S(1)} %pack.11.after_ref.refs_4_), channel_id=1, source_target_pairs={{0,1},{1,0},{2,3},{3,2},{4,5},{5,4},{6,7},{7,6},{8,9},{9,8},{10,11... | collective-permute-start | bytes 835592 | tf_op jit(solution)/shard_map/ppermute | solution.py:54
  13.7 8.8 %collective-permute-start.4 = (bf16[17,32,128]{2,1,0:T(8,128)(2,1)S(1)}, bf16[17,32,128]{2,1,0:T(8,128)(2,1)S(1)}, u32[]{:S(2)}, u32[]{:S(2)}) collective-permute-start(bf16[17,32,128]{2,1,0:T(8,128)(2,1)S(1)} %pack.15.refs_3_), channel_id=1, source_target_pairs={{1,2},{2,1},{3,4},{4,3},{5,6},{6,5},{7,8},{8,7},{9,10},{10,9},{11,... | collective-permute-start | bytes 417800 | tf_op jit(solution)/shard_map/ppermute | solution.py:58
  16.2 6.4 %collective-permute-start.5 = (bf16[17,32,128]{2,1,0:T(8,128)(2,1)S(1)}, bf16[17,32,128]{2,1,0:T(8,128)(2,1)S(1)}, u32[]{:S(2)}, u32[]{:S(2)}) collective-permute-start(bf16[17,32,128]{2,1,0:T(8,128)(2,1)S(1)} %pack.15.refs_3_), channel_id=1, source_target_pairs={{0,1},{1,0},{2,3},{3,2},{4,5},{5,4},{6,7},{7,6},{8,9},{9,8},{10,11... | collective-permute-start | bytes 417800 | tf_op jit(solution)/shard_map/ppermute | solution.py:54
  23.1 5.0 %collective-permute-start.6 = (bf16[16,32,128]{2,1,0:T(8,128)(2,1)S(1)}, bf16[16,32,128]{2,1,0:T(8,128)(2,1)S(1)}, u32[]{:S(2)}, u32[]{:S(2)}) collective-permute-start(bf16[16,32,128]{2,1,0:T(8,128)(2,1)S(1)} %late_lower.1.after_ref.refs_0_), channel_id=1, source_target_pairs={{0,16},{16,0},{32,48},{48,32},{64,80},{80,64},{96,112},{112,96},{1... | collective-permute-start | bytes 393224 | tf_op jit(solution)/shard_map/ppermute | solution.py:54
  28.2 1.6 %collective-permute-start.7 = (bf16[32,32,128]{2,1,0:T(8,128)(2,1)S(1)}, bf16[32,32,128]{2,1,0:T(8,128)(2,1)S(1)}, u32[]{:S(2)}, u32[]{:S(2)}) collective-permute-start(bf16[32,32,128]{2,1,0:T(8,128)(2,1)S(1)} %pack.16.own_ref), channel_id=1, source_target_pairs={{0,1},{1,0},{2,3},{3,2},{4,5},{5,4},{6,7},{7,6},{8,9},{9,8},{10,11... | collective-permute-start | bytes 786440 | tf_op jit(solution)/shard_map/ppermute | solution.py:54
  30.5 5.6 %collective-permute-start.9 = (bf16[16,32,128]{2,1,0:T(8,128)(2,1)S(1)}, bf16[16,32,128]{2,1,0:T(8,128)(2,1)S(1)}, u32[]{:S(2)}, u32[]{:S(2)}) collective-permute-start(bf16[16,32,128]{2,1,0:T(8,128)(2,1)S(1)} %parent.1.skel_ref.refs_0_), channel_id=1, source_target_pairs={{0,16},{16,0},{32,48},{48,32},{64,80},{80,64},{96,112},{112,96},{1... | collective-permute-start | bytes 393224 | tf_op jit(solution)/shard_map/ppermute | solution.py:54
  32.1 8.9 %collective-permute-start.8 = (bf16[16,32,128]{2,1,0:T(8,128)(2,1)S(1)}, bf16[16,32,128]{2,1,0:T(8,128)(2,1)S(1)}, u32[]{:S(2)}, u32[]{:S(2)}) collective-permute-start(bf16[16,32,128]{2,1,0:T(8,128)(2,1)S(1)} %parent.1.skel_ref.refs_0_), channel_id=1, source_target_pairs={{16,32},{32,16},{48,64},{64,48},{80,96},{96,80},{0,112},{112,0},{1... | collective-permute-start | bytes 393224 | tf_op jit(solution)/shard_map/ppermute | solution.py:58
  36.2 8.0 %collective-permute-start.12 = (bf16[32,32,128]{2,1,0:T(8,128)(2,1)S(1)}, bf16[32,32,128]{2,1,0:T(8,128)(2,1)S(1)}, u32[]{:S(2)}, u32[]{:S(2)}) collective-permute-start(bf16[32,32,128]{2,1,0:T(8,128)(2,1)S(1)} %pack.17.after_ref.refs_4_), channel_id=1, source_target_pairs={{1,2},{2,1},{3,4},{4,3},{5,6},{6,5},{7,8},{8,7},{9,10},{10,9},{11,... | collective-permute-start | bytes 786440 | tf_op jit(solution)/shard_map/ppermute | solution.py:58
  37.2 7.0 %collective-permute-start.13 = (bf16[32,32,128]{2,1,0:T(8,128)(2,1)S(1)}, bf16[32,32,128]{2,1,0:T(8,128)(2,1)S(1)}, u32[]{:S(2)}, u32[]{:S(2)}) collective-permute-start(bf16[32,32,128]{2,1,0:T(8,128)(2,1)S(1)} %pack.17.after_ref.refs_4_), channel_id=1, source_target_pairs={{0,1},{1,0},{2,3},{3,2},{4,5},{5,4},{6,7},{7,6},{8,9},{9,8},{10,11... | collective-permute-start | bytes 786440 | tf_op jit(solution)/shard_map/ppermute | solution.py:54
  41.0 6.6 %collective-permute-start.10 = (bf16[16,32,128]{2,1,0:T(8,128)(2,1)S(1)}, bf16[16,32,128]{2,1,0:T(8,128)(2,1)S(1)}, u32[]{:S(2)}, u32[]{:S(2)}) collective-permute-start(bf16[16,32,128]{2,1,0:T(8,128)(2,1)S(1)} %pack.21.refs_3_), channel_id=1, source_target_pairs={{1,2},{2,1},{3,4},{4,3},{5,6},{6,5},{7,8},{8,7},{9,10},{10,9},{11,... | collective-permute-start | bytes 393224 | tf_op jit(solution)/shard_map/ppermute | solution.py:58
  42.5 5.1 %collective-permute-start.11 = (bf16[16,32,128]{2,1,0:T(8,128)(2,1)S(1)}, bf16[16,32,128]{2,1,0:T(8,128)(2,1)S(1)}, u32[]{:S(2)}, u32[]{:S(2)}) collective-permute-start(bf16[16,32,128]{2,1,0:T(8,128)(2,1)S(1)} %pack.21.refs_3_), channel_id=1, source_target_pairs={{0,1},{1,0},{2,3},{3,2},{4,5},{5,4},{6,7},{7,6},{8,9},{9,8},{10,11... | collective-permute-start | bytes 393224 | tf_op jit(solution)/shard_map/ppermute | solution.py:54

commit v5 on v4

--- a/solution.py
+++ b/solution.py
@@ -46,16 +46,27 @@
     return [(i, i ^ 1) for i in range(peers)]
 
 
-def odd_pairs(peers):
-    return [(i, ((i + 1) ^ 1) - 1) for i in range(1, peers - 1)] + [(0, peers - 1), (peers - 1, 0)]
-
-
 def even_swap(value, axis):
     return lax.ppermute(value, axis, even_pairs(lax.axis_size(axis)))
 
 
 def odd_swap(value, axis):
-    return lax.ppermute(value, axis, odd_pairs(lax.axis_size(axis)))
+    across, along = lax.axis_size("bx"), lax.axis_size("by")
+
+    def other(i, peers):
+        return ((i + 1) ^ 1) - 1 if 0 < i < peers - 1 else None
+
+    pairs = []
+    for i in range(across):
+        for j in range(along):
+            if axis == "bx":
+                to = other(i, across)
+                to = (i, j ^ 1) if to is None else (to, j)
+            else:
+                to = other(j, along)
+                to = (i ^ 1, j) if to is None else (i, to)
+            pairs.append((i * along + j, to[0] * along + to[1]))
+    return lax.ppermute(value, ("bx", "by"), pairs)
 
 
 def find_places(codes, counts, planes, out_ref):

time: 49.5 us -> 47.4 us (0.958)
  the two profiles are of different devices: /device:TPU:0 before, /device:TPU:26 now
where the time goes in v5:
time: 47.4 us; the launch traced here: 47.2 us
  Pallas kernels  19.5 us (41%)
  starting transfers between devices  14.1 us (30%)
  waiting for transfers between devices  13.4 us (28%)
    ppermute x6, starting transfers between devices, odd_swap(): return lax.ppermute(value, ('bx', 'by'), pairs)  11.5 us
    ppermute x6, waiting for transfers between devices, odd_swap(): return lax.ppermute(value, ('bx', 'by'), pairs)  7.21 us
    pallas_call x3, Pallas kernels, fetch(): call(functools.partial(fetch_kernel, start=start), 'fetch', [HB, AN], [pl...  6.6 us
    ppermute x8, waiting for transfers between devices, even_swap(): return lax.ppermute(value, axis, even_pairs(lax.axis_size(axis)))  6.2 us
    pallas_call x1, Pallas kernels, early_lower(): call(early_lower_kernel, 'early_lower', [SM] + [VM] * 6 + [HB], [pltpu.VM...  3.65 us
    ppermute x8, starting transfers between devices, even_swap(): return lax.ppermute(value, axis, even_pairs(lax.axis_size(axis)))  2.57 us
    pallas_call x1, Pallas kernels, first(): call(first_kernel, 'first', [HB] * 4, [pltpu.VMEM((height, rhs_count, ran...  2.3 us
    pallas_call x1, Pallas kernels, places(): call(functools.partial(places_kernel, planes=planes), 'places', [HB, HB,...  1.86 us
  transfers between devices with their start and end apart: 14, of which 8 were waited for; matrix products, arithmetic and copies ran while one was open for 0% of the time, Pallas kernels for 30%

profile of v5, /device:TPU:26, one launch (start us, length us, event | category | flops | bytes accessed | tf_op | source)
XLA Modules:
  0.0 47.2 jit_solution(7581164579274430581)
XLA Ops:
  0.0 2.3 %first.1 = (f32[16,32,128]{2,1,0:T(8,128)S(1)}, bf16[17,32,128]{2,1,0:T(8,128)(2,1)S(1)}, bf16[16,256,256]{2,1,0:T(8,128)(2,1)S(1)}) custom-call(bf16[16,32,256]{2,1,0:T(8,128)(2,1)} %bitcast.17, bf16[16,256,256]{2,1,0:T(8,128)(2,1)} %bitcast.15, bf16[16,128,128]{2,1,0:T(8,128)(2,1)} %bitcast.16, s32[1,16]{1,0:T(1,128)} %bitcast.19), custom_call_target="tpu_custom_call" | custom-call | tf_op jit(solution)/shard_map/first/pallas_call | solution.py:176
  2.3 0.8 %collective-permute-start = (bf16[17,32,128]{2,1,0:T(8,128)(2,1)S(1)}, bf16[17,32,128]{2,1,0:T(8,128)(2,1)S(1)}, u32[]{:S(2)}, u32[]{:S(2)}) collective-permute-start(bf16[17,32,128]{2,1,0:T(8,128)(2,1)S(1)} %get-tuple-element.22.refs_0_.refs_5_), channel_id=1, source_target_pairs={{0,16},{16,0},{32,48},{48,32},{64,80},{80,64},{96,112},{112,96},{1... | collective-permute-start | bytes 417800 | tf_op jit(solution)/shard_map/ppermute | solution.py:50
  3.1 2.6 %collective-permute-start.3 = (bf16[17,32,128]{2,1,0:T(8,128)(2,1)S(1)}, bf16[17,32,128]{2,1,0:T(8,128)(2,1)S(1)}, u32[]{:S(2)}, u32[]{:S(2)}) collective-permute-start(bf16[17,32,128]{2,1,0:T(8,128)(2,1)S(1)} %get-tuple-element.22.refs_0_.refs_5_), channel_id=1, source_target_pairs={{0,1},{1,0},{2,3},{3,2},{4,5},{5,4},{6,7},{7,6},{8,9},{9,8},{10,11... | collective-permute-start | bytes 417800 | tf_op jit(solution)/shard_map/ppermute | solution.py:69
  5.7 2.1 %collective-permute-done.refs_1_ = bf16[17,32,128]{2,1,0:T(8,128)(2,1)S(1)} collective-permute-done((bf16[17,32,128]{2,1,0:T(8,128)(2,1)S(1)}, bf16[17,32,128]{2,1,0:T(8,128)(2,1)S(1)}, u32[]{:S(2)}, u32[]{:S(2)}) %collective-permute-start) | collective-permute-done | bytes 139296 | tf_op jit(solution)/shard_map/ppermute | solution.py:50
  7.8 2.7 %collective-permute-start.1 = (bf16[34,32,128]{2,1,0:T(8,128)(2,1)S(1)}, bf16[34,32,128]{2,1,0:T(8,128)(2,1)S(1)}, u32[]{:S(2)}, u32[]{:S(2)}) collective-permute-start(bf16[34,32,128]{2,1,0:T(8,128)(2,1)S(1)} %pack.11.after_ref.refs_4_), channel_id=1, source_target_pairs={{0,16},{1,2},{2,1},{3,4},{4,3},{5,6},{6,5},{7,8},{8,7},{9,10},{10,... | collective-permute-start | bytes 835592 | tf_op jit(solution)/shard_map/ppermute | solution.py:69
  10.5 1.9 %places.1 = (s32[48,16]{1,0:T(8,128)S(4)}, f32[8,128]{1,0:T(8,128)S(1)}, bf16[4,16,128,128]{3,2,1,0:T(8,128)(2,1)S(1)}) custom-call(s32[16,16]{1,0:T(8,128)} %bitcast.18, s32[1,16]{1,0:T(1,128)} %bitcast.20, bf16[16,16,128,128]{3,2,1,0:T(8,128)(2,1)} %bitcast.10, bf16[34,32,128]{2,1,0:T(8,128)(2,1)S(1)} %pack.11.after_ref.refs_4_), custom_call_target="tpu_custom_call" | custom-call | bytes 4194304 | tf_op jit(solution)/shard_map/places/pallas_call | solution.py:127
  12.4 1.8 %collective-permute-start.4 = (bf16[17,32,128]{2,1,0:T(8,128)(2,1)S(1)}, bf16[17,32,128]{2,1,0:T(8,128)(2,1)S(1)}, u32[]{:S(2)}, u32[]{:S(2)}) collective-permute-start(bf16[17,32,128]{2,1,0:T(8,128)(2,1)S(1)} %pack.15.refs_3_), channel_id=1, source_target_pairs={{0,16},{1,2},{2,1},{3,4},{4,3},{5,6},{6,5},{7,8},{8,7},{9,10},{10,... | collective-permute-start | bytes 417800 | tf_op jit(solution)/shard_map/ppermute | solution.py:69
  14.3 2.5 %collective-permute-done.1.refs_1_ = bf16[34,32,128]{2,1,0:T(8,128)(2,1)S(1)} collective-permute-done((bf16[34,32,128]{2,1,0:T(8,128)(2,1)S(1)}, bf16[34,32,128]{2,1,0:T(8,128)(2,1)S(1)}, u32[]{:S(2)}, u32[]{:S(2)}) %collective-permute-start.1) | collective-permute-done | bytes 278560 | tf_op jit(solution)/shard_map/ppermute | solution.py:69
  16.7 3.6 %early_lower.1 = (f32[16,32,128]{2,1,0:T(8,128)S(1)}, s32[16,128]{1,0:T(8,128)S(4)}, bf16[12,16,128,128]{3,2,1,0:T(8,128)(2,1)S(1)}) custom-call(s32[48,16]{1,0:T(8,128)S(4)} %get-tuple-element.23.refs_0_.where_ref, bf16[34,32,128]{2,1,0:T(8,128)(2,1)S(1)} %collective-permute-done.1.refs_1_, bf16[34,32,128]{2,1,0:T(8,128)(2,1)S(1)} %collective-permute-done.2.refs_2_, ...), custom_call_target="tpu_custom_call" | custom-call | bytes 16777216 | tf_op jit(solution)/shard_map/early_lower/pallas_call | solution.py:284
  21.1 2.2 %fetch.3 = (bf16[16,1024,128]{2,1,0:T(8,128)(2,1)S(1)}, f32[8,128]{1,0:T(8,128)S(1)}) custom-call(bf16[16,1024,128]{2,1,0:T(8,128)(2,1)} %bitcast.14, bf16[16,32,128]{2,1,0:T(8,128)(2,1)S(1)} %late_lower.1.after_ref.refs_0_), custom_call_target="tpu_custom_call" | custom-call | bytes 8388608 | tf_op jit(solution)/shard_map/fetch/pallas_call | solution.py:203
  23.3 2.2 %fetch.4 = (bf16[8,16,128,128]{3,2,1,0:T(8,128)(2,1)S(1)}, f32[8,128]{1,0:T(8,128)S(1)}) custom-call(bf16[16,16,128,128]{3,2,1,0:T(8,128)(2,1)} %bitcast.12, bf16[16,32,128]{2,1,0:T(8,128)(2,1)S(1)} %late_lower.1.after_ref.refs_0_), custom_call_target="tpu_custom_call" | custom-call | bytes 8388608 | tf_op jit(solution)/shard_map/fetch/pallas_call | solution.py:203
  26.2 1.5 %collective-permute-done.7.far_ref = bf16[32,32,128]{2,1,0:T(8,128)(2,1)S(1)} collective-permute-done((bf16[32,32,128]{2,1,0:T(8,128)(2,1)S(1)}, bf16[32,32,128]{2,1,0:T(8,128)(2,1)S(1)}, u32[]{:S(2)}, u32[]{:S(2)}) %collective-permute-start.7) | collective-permute-done | bytes 262176 | tf_op jit(solution)/shard_map/ppermute | solution.py:50
  27.7 0.7 %parent.1.skel_ref.refs_0_ = bf16[16,32,128]{2,1,0:T(8,128)(2,1)S(1)} custom-call(s32[16,128]{1,0:T(8,128)S(4)} %get-tuple-element.27.child_ref, bf16[32,32,128]{2,1,0:T(8,128)(2,1)S(1)} %pack.16.own_ref, bf16[32,32,128]{2,1,0:T(8,128)(2,1)S(1)} %collective-permute-done.7.far_ref, bf16[16,1024,128]{2,1,0:T(8,128)(2,1)S(1)} %get-tuple-element.32.rows_ref), custom_call_target="tpu_custom_call" | custom-call | tf_op jit(solution)/shard_map/parent/pallas_call | solution.py:328
  28.4 1.6 %collective-permute-start.9 = (bf16[16,32,128]{2,1,0:T(8,128)(2,1)S(1)}, bf16[16,32,128]{2,1,0:T(8,128)(2,1)S(1)}, u32[]{:S(2)}, u32[]{:S(2)}) collective-permute-start(bf16[16,32,128]{2,1,0:T(8,128)(2,1)S(1)} %parent.1.skel_ref.refs_0_), channel_id=1, source_target_pairs={{0,16},{16,0},{32,48},{48,32},{64,80},{80,64},{96,112},{112,96},{1... | collective-permute-start | bytes 393224 | tf_op jit(solution)/shard_map/ppermute | solution.py:50
  30.0 1.5 %collective-permute-start.8 = (bf16[16,32,128]{2,1,0:T(8,128)(2,1)S(1)}, bf16[16,32,128]{2,1,0:T(8,128)(2,1)S(1)}, u32[]{:S(2)}, u32[]{:S(2)}) collective-permute-start(bf16[16,32,128]{2,1,0:T(8,128)(2,1)S(1)} %parent.1.skel_ref.refs_0_), channel_id=1, source_target_pairs={{0,1},{1,0},{2,3},{3,2},{4,5},{5,4},{6,7},{7,6},{8,9},{9,8},{10,11... | collective-permute-start | bytes 393224 | tf_op jit(solution)/shard_map/ppermute | solution.py:69
  32.0 2.1 %collective-permute-done.9.refs_1_ = bf16[16,32,128]{2,1,0:T(8,128)(2,1)S(1)} collective-permute-done((bf16[16,32,128]{2,1,0:T(8,128)(2,1)S(1)}, bf16[16,32,128]{2,1,0:T(8,128)(2,1)S(1)}, u32[]{:S(2)}, u32[]{:S(2)}) %collective-permute-start.9) | collective-permute-done | bytes 131104 | tf_op jit(solution)/shard_map/ppermute | solution.py:50
  34.1 1.4 %collective-permute-start.12 = (bf16[32,32,128]{2,1,0:T(8,128)(2,1)S(1)}, bf16[32,32,128]{2,1,0:T(8,128)(2,1)S(1)}, u32[]{:S(2)}, u32[]{:S(2)}) collective-permute-start(bf16[32,32,128]{2,1,0:T(8,128)(2,1)S(1)} %pack.17.after_ref.refs_4_), channel_id=1, source_target_pairs={{0,16},{1,2},{2,1},{3,4},{4,3},{5,6},{6,5},{7,8},{8,7},{9,10},{10,... | collective-permute-start | bytes 786440 | tf_op jit(solution)/shard_map/ppermute | solution.py:69
  35.5 2.2 %fetch.5 = (bf16[8,16,128,128]{3,2,1,0:T(8,128)(2,1)S(1)}, f32[8,128]{1,0:T(8,128)S(1)}) custom-call(bf16[16,16,128,128]{3,2,1,0:T(8,128)(2,1)} %bitcast.13, bf16[32,32,128]{2,1,0:T(8,128)(2,1)S(1)} %pack.17.after_ref.refs_4_), custom_call_target="tpu_custom_call" | custom-call | bytes 8388608 | tf_op jit(solution)/shard_map/fetch/pallas_call | solution.py:203
  37.7 1.2 %collective-permute-done.8.refs_0_ = bf16[16,32,128]{2,1,0:T(8,128)(2,1)S(1)} collective-permute-done((bf16[16,32,128]{2,1,0:T(8,128)(2,1)S(1)}, bf16[16,32,128]{2,1,0:T(8,128)(2,1)S(1)}, u32[]{:S(2)}, u32[]{:S(2)}) %collective-permute-start.8) | collective-permute-done | bytes 131104 | tf_op jit(solution)/shard_map/ppermute | solution.py:69
  39.0 1.4 %collective-permute-start.10 = (bf16[16,32,128]{2,1,0:T(8,128)(2,1)S(1)}, bf16[16,32,128]{2,1,0:T(8,128)(2,1)S(1)}, u32[]{:S(2)}, u32[]{:S(2)}) collective-permute-start(bf16[16,32,128]{2,1,0:T(8,128)(2,1)S(1)} %pack.21.refs_3_), channel_id=1, source_target_pairs={{0,16},{1,2},{2,1},{3,4},{4,3},{5,6},{6,5},{7,8},{8,7},{9,10},{10,... | collective-permute-start | bytes 393224 | tf_op jit(solution)/shard_map/ppermute | solution.py:69
  40.4 1.7 %collective-permute-done.12.refs_1_ = bf16[32,32,128]{2,1,0:T(8,128)(2,1)S(1)} collective-permute-done((bf16[32,32,128]{2,1,0:T(8,128)(2,1)S(1)}, bf16[32,32,128]{2,1,0:T(8,128)(2,1)S(1)}, u32[]{:S(2)}, u32[]{:S(2)}) %collective-permute-start.12) | collective-permute-done | bytes 262176 | tf_op jit(solution)/shard_map/ppermute | solution.py:69
  42.1 1.6 %early_upper.1.base_ref = f32[16,32,128]{2,1,0:T(8,128)S(1)} custom-call(s32[48,16]{1,0:T(8,128)S(4)} %get-tuple-element.23.refs_0_.where_ref, bf16[32,32,128]{2,1,0:T(8,128)(2,1)S(1)} %collective-permute-done.12.refs_1_, bf16[32,32,128]{2,1,0:T(8,128)(2,1)S(1)} %collective-permute-done.13.refs_2_, bf16[16,32,128]{2,1,0:T(8,128)(2,1)S(1)} %pack.21.refs_3_, ...), custom_call_target="tpu_custom_call" | custom-call | bytes 16777216 | tf_op jit(solution)/shard_map/early_upper/pallas_call | solution.py:366
  43.6 1.9 %collective-permute-done.10.odd_ref = bf16[16,32,128]{2,1,0:T(8,128)(2,1)S(1)} collective-permute-done((bf16[16,32,128]{2,1,0:T(8,128)(2,1)S(1)}, bf16[16,32,128]{2,1,0:T(8,128)(2,1)S(1)}, u32[]{:S(2)}, u32[]{:S(2)}) %collective-permute-start.10) | collective-permute-done | bytes 131104 | tf_op jit(solution)/shard_map/ppermute | solution.py:69
  45.5 1.6 %late_upper.1 = bf16[16,32,256]{2,1,0:T(8,128)(2,1)} custom-call(s32[48,16]{1,0:T(8,128)S(4)} %get-tuple-element.23.refs_0_.where_ref, bf16[16,32,128]{2,1,0:T(8,128)(2,1)S(1)} %collective-permute-done.10.odd_ref, bf16[16,32,128]{2,1,0:T(8,128)(2,1)S(1)} %collective-permute-done.11.even_ref, f32[16,32,128]{2,1,0:T(8,128)S(1)} %early_upper.1.base_ref, ...), custom_call_target="tpu_custom_call" | custom-call | tf_op jit(solution)/shard_map/late_upper/pallas_call | solution.py:397
  (26 shorter events, 1.9 us)
Async XLA Ops:
  2.3 5.5 %collective-permute-start = (bf16[17,32,128]{2,1,0:T(8,128)(2,1)S(1)}, bf16[17,32,128]{2,1,0:T(8,128)(2,1)S(1)}, u32[]{:S(2)}, u32[]{:S(2)}) collective-permute-start(bf16[17,32,128]{2,1,0:T(8,128)(2,1)S(1)} %get-tuple-element.22.refs_0_.refs_5_), channel_id=1, source_target_pairs={{0,16},{16,0},{32,48},{48,32},{64,80},{80,64},{96,112},{112,96},{1... | collective-permute-start | bytes 417800 | tf_op jit(solution)/shard_map/ppermute | solution.py:50
  3.1 9.2 %collective-permute-start.3 = (bf16[17,32,128]{2,1,0:T(8,128)(2,1)S(1)}, bf16[17,32,128]{2,1,0:T(8,128)(2,1)S(1)}, u32[]{:S(2)}, u32[]{:S(2)}) collective-permute-start(bf16[17,32,128]{2,1,0:T(8,128)(2,1)S(1)} %get-tuple-element.22.refs_0_.refs_5_), channel_id=1, source_target_pairs={{0,1},{1,0},{2,3},{3,2},{4,5},{5,4},{6,7},{7,6},{8,9},{9,8},{10,11... | collective-permute-start | bytes 417800 | tf_op jit(solution)/shard_map/ppermute | solution.py:69
  7.8 8.9 %collective-permute-start.1 = (bf16[34,32,128]{2,1,0:T(8,128)(2,1)S(1)}, bf16[34,32,128]{2,1,0:T(8,128)(2,1)S(1)}, u32[]{:S(2)}, u32[]{:S(2)}) collective-permute-start(bf16[34,32,128]{2,1,0:T(8,128)(2,1)S(1)} %pack.11.after_ref.refs_4_), channel_id=1, source_target_pairs={{0,16},{1,2},{2,1},{3,4},{4,3},{5,6},{6,5},{7,8},{8,7},{9,10},{10,... | collective-permute-start | bytes 835592 | tf_op jit(solution)/shard_map/ppermute | solution.py:69
  10.5 6.3 %collective-permute-start.2 = (bf16[34,32,128]{2,1,0:T(8,128)(2,1)S(1)}, bf16[34,32,128]{2,1,0:T(8,128)(2,1)S(1)}, u32[]{:S(2)}, u32[]{:S(2)}) collective-permute-start(bf16[34,32,128]{2,1,0:T(8,128)(2,1)S(1)} %pack.11.after_ref.refs_4_), channel_id=1, source_target_pairs={{0,1},{1,0},{2,3},{3,2},{4,5},{5,4},{6,7},{7,6},{8,9},{9,8},{10,11... | collective-permute-start | bytes 835592 | tf_op jit(solution)/shard_map/ppermute | solution.py:50
  12.4 8.0 %collective-permute-start.4 = (bf16[17,32,128]{2,1,0:T(8,128)(2,1)S(1)}, bf16[17,32,128]{2,1,0:T(8,128)(2,1)S(1)}, u32[]{:S(2)}, u32[]{:S(2)}) collective-permute-start(bf16[17,32,128]{2,1,0:T(8,128)(2,1)S(1)} %pack.15.refs_3_), channel_id=1, source_target_pairs={{0,16},{1,2},{2,1},{3,4},{4,3},{5,6},{6,5},{7,8},{8,7},{9,10},{10,... | collective-permute-start | bytes 417800 | tf_op jit(solution)/shard_map/ppermute | solution.py:69
  14.3 6.1 %collective-permute-start.5 = (bf16[17,32,128]{2,1,0:T(8,128)(2,1)S(1)}, bf16[17,32,128]{2,1,0:T(8,128)(2,1)S(1)}, u32[]{:S(2)}, u32[]{:S(2)}) collective-permute-start(bf16[17,32,128]{2,1,0:T(8,128)(2,1)S(1)} %pack.15.refs_3_), channel_id=1, source_target_pairs={{0,1},{1,0},{2,3},{3,2},{4,5},{5,4},{6,7},{7,6},{8,9},{9,8},{10,11... | collective-permute-start | bytes 417800 | tf_op jit(solution)/shard_map/ppermute | solution.py:50
  21.0 5.0 %collective-permute-start.6 = (bf16[16,32,128]{2,1,0:T(8,128)(2,1)S(1)}, bf16[16,32,128]{2,1,0:T(8,128)(2,1)S(1)}, u32[]{:S(2)}, u32[]{:S(2)}) collective-permute-start(bf16[16,32,128]{2,1,0:T(8,128)(2,1)S(1)} %late_lower.1.after_ref.refs_0_), channel_id=1, source_target_pairs={{0,16},{16,0},{32,48},{48,32},{64,80},{80,64},{96,112},{112,96},{1... | collective-permute-start | bytes 393224 | tf_op jit(solution)/shard_map/ppermute | solution.py:50
  26.1 1.6 %collective-permute-start.7 = (bf16[32,32,128]{2,1,0:T(8,128)(2,1)S(1)}, bf16[32,32,128]{2,1,0:T(8,128)(2,1)S(1)}, u32[]{:S(2)}, u32[]{:S(2)}) collective-permute-start(bf16[32,32,128]{2,1,0:T(8,128)(2,1)S(1)} %pack.16.own_ref), channel_id=1, source_target_pairs={{0,1},{1,0},{2,3},{3,2},{4,5},{5,4},{6,7},{7,6},{8,9},{9,8},{10,11... | collective-permute-start | bytes 786440 | tf_op jit(solution)/shard_map/ppermute | solution.py:50
  28.4 5.6 %collective-permute-start.9 = (bf16[16,32,128]{2,1,0:T(8,128)(2,1)S(1)}, bf16[16,32,128]{2,1,0:T(8,128)(2,1)S(1)}, u32[]{:S(2)}, u32[]{:S(2)}) collective-permute-start(bf16[16,32,128]{2,1,0:T(8,128)(2,1)S(1)} %parent.1.skel_ref.refs_0_), channel_id=1, source_target_pairs={{0,16},{16,0},{32,48},{48,32},{64,80},{80,64},{96,112},{112,96},{1... | collective-permute-start | bytes 393224 | tf_op jit(solution)/shard_map/ppermute | solution.py:50
  30.0 8.9 %collective-permute-start.8 = (bf16[16,32,128]{2,1,0:T(8,128)(2,1)S(1)}, bf16[16,32,128]{2,1,0:T(8,128)(2,1)S(1)}, u32[]{:S(2)}, u32[]{:S(2)}) collective-permute-start(bf16[16,32,128]{2,1,0:T(8,128)(2,1)S(1)} %parent.1.skel_ref.refs_0_), channel_id=1, source_target_pairs={{0,1},{1,0},{2,3},{3,2},{4,5},{5,4},{6,7},{7,6},{8,9},{9,8},{10,11... | collective-permute-start | bytes 393224 | tf_op jit(solution)/shard_map/ppermute | solution.py:69
  34.1 8.0 %collective-permute-start.12 = (bf16[32,32,128]{2,1,0:T(8,128)(2,1)S(1)}, bf16[32,32,128]{2,1,0:T(8,128)(2,1)S(1)}, u32[]{:S(2)}, u32[]{:S(2)}) collective-permute-start(bf16[32,32,128]{2,1,0:T(8,128)(2,1)S(1)} %pack.17.after_ref.refs_4_), channel_id=1, source_target_pairs={{0,16},{1,2},{2,1},{3,4},{4,3},{5,6},{6,5},{7,8},{8,7},{9,10},{10,... | collective-permute-start | bytes 786440 | tf_op jit(solution)/shard_map/ppermute | solution.py:69
  35.5 6.6 %collective-permute-start.13 = (bf16[32,32,128]{2,1,0:T(8,128)(2,1)S(1)}, bf16[32,32,128]{2,1,0:T(8,128)(2,1)S(1)}, u32[]{:S(2)}, u32[]{:S(2)}) collective-permute-start(bf16[32,32,128]{2,1,0:T(8,128)(2,1)S(1)} %pack.17.after_ref.refs_4_), channel_id=1, source_target_pairs={{0,1},{1,0},{2,3},{3,2},{4,5},{5,4},{6,7},{7,6},{8,9},{9,8},{10,11... | collective-permute-start | bytes 786440 | tf_op jit(solution)/shard_map/ppermute | solution.py:50
  39.0 6.6 %collective-permute-start.10 = (bf16[16,32,128]{2,1,0:T(8,128)(2,1)S(1)}, bf16[16,32,128]{2,1,0:T(8,128)(2,1)S(1)}, u32[]{:S(2)}, u32[]{:S(2)}) collective-permute-start(bf16[16,32,128]{2,1,0:T(8,128)(2,1)S(1)} %pack.21.refs_3_), channel_id=1, source_target_pairs={{0,16},{1,2},{2,1},{3,4},{4,3},{5,6},{6,5},{7,8},{8,7},{9,10},{10,... | collective-permute-start | bytes 393224 | tf_op jit(solution)/shard_map/ppermute | solution.py:69
  40.4 5.1 %collective-permute-start.11 = (bf16[16,32,128]{2,1,0:T(8,128)(2,1)S(1)}, bf16[16,32,128]{2,1,0:T(8,128)(2,1)S(1)}, u32[]{:S(2)}, u32[]{:S(2)}) collective-permute-start(bf16[16,32,128]{2,1,0:T(8,128)(2,1)S(1)} %pack.21.refs_3_), channel_id=1, source_target_pairs={{0,1},{1,0},{2,3},{3,2},{4,5},{5,4},{6,7},{7,6},{8,9},{9,8},{10,11... | collective-permute-start | bytes 393224 | tf_op jit(solution)/shard_map/ppermute | solution.py:50
